TPU v7x, 32 devices: a whole 2x2x4 slice. The times are simulated.
32 devices in a mesh: req: 16 (over z, y, x), tp: 2 (over core).
Axes of the slice: x: 2, y: 2, z: 4, core: 2. Of those that a mesh axis runs over, the one named last changes fastest.
Arguments:
- hidden_in: bfloat16 [2048, 5120], P('req', 'tp'), may hold values from -1.5 to 1.5
- queries: bfloat16 [2048, 5120], P('req', 'tp'), may hold values from -100 to 100
- new_keys: bfloat16 [2048, 5120], P('req', 'tp'), may hold values from -12 to 12
- new_values: bfloat16 [2048, 5120], P('req', 'tp'), may hold values from -6 to 6
- query_gain: float32 [5120], P('tp'), may hold values from 0.1 to 1.9
- key_gain: float32 [5120], P('tp'), may hold values from 0.1 to 1.9
- cache_keys: bfloat16 [256, 256, 5120], P('req', None, 'tp'), may hold values from -50 to 50
- cache_values: bfloat16 [256, 256, 5120], P('req', None, 'tp'), may hold values from -6 to 6
- seg_ids: int32 [2048], replicated, may hold values from 0 to 15, never falling along the last dimension, each value on 1 to 256 neighbouring positions
- cache_pages: int32 [16], replicated, may hold values from 1 to 32, 256 in all
- page_table: int32 [256], replicated, may hold values from 0 to 255, each once
- out_weight: bfloat16 [5120, 5120], P('tp', 'req'), may hold values from -0.078125 to 0.078125
- out_bias: float32 [5120], P('tp'), may hold values from -1.8 to 1.8
- gate_mod: float32 [16, 5120], P(None, 'tp'), may hold values from -8 to 8
Outputs:
- hidden_out: bfloat16 [2048, 5120], P('req', 'tp')
Inputs may be any that keep to these rules, and one draw needn't show every extreme that they name: `seg_ids`: segment numbers never fall; segment r holds the new tokens of request r; every request has 1 to 256 new tokens, one exactly 256. `cache_pages`: every request has at least one cached page; the counts sum to 256; the largest is exactly 32. A permutation; logical page g (the requests' pages in order of request, each request's in order) lies in slot page_table[g] % 16 of the req index page_table[g] // 16.
All inputs are finite; a program needn't handle non-finite values.
Results may differ from a plain program's by a relative error of at most 0.012.
Values may be sent and summed in bfloat16 or wider, within the bound.
No kernel may reach another device: no remote copies, remote signals or barrier semaphores. Data moves between devices by JAX's collectives and lax.ppermute only.
A program may use at most 192 MiB of HBM per device.

v0:
```python
import math

import jax
import jax.numpy as jnp
from jax import lax
from jax.sharding import PartitionSpec as P

D = 5120
HEAD_DIM = 128


EPSILON = 1e-06
LOW_SCORE = -1e30


def passed_along(value, axis, by):
    size = lax.axis_size(axis)
    pairs = [(i, i + by) for i in range(size) if 0 <= i + by < size]
    return lax.ppermute(value, axis, pairs)


def turn_heads(normed, positions):
    row_count, width_count = normed.shape
    split_heads = normed.reshape(row_count, width_count // HEAD_DIM, HEAD_DIM)
    halfway = HEAD_DIM // 2
    frequency = 10000.0 ** (-jnp.arange(halfway, dtype=jnp.float32) / halfway)
    angles = positions.astype(jnp.float32)[:, None] * frequency[None, :]
    cosine = jnp.cos(angles)[:, None, :]
    sine_part = jnp.sin(angles)[:, None, :]
    lower_half = split_heads[:, :, :halfway]
    upper_half = split_heads[:, :, halfway:]
    turned = jnp.concatenate(
        [
            lower_half * cosine - upper_half * sine_part,
            upper_half * cosine + lower_half * sine_part,
        ],
        axis=2,
    )
    return turned.reshape(row_count, width_count).astype(jnp.bfloat16)


def combine_pair(first, second):
    first_max, first_sum, first_out = first
    second_max, second_sum, second_out = second
    highest = jnp.maximum(first_max, second_max)
    first_weight = jnp.exp(first_max - highest)
    second_weight = jnp.exp(second_max - highest)
    return (
        highest,
        first_sum * first_weight + second_sum * second_weight,
        first_out * first_weight[..., None] + second_out * second_weight[..., None],
    )


def attend_block(query_rows, key_rows, value_rows, allowed):
    heads_here = query_rows.shape[1] // HEAD_DIM
    score_scale = 1.0 / math.sqrt(HEAD_DIM)
    query_split = query_rows.reshape(query_rows.shape[0], heads_here, HEAD_DIM)
    key_split = key_rows.reshape(key_rows.shape[0], heads_here, HEAD_DIM)
    scores = (
        jnp.einsum("qhd,khd->hqk", query_split, key_split, preferred_element_type=jnp.float32)
        * score_scale
    )
    scores = jnp.where(allowed[None], scores, LOW_SCORE)
    peak_score = jnp.max(scores, axis=2)
    weights = jnp.where(allowed[None], jnp.exp(scores - peak_score[:, :, None]), 0.0)
    weight_sum = jnp.sum(weights, axis=2)
    value_split = value_rows.reshape(value_rows.shape[0], heads_here, HEAD_DIM)
    blended = jnp.einsum(
        "hqk,khd->qhd",
        weights.astype(jnp.bfloat16),
        value_split,
        preferred_element_type=jnp.float32,
    )
    row_any = jnp.any(allowed, axis=1)
    peak_score = jnp.where(row_any[None, :], peak_score, LOW_SCORE)
    return (peak_score.T, weight_sum.T, blended)


def local(
    hidden_in,
    queries,
    new_keys,
    new_values,
    query_gain,
    key_gain,
    cache_keys,
    cache_values,
    seg_ids,
    cache_pages,
    page_table,
    out_weight,
    out_bias,
    gate_mod,
):
    tok_dev, local_width = queries.shape
    heads_local = local_width // HEAD_DIM
    groups = lax.axis_size("req")
    device = lax.axis_index("req")
    total_tokens = tok_dev * groups
    seg_most = 2 * tok_dev
    slot_count = cache_keys.shape[0]
    page_len = cache_keys.shape[1]
    request_count = cache_pages.shape[0]
    total_pages = page_table.shape[0]
    first_row = device * tok_dev
    own_rows = first_row + jnp.arange(tok_dev, dtype=jnp.int32)
    own_segs = lax.dynamic_slice_in_dim(seg_ids, first_row, tok_dev, 0)
    req_ids = jnp.arange(request_count, dtype=jnp.int32)
    starts = jnp.sum((seg_ids[None, :] < req_ids[:, None]).astype(jnp.int32), axis=1)
    own_pick = own_segs[:, None] == req_ids[None, :]
    own_start = jnp.sum(jnp.where(own_pick, starts[None, :], 0), axis=1)
    own_cache = jnp.sum(jnp.where(own_pick, cache_pages[None, :], 0), axis=1)
    positions = own_cache * page_len + own_rows - own_start
    wide_q = queries.astype(jnp.float32)
    wide_k = new_keys.astype(jnp.float32)
    sums_q, sums_k = lax.psum(
        (jnp.sum(wide_q * wide_q, axis=1), jnp.sum(wide_k * wide_k, axis=1)), "tp"
    )
    q_rot = turn_heads(
        wide_q * lax.rsqrt(sums_q[:, None] / D + EPSILON) * query_gain[None, :], positions
    )
    k_rot = turn_heads(
        wide_k * lax.rsqrt(sums_k[:, None] / D + EPSILON) * key_gain[None, :], positions
    )
    moved = {}
    for distance in (1, 2):
        moved[distance] = passed_along((k_rot, new_values), "req", distance)
    keys_near = jnp.concatenate([moved[2][0], moved[1][0], k_rot], axis=0)
    values_near = jnp.concatenate([moved[2][1], moved[1][1], new_values], axis=0)
    front_segs = jnp.concatenate([jnp.full((2 * tok_dev,), -1, jnp.int32), seg_ids])
    near_segs = lax.dynamic_slice_in_dim(front_segs, first_row, 3 * tok_dev, 0)
    near_rows = first_row - 2 * tok_dev + jnp.arange(3 * tok_dev, dtype=jnp.int32)
    near_allowed = (near_segs[None, :] == own_segs[:, None]) & (
        near_rows[None, :] <= own_rows[:, None]
    )
    near_part = attend_block(q_rot, keys_near, values_near, near_allowed)
    gathered = lax.all_gather(q_rot, "req", axis=0, tiled=True)
    padded_queries = jnp.concatenate(
        [gathered, jnp.zeros((seg_most, local_width), jnp.bfloat16)], axis=0
    )
    padded_segs = jnp.concatenate([seg_ids, jnp.full((seg_most,), -1, jnp.int32)])
    physical = device * slot_count + jnp.arange(slot_count, dtype=jnp.int32)
    logical = jnp.sum(
        jnp.where(
            page_table[None, :] == physical[:, None],
            jnp.arange(total_pages, dtype=jnp.int32)[None, :],
            0,
        ),
        axis=1,
    )
    page_ends = jnp.cumsum(cache_pages)
    owners = jnp.sum((page_ends[None, :] <= logical[:, None]).astype(jnp.int32), axis=1)
    owner_starts = jnp.sum(
        jnp.where(owners[:, None] == req_ids[None, :], starts[None, :], 0), axis=1
    )

    def absorb_page(running, page_item):
        page_keys, page_values, owner_req, owner_row = page_item
        window = lax.dynamic_slice_in_dim(padded_queries, owner_row, seg_most, 0)
        inside = lax.dynamic_slice_in_dim(padded_segs, owner_row, seg_most, 0) == owner_req
        allowed = jnp.broadcast_to(inside[:, None], (seg_most, page_len))
        fresh = attend_block(window, page_keys, page_values, allowed)
        earlier = tuple(
            (lax.dynamic_slice_in_dim(part_arr, owner_row, seg_most, 0) for part_arr in running)
        )
        merged = combine_pair(earlier, fresh)
        updated = tuple(
            (
                lax.dynamic_update_slice_in_dim(whole_arr, new_arr, owner_row, 0)
                for whole_arr, new_arr in zip(running, merged)
            )
        )
        return (updated, None)

    start_state = (
        jnp.full((total_tokens + seg_most, heads_local), LOW_SCORE, jnp.float32),
        jnp.zeros((total_tokens + seg_most, heads_local), jnp.float32),
        jnp.zeros((total_tokens + seg_most, heads_local, HEAD_DIM), jnp.float32),
    )
    running, _ = lax.scan(
        absorb_page, start_state, (cache_keys, cache_values, owners, owner_starts)
    )
    cache_max = running[0][:total_tokens]
    cache_sum = running[1][:total_tokens]
    holder_out = (running[2][:total_tokens] / jnp.maximum(cache_sum, 1.0)[..., None]).astype(
        jnp.bfloat16
    )
    common_max = lax.pmax(cache_max, "req")
    scaled = cache_sum * jnp.exp(cache_max - common_max)
    part_sum, part_out = (
        lax.psum_scatter(scaled, "req", scatter_dimension=0, tiled=True),
        lax.psum_scatter(
            holder_out.astype(jnp.float32) * scaled[..., None],
            "req",
            scatter_dimension=0,
            tiled=True,
        ),
    )
    own_max = lax.dynamic_slice_in_dim(common_max, first_row, tok_dev, 0)
    highest, total_sum, total_out = combine_pair((own_max, part_sum, part_out), near_part)
    attended = (total_out / total_sum[..., None]).reshape(tok_dev, local_width).astype(jnp.bfloat16)
    partial_proj = jnp.dot(
        attended,
        lax.all_gather(out_weight, "req", axis=1, tiled=True),
        preferred_element_type=jnp.float32,
    )
    summed = lax.psum_scatter(partial_proj, "tp", scatter_dimension=1, tiled=True)
    gate_rows = jnp.dot(own_pick.astype(jnp.float32), gate_mod, precision=lax.Precision.HIGHEST)
    return (hidden_in.astype(jnp.float32) + gate_rows * (summed + out_bias[None, :])).astype(
        jnp.bfloat16
    )


def solution(mesh):
    return jax.shard_map(
        local,
        mesh=mesh,
        in_specs=(
            P("req", "tp"),
            P("req", "tp"),
            P("req", "tp"),
            P("req", "tp"),
            P("tp"),
            P("tp"),
            P("req", None, "tp"),
            P("req", None, "tp"),
            P(),
            P(),
            P(),
            P("tp", "req"),
            P("tp"),
            P(None, "tp"),
        ),
        out_specs=P("req", "tp"),
        check_vma=False,
    )
```

profile of v0, /device:TPU:0, one launch (start us, length us, event | category | flops | bytes accessed | tf_op | source)
XLA Modules:
  0.0 1808.4 jit_solution(11236233920601688400)
XLA Ops:
  21.1 171.0 %all-gather.3.cloned.1.call-done = bf16[2048,2560]{0,1:T(8,128)(2,1)} async-done(((bf16[128,2560]{0,1:T(8,128)(2,1)}), bf16[2048,2560]{0,1:T(8,128)(2,1)}) %all-gather.3.cloned.1.call-update) | async-done | bytes 10485776 | tf_op jit(solution)/shard_map/all_gather | solution.py:138
  213.5 648.7 %while.14 = (s32[]{:T(128)}, f32[2304,20]{0,1:T(8,128)}, f32[2304,20]{0,1:T(8,128)}, f32[2304,20,128]{0,2,1:T(8,128)}, s32[16]{0:T(128)S(1)}, /*index=5*/s32[230...) while((s32[]{:T(128)}, f32[2304,20]{0,1:T(8,128)}, ...), condition=%wide.region_13.14_spmd, body=%wide.region_9.13_spmd.sunk | while | flops 690185216 | bytes 69914824 | solution.py:181
  236.4 14.9 dynamic_update_slice.14
  277.4 14.8 dynamic_update_slice.14
  318.4 14.8 dynamic_update_slice.14
  359.3 12.8 dynamic_update_slice.14
  397.9 12.8 dynamic_update_slice.14
  436.5 14.9 dynamic_update_slice.14
  477.5 14.9 dynamic_update_slice.14
  518.5 14.9 dynamic_update_slice.14
  559.4 14.9 dynamic_update_slice.14
  600.5 12.8 dynamic_update_slice.14
  639.1 14.9 dynamic_update_slice.14
  680.1 14.9 dynamic_update_slice.14
  721.1 14.9 dynamic_update_slice.14
  762.1 14.9 dynamic_update_slice.14
  803.1 14.9 dynamic_update_slice.14
  844.1 14.9 dynamic_update_slice.14
  864.0 110.9 %all-reduce.6.cloned.1.call-done = f32[2048,20]{0,1:T(8,128)} async-done(((f32[2048,20]{0,1:T(8,128)}), f32[2048,20]{0,1:T(8,128)}) %all-reduce.6.cloned.1.call-update) | async-done | bytes 163856 | tf_op jit(solution)/shard_map/pmax | solution.py:189
  976.8 17.1 convert_multiply_fusion
  1012.0 31.3 %collective-permute-done.2 = bf16[128,2560]{1,0:T(8,128)(2,1)} collective-permute-done((bf16[128,2560]{1,0:T(8,128)(2,1)}, bf16[128,2560]{1,0:T(8,128)(2,1)}, u32[]{:S(2)}, u32[]{:S(2)}) %collective-permute-start.2) | collective-permute-done | bytes 655392 | tf_op jit(solution)/shard_map/ppermute | solution.py:19
  1060.8 421.2 %reduce-scatter.4.cloned.1.call-done = f32[128,20,128]{0,2,1:T(8,128)} async-done(((f32[2048,20,128]{0,2,1:T(8,128)}), f32[128,20,128]{0,2,1:T(8,128)}) %reduce-scatter.4.cloned.1.call-update) | async-done | bytes 1310736 | tf_op jit(solution)/shard_map/reduce_scatter | solution.py:193
  1485.8 289.2 %all-gather.5.cloned.1.call-done = bf16[2560,5120]{0,1:T(8,128)(2,1)} async-done(((bf16[2560,320]{0,1:T(8,128)(2,1)}), bf16[2560,5120]{0,1:T(8,128)(2,1)}) %all-gather.5.cloned.1.call-update) | async-done | bytes 26214416 | tf_op jit(solution)/shard_map/all_gather | solution.py:205
  1775.1 15.0 fusion.58
  (587 shorter events, 474.4 us)
Async XLA Ops:
  6.5 1792.1 %copy-start = (f32[16,2560]{1,0:T(8,128)S(1)}, f32[16,2560]{1,0:T(8,128)}, u32[]{:S(2)}) copy-start(f32[16,2560]{1,0:T(8,128)} %param.29) | copy-start | bytes 491524
  6.5 185.6 %all-gather.3.cloned.1.call-start = ((), (), s32[]{:S(2)}) async-start(), calls=%async_computation.3 | async-start | bytes 11141120 | tf_op jit(solution)/shard_map/all_gather | solution.py:138
  19.1 182.6 %copy-start.4 = (bf16[128,20,128]{2,0,1:T(8,128)(2,1)}, bf16[128,20,128]{2,0,1:T(8,128)(2,1)S(1)}, u32[]{:S(2)}) copy-start(bf16[128,20,128]{2,0,1:T(8,128)(2,1)S(1)} %maximum_convert_fusion) | copy-start | bytes 1966084
  20.2 954.7 %all-reduce.6.cloned.1.call-start = ((), (), s32[]{:S(2)}) async-start(), calls=%async_computation.4 | async-start | bytes 393216 | tf_op jit(solution)/shard_map/pmax | solution.py:189
  477.4 18.0 copy-start.14
  477.5 18.0 copy-start.23
  559.4 18.0 copy-start.14
  559.4 18.0 copy-start.23
  639.0 18.0 copy-start.14
  639.1 18.0 copy-start.23
  762.0 18.0 copy-start.14
  803.1 18.0 copy-start.14
  844.1 18.1 copy-start.14
  844.1 18.0 copy-start.23
  844.1 18.0 copy-start.25
  863.8 196.3 %reduce-scatter.6.cloned.1.call-start = ((), (), s32[]{:S(2)}) async-start(), calls=%async_computation.6 | async-start | bytes 208896 | tf_op jit(solution)/shard_map/reduce_scatter | solution.py:192
  976.8 505.2 %reduce-scatter.4.cloned.1.call-start = ((), (), s32[]{:S(2)}) async-start(), calls=%async_computation.5 | async-start | bytes 22282240 | tf_op jit(solution)/shard_map/reduce_scatter | solution.py:193
  994.0 781.1 %all-gather.5.cloned.1.call-start = ((), (), s32[]{:S(2)}) async-start(), calls=%async_computation.7 | async-start | bytes 27852800 | tf_op jit(solution)/shard_map/all_gather | solution.py:205
  994.6 804.1 %reduce-scatter.8.cloned.1.call-start = ((), (), s32[]{:S(2)}) async-start(), calls=%async_computation.8 | async-start | bytes 3932160 | tf_op jit(solution)/shard_map/reduce_scatter | solution.py:208
  994.6 48.7 %collective-permute-start.2 = (bf16[128,2560]{1,0:T(8,128)(2,1)}, bf16[128,2560]{1,0:T(8,128)(2,1)}, u32[]{:S(2)}, u32[]{:S(2)}) collective-permute-start(bf16[128,2560]{1,0:T(8,128)(2,1)} %param.19), channel_id=1, source_target_pairs={{0,4},{2,6},{4,8},{6,10},{8,12},{10,14},{12,16},{14,18},{16,20},{1... | collective-permute-start | bytes 1966088 | tf_op jit(solution)/shard_map/ppermute | solution.py:19
  998.8 44.5 %collective-permute-start.3 = (bf16[128,2560]{1,0:T(8,128)(2,1)}, bf16[128,2560]{1,0:T(8,128)(2,1)}, u32[]{:S(2)}, u32[]{:S(2)}) collective-permute-start(bf16[128,2560]{1,0:T(8,128)(2,1)} %param.19), channel_id=1, source_target_pairs={{0,2},{2,4},{4,6},{6,8},{8,10},{10,12},{12,14},{14,16},{16,18},{18... | collective-permute-start | bytes 1966088 | tf_op jit(solution)/shard_map/ppermute | solution.py:19
  1005.7 48.6 %collective-permute-start = (bf16[128,2560]{0,1:T(8,128)(2,1)S(1)}, bf16[128,2560]{0,1:T(8,128)(2,1)S(1)}, u32[]{:S(2)}, u32[]{:S(2)}) collective-permute-start(bf16[128,2560]{0,1:T(8,128)(2,1)S(1)} %bitcast.81), channel_id=1, source_target_pairs={{0,4},{2,6},{4,8},{6,10},{8,12},{10,14},{12,16},{14,18},{16,20},{1... | collective-permute-start | bytes 1966088 | tf_op jit(solution)/shard_map/ppermute | solution.py:19
  1007.5 46.8 %collective-permute-start.1 = (bf16[128,2560]{0,1:T(8,128)(2,1)S(1)}, bf16[128,2560]{0,1:T(8,128)(2,1)}, u32[]{:S(2)}, u32[]{:S(2)}) collective-permute-start(bf16[128,2560]{0,1:T(8,128)(2,1)S(1)} %bitcast.82), channel_id=1, source_target_pairs={{0,2},{2,4},{4,6},{6,8},{8,10},{10,12},{12,14},{14,16},{16,18},{18... | collective-permute-start | bytes 1966088 | tf_op jit(solution)/shard_map/ppermute | solution.py:19
  1058.7 423.3 %copy-start.6 = (bf16[384,2560]{0,1:T(8,128)(2,1)S(1)}, bf16[384,2560]{0,1:T(8,128)(2,1)}, u32[]{:S(2)}) copy-start(bf16[384,2560]{0,1:T(8,128)(2,1)} %copy.50) | copy-start | bytes 5898244
  (132 other events, 1262.9 us)
Sparse Core Ops, SparseCore 0:
  20.3 171.7 all-gather.2
  863.9 110.9 all-reduce.5
  977.2 75.3 reduce-scatter.5
  1054.8 427.1 reduce-scatter.3
  1484.9 290.0 all-gather.4
  1790.2 8.3 reduce-scatter.7
where the time goes:
time: 1820 us; the launch traced here: 1810 us
  waiting for transfers between devices  1040 us (57%)
  local copies, waits for them, and re-layouts  489 us (27%)
  matrix products  127 us (7%)
  other arithmetic  89.5 us (5%)
  loops' own time  32.3 us (2%)
    reduce_scatter x1, waiting for transfers between devices, local(): lax.psum_scatter(holder_out.astype(jnp.float32) * scaled[..., None], 'req...  421 us
    all_gather x1, waiting for transfers between devices, local(): lax.all_gather(out_weight, 'req', axis=1, tiled=True)  289 us
    dynamic_update_slice x48, local copies, waits for them, and re-layouts, absorb_page(): lax.dynamic_update_slice_in_dim(whole_arr, new_arr, owner_row, 0)  280 us
    all_gather x1, waiting for transfers between devices, local(): gathered = lax.all_gather(q_rot, 'req', axis=0, tiled=True)  171 us
    dynamic_slice x80, local copies, waits for them, and re-layouts, local(): lax.scan(absorb_page, start_state, (cache_keys, cache_values, owners, own...  122 us
    pmax x1, waiting for transfers between devices, local(): common_max = lax.pmax(cache_max, 'req')  111 us
    dot_general x17, matrix products, attend_block(): jnp.einsum('hqk,khd->qhd', weights.astype(jnp.bfloat16), value_split, pre...  91.7 us
    ppermute x4, waiting for transfers between devices, passed_along(): return lax.ppermute(value, axis, pairs)  38.3 us
  transfers between devices with their start and end apart: 10, of which 7 were waited for; matrix products, arithmetic and copies ran while one was open for 2% of the time, Pallas kernels for 0%

commit v1 on v0

v1 whole, which is shorter than its diff:
```python
import functools
import math

import jax
import jax.numpy as jnp
from jax import lax
from jax.experimental import pallas as pl
from jax.experimental.pallas import tpu as pltpu
from jax.sharding import PartitionSpec as P

HEAD_DIM = 128
EPSILON = 1e-06
LOW_SCORE = -1e30
PLANE = 4
PIECE = 16
SCORE_SCALE = math.log2(math.e) / math.sqrt(HEAD_DIM)


def send_xor(value, by):
    size = lax.axis_size("req")
    return lax.ppermute(value, "req", [(i, i ^ by) for i in range(size)])


def send_line(value, by):
    size = lax.axis_size("req")
    line = size // PLANE
    pairs = [(i, ((i // PLANE + by) % line) * PLANE + i % PLANE) for i in range(size)]
    return lax.ppermute(value, "req", pairs)


def group_count(width):
    return 2 if width // HEAD_DIM % 2 == 0 else 1


def turn_kernel(q_ref, k_ref, scale_ref, gain_q_ref, gain_k_ref, cos_ref, sin_ref, *outs):
    cosine = cos_ref[...]
    sine = sin_ref[...]
    width = q_ref.shape[1]
    group_width = width // group_count(width)
    k_out = outs[-1]
    for side, (ref, gain) in enumerate(((q_ref, gain_q_ref), (k_ref, gain_k_ref))):
        scale = scale_ref[:, side : side + 1]
        for col in range(0, width, HEAD_DIM):
            x = ref[:, col : col + HEAD_DIM].astype(jnp.float32) * scale * gain[:, col : col + HEAD_DIM]
            y = (x * cosine + pltpu.roll(x, HEAD_DIM // 2, 1) * sine).astype(jnp.bfloat16)
            if side == 1:
                k_out[:, col : col + HEAD_DIM] = y
            else:
                at = col % group_width
                outs[col // group_width][:, at : at + HEAD_DIM] = y


def turn(queries, new_keys, scales, gain_q, gain_k, cosine, sine):
    rows, width = queries.shape
    groups = group_count(width)
    part = jax.ShapeDtypeStruct((rows, width // groups), jnp.bfloat16)
    return pl.pallas_call(
        turn_kernel,
        out_shape=[part] * groups + [jax.ShapeDtypeStruct((rows, width), jnp.bfloat16)],
        compiler_params=pltpu.CompilerParams(vmem_limit_bytes=32 * 2**20),
        name="norm_turn",
    )(queries, new_keys, scales, gain_q[None], gain_k[None], cosine, sine)


def attend_kernel(
    table_ref,
    slot_ref,
    q_low_ref,
    q_high_ref,
    keys_ref,
    values_ref,
    near_keys_ref,
    near_values_ref,
    near_starts_ref,
    keep_ref,
    send_ref,
    q_all,
    acc,
    peak,
    total,
    sems,
):
    step = pl.program_id(0)
    half, rows, width = q_low_ref.shape
    blocks = 2 * half
    heads = width // HEAD_DIM
    lane = lax.broadcasted_iota(jnp.int32, (1, rows), 1)

    def update(slots, keys, values, row_masks, allowed):
        old_peak = [peak[s] for s in slots]
        old_total = [total[s] for s in slots]
        new_peak = [[] for _ in slots]
        new_total = [[] for _ in slots]
        for h in range(heads):
            cols = slice(h * HEAD_DIM, (h + 1) * HEAD_DIM)
            q = [q_all[s, :, cols] for s in slots]
            q = q[0] if len(q) == 1 else jnp.concatenate(q, axis=0)
            scores = lax.dot_general(
                keys[:, cols], q, (((1,), (1,)), ((), ())), preferred_element_type=jnp.float32
            )
            if allowed is not None:
                scores = jnp.where(allowed, scores, LOW_SCORE)
            before = [p[h : h + 1] for p in old_peak]
            before = before[0] if len(before) == 1 else jnp.concatenate(before, axis=1)
            top = jnp.maximum(jnp.max(scores, axis=0, keepdims=True), before)
            weights = jnp.exp2(scores * SCORE_SCALE - top * SCORE_SCALE)
            weight_sum = jnp.sum(weights, axis=0, keepdims=True)
            fade = jnp.exp2((before - top) * SCORE_SCALE)
            blended = lax.dot_general(
                values[:, cols],
                weights.astype(jnp.bfloat16),
                (((0,), (0,)), ((), ())),
                preferred_element_type=jnp.float32,
            )
            for i, s in enumerate(slots):
                span = slice(i * rows, (i + 1) * rows)
                mask = row_masks[i]
                held = acc[s, cols, :]
                acc[s, cols, :] = jnp.where(mask, held * fade[:, span] + blended[:, span], held)
                new_peak[i].append(jnp.where(mask, top[:, span], old_peak[i][h : h + 1]))
                earlier = old_total[i][h : h + 1]
                new_total[i].append(
                    jnp.where(mask, earlier * fade[:, span] + weight_sum[:, span], earlier)
                )
        for i, s in enumerate(slots):
            for h in range(heads):
                peak[s, h : h + 1, :] = new_peak[i][h]
                total[s, h : h + 1, :] = new_total[i][h]

    @pl.when(step == 0)
    def _():
        low = pltpu.make_async_copy(q_low_ref, q_all.at[pl.ds(0, half)], sems.at[0])
        high = pltpu.make_async_copy(q_high_ref, q_all.at[pl.ds(half, half)], sems.at[1])
        low.start()
        high.start()
        acc[...] = jnp.zeros_like(acc)
        peak[...] = jnp.full(peak.shape, LOW_SCORE, jnp.float32)
        total[...] = jnp.zeros_like(total)
        low.wait()
        high.wait()
        first = slot_ref[blocks + 1]

        def near_block(j, carry):
            slot = slot_ref[jnp.minimum(first + j, blocks)]
            row = (first + j) * rows + lane
            begin = near_starts_ref[j]
            key = first * rows + lax.broadcasted_iota(jnp.int32, (rows, rows), 0)
            allowed = (key >= begin) & (key <= row)
            some = begin < (first + 1) * rows
            update([slot], near_keys_ref[...], near_values_ref[...], [some], allowed)
            return carry

        lax.fori_loop(0, 3, near_block, 0)

    @pl.when(step > 0)
    def _():
        begin = table_ref[4 * step - 4]
        end = table_ref[4 * step - 3]
        first = table_ref[4 * step - 2]
        count = table_ref[4 * step - 1]

        def pair(j, carry):
            low = first + 2 * j
            row = low * rows + lane
            masks = [(r >= begin) & (r < end) for r in (row, row + rows)]
            update([slot_ref[low], slot_ref[low + 1]], keys_ref[0], values_ref[0], masks, None)
            return carry

        lax.fori_loop(0, count, pair, 0)

    @pl.when(step == pl.num_programs(0) - 1)
    def _():
        for at, out in ((0, keep_ref), (half, send_ref)):

            def finish(i, carry, at=at, out=out):
                sums = jnp.maximum(total[at + i], 1.0)
                write_block(
                    out.at[i],
                    lambda h: acc[at + i, h * HEAD_DIM : (h + 1) * HEAD_DIM, :],
                    1.0 / sums,
                    peak[at + i] * SCORE_SCALE + jnp.log2(sums),
                    heads,
                )
                return carry

            lax.fori_loop(0, half, finish, 0)


def write_block(out, block, factors, levels, heads):
    for h in range(heads):
        out[h * HEAD_DIM : (h + 1) * HEAD_DIM, :] = (block(h) * factors[h : h + 1]).astype(jnp.bfloat16)
    left = levels
    for i in range(3):
        part = left.astype(jnp.bfloat16)
        at = heads * HEAD_DIM + i * PIECE
        out[at : at + PIECE, :] = part
        left = left - part.astype(jnp.float32)


def read_levels(ref, heads):
    at = heads * HEAD_DIM
    parts = [ref[at + i * PIECE : at + (i + 1) * PIECE, :].astype(jnp.float32) for i in range(3)]
    return parts[0] + (parts[1] + parts[2])


def attend(group, table, slots, q_low, q_high, cache_keys, cache_values, near_keys, near_values, near_starts):
    half, rows, width = q_low.shape
    pages, page_len, _ = cache_keys.shape
    heads = width // HEAD_DIM
    blocks = 2 * half
    out = jax.ShapeDtypeStruct((half, width + 3 * PIECE, rows), jnp.bfloat16)
    page_spec = pl.BlockSpec((1, page_len, width), lambda i, *_: (jnp.maximum(i - 1, 0), 0, group))
    near_spec = pl.BlockSpec((rows, width), lambda i, *_: (0, group))
    whole = lambda shape: pl.BlockSpec(shape, lambda i, *_: (0,) * len(shape))
    return pl.pallas_call(
        attend_kernel,
        grid_spec=pltpu.PrefetchScalarGridSpec(
            num_scalar_prefetch=2,
            grid=(pages + 1,),
            in_specs=[
                pl.BlockSpec(memory_space=pl.ANY),
                pl.BlockSpec(memory_space=pl.ANY),
                page_spec,
                page_spec,
                near_spec,
                near_spec,
                whole((3, 1, rows)),
            ],
            out_specs=[whole(out.shape), whole(out.shape)],
            scratch_shapes=[
                pltpu.VMEM((blocks + 1, rows, width), jnp.bfloat16),
                pltpu.VMEM((blocks + 1, width, rows), jnp.float32),
                pltpu.VMEM((blocks + 1, PIECE, rows), jnp.float32),
                pltpu.VMEM((blocks + 1, PIECE, rows), jnp.float32),
                pltpu.SemaphoreType.DMA((2,)),
            ],
        ),
        out_shape=[out, out],
        compiler_params=pltpu.CompilerParams(
            dimension_semantics=("arbitrary",), vmem_limit_bytes=56 * 2**20
        ),
        cost_estimate=pl.CostEstimate(
            flops=pages * heads * 256 * page_len * HEAD_DIM * 16,
            bytes_accessed=pages * page_len * width * 4,
            transcendentals=pages * heads * 256 * page_len,
        ),
        name="cache_attend",
    )(table, slots, q_low, q_high, cache_keys, cache_values, near_keys, near_values, near_starts)


def merged(refs, heads):
    levels = [read_levels(ref, heads) for ref in refs]
    top = functools.reduce(jnp.maximum, levels)
    weights = [jnp.exp2(level - top) for level in levels]
    total = functools.reduce(jnp.add, weights)
    factors = [w / total for w in weights]

    def block(h):
        cols = slice(h * HEAD_DIM, (h + 1) * HEAD_DIM)
        return functools.reduce(
            jnp.add, [ref[cols, :].astype(jnp.float32) * f[h : h + 1] for ref, f in zip(refs, factors)]
        )

    return block, top + jnp.log2(total)


def combine_kernel(mine_low, mine_high, got_low, got_high, keep_ref, send_ref):
    heads = (mine_low.shape[1] - 3 * PIECE) // HEAD_DIM
    for mine, got, out in ((mine_low, got_low, keep_ref), (mine_high, got_high, send_ref)):
        block, levels = merged([mine.at[0], got.at[0]], heads)
        write_block(out.at[0], block, jnp.ones_like(levels), levels, heads)


def combine(mine, got):
    count, depth, rows = mine.shape
    half = count // 2
    low = pl.BlockSpec((1, depth, rows), lambda i: (i, 0, 0))
    high = pl.BlockSpec((1, depth, rows), lambda i: (i + half, 0, 0))
    out = jax.ShapeDtypeStruct((half, depth, rows), jnp.bfloat16)
    return pl.pallas_call(
        combine_kernel,
        grid=(half,),
        in_specs=[low, high, low, high],
        out_specs=[low, low],
        out_shape=[out, out],
        compiler_params=pltpu.CompilerParams(vmem_limit_bytes=24 * 2**20),
        cost_estimate=pl.CostEstimate(
            flops=count * depth * rows * 4, bytes_accessed=count * depth * rows * 6, transcendentals=0
        ),
        name="combine_pairs",
    )(mine, mine, got, got)


def last_kernel(*refs):
    out_ref = refs[-1]
    heads = out_ref.shape[0] // HEAD_DIM
    block, _ = merged(refs[:-1], heads)
    for h in range(heads):
        out_ref[h * HEAD_DIM : (h + 1) * HEAD_DIM, :] = block(h).astype(jnp.bfloat16)


def combine_last(parts):
    depth, rows = parts[0].shape
    return pl.pallas_call(
        last_kernel,
        out_shape=jax.ShapeDtypeStruct((depth - 3 * PIECE, rows), jnp.bfloat16),
        compiler_params=pltpu.CompilerParams(vmem_limit_bytes=24 * 2**20),
        cost_estimate=pl.CostEstimate(
            flops=len(parts) * depth * rows * 2,
            bytes_accessed=(len(parts) + 1) * depth * rows * 2,
            transcendentals=0,
        ),
        name="combine_last",
    )(*parts)


def local(
    hidden_in,
    queries,
    new_keys,
    new_values,
    query_gain,
    key_gain,
    cache_keys,
    cache_values,
    seg_ids,
    cache_pages,
    page_table,
    out_weight,
    out_bias,
    gate_mod,
):
    tok_dev, local_width = queries.shape
    size = lax.axis_size("req")
    tp_size = lax.axis_size("tp")
    model_width = local_width * tp_size
    line = size // PLANE
    device = lax.axis_index("req")
    spot = device % PLANE
    place = device // PLANE
    slot_count, page_len, _ = cache_keys.shape
    request_count = cache_pages.shape[0]
    total_pages = page_table.shape[0]
    first_row = device * tok_dev
    own_rows = first_row + jnp.arange(tok_dev, dtype=jnp.int32)
    own_segs = lax.dynamic_slice_in_dim(seg_ids, first_row, tok_dev, 0)
    req_ids = jnp.arange(request_count, dtype=jnp.int32)
    starts = jnp.sum((seg_ids[None, :] < req_ids[:, None]).astype(jnp.int32), axis=1)
    ends = jnp.sum((seg_ids[None, :] <= req_ids[:, None]).astype(jnp.int32), axis=1)
    own_pick = own_segs[:, None] == req_ids[None, :]
    own_start = jnp.sum(jnp.where(own_pick, starts[None, :], 0), axis=1)
    own_cache = jnp.sum(jnp.where(own_pick, cache_pages[None, :], 0), axis=1)
    positions = own_cache * page_len + own_rows - own_start

    wide_q = queries.astype(jnp.float32)
    wide_k = new_keys.astype(jnp.float32)
    sums = lax.psum(
        jnp.stack([jnp.sum(wide_q * wide_q, axis=1), jnp.sum(wide_k * wide_k, axis=1)], axis=1), "tp"
    )
    scales = lax.rsqrt(sums / model_width + EPSILON)
    halfway = HEAD_DIM // 2
    frequency = 10000.0 ** (-jnp.arange(halfway, dtype=jnp.float32) / halfway)
    angles = positions.astype(jnp.float32)[:, None] * frequency[None, :]
    cosine = jnp.cos(angles)
    sine = jnp.sin(angles)
    turned = turn(
        queries,
        new_keys,
        scales,
        query_gain,
        key_gain,
        jnp.concatenate([cosine, cosine], axis=1),
        jnp.concatenate([-sine, sine], axis=1),
    )
    q_parts, k_rot = turned[:-1], turned[-1]

    physical = device * slot_count + jnp.arange(slot_count, dtype=jnp.int32)
    logical = jnp.sum(
        jnp.where(
            page_table[None, :] == physical[:, None],
            jnp.arange(total_pages, dtype=jnp.int32)[None, :],
            0,
        ),
        axis=1,
    )
    page_ends = jnp.cumsum(cache_pages)
    owners = jnp.sum((page_ends[None, :] <= logical[:, None]).astype(jnp.int32), axis=1)
    owner_pick = owners[:, None] == req_ids[None, :]
    owner_starts = jnp.sum(jnp.where(owner_pick, starts[None, :], 0), axis=1)
    owner_ends = jnp.sum(jnp.where(owner_pick, ends[None, :], 0), axis=1)
    owner_first = owner_starts // tok_dev
    owner_pairs = ((owner_ends - 1) // tok_dev - owner_first + 2) // 2
    table = jnp.stack([owner_starts, owner_ends, owner_first, owner_pairs], axis=1).reshape(-1)

    near_blocks = device + jnp.arange(3, dtype=jnp.int32)
    near_rows = (near_blocks[:, None] * tok_dev + jnp.arange(tok_dev, dtype=jnp.int32)[None, :]).reshape(-1)
    padded_segs = jnp.concatenate([seg_ids, jnp.full((2 * tok_dev,), -1, jnp.int32)])
    near_segs = lax.dynamic_slice_in_dim(padded_segs, first_row, 3 * tok_dev, 0)
    near_starts = jnp.sum(
        jnp.where(near_segs[:, None] == req_ids[None, :], starts[None, :], 0), axis=1
    )
    near_starts = jnp.where(near_segs < 0, near_rows + size * tok_dev, near_starts)
    near_starts = near_starts.reshape(3, 1, tok_dev)

    block = jnp.arange(size, dtype=jnp.int32)
    back = (place - block // PLANE) % line
    across = (block % PLANE) ^ spot

    def gather_queries(part, order):
        got = [part[None]] + [send_line(part, k)[None] for k in range(1, line)]
        near = jnp.concatenate(got, axis=0)
        low = jnp.concatenate([near, send_xor(near, order[0])], axis=0)
        return low, send_xor(low, order[1])

    attended = []
    for group in range(len(q_parts)):
        order = (2, 1) if group % 2 == 0 else (1, 2)
        low, high = gather_queries(q_parts[group], order)
        slot = jnp.where((across & order[1]) > 0, 2 * line, 0)
        slot = slot + jnp.where((across & order[0]) > 0, line, 0) + back
        slots = jnp.concatenate([slot, jnp.stack([jnp.int32(size), device])])
        keep, send = attend(
            group, table, slots, low, high, cache_keys, cache_values, k_rot, new_values, near_starts
        )
        keep, send = combine(keep, send_xor(send, order[1]))
        parts = combine_line(keep, send_xor(send, order[0]))
        attended.append(combine_last([parts[0]] + [send_line(parts[k], -k) for k in range(1, line)]))
    attended = jnp.concatenate(attended, axis=0)

    weight = out_weight.T
    columns = weight.shape[0]
    gathered = jnp.zeros((line * columns, local_width), jnp.bfloat16)
    for k in range(line):
        got = weight if k == 0 else send_line(weight, k)
        gathered = lax.dynamic_update_slice_in_dim(gathered, got, ((place - k) % line) * columns, 0)

    spread = jnp.concatenate([attended] + [send_xor(attended, k) for k in range(1, PLANE)], axis=1)
    partial_proj = jnp.dot(gathered, spread, preferred_element_type=jnp.float32)
    summed = lax.psum_scatter(partial_proj, "tp", scatter_dimension=0, tiled=True)
    mine = [summed[:, :tok_dev]] + [
        send_xor(summed[:, k * tok_dev : (k + 1) * tok_dev], k) for k in range(1, PLANE)
    ]
    mine = [part.reshape(line // tp_size, columns, tok_dev) for part in mine]
    swapped = [jnp.where((spot & 1) > 0, mine[i ^ 1], mine[i]) for i in range(PLANE)]
    swapped = [jnp.where((spot & 2) > 0, swapped[i ^ 2], swapped[i]) for i in range(PLANE)]
    projected = jnp.stack(swapped, axis=1).reshape(local_width, tok_dev).T

    gate_rows = jnp.dot(own_pick.astype(jnp.float32), gate_mod, precision=lax.Precision.HIGHEST)
    return (hidden_in.astype(jnp.float32) + gate_rows * (projected + out_bias[None, :])).astype(
        jnp.bfloat16
    )


def pair_kernel(mine, got, *outs):
    heads = (mine.shape[1] - 3 * PIECE) // HEAD_DIM
    for i, out in enumerate(outs):
        block, levels = merged([mine.at[i], got.at[i]], heads)
        write_block(out, block, jnp.ones_like(levels), levels, heads)


def combine_line(mine, got):
    count, depth, rows = mine.shape
    out = jax.ShapeDtypeStruct((depth, rows), jnp.bfloat16)
    return pl.pallas_call(
        pair_kernel,
        out_shape=[out] * count,
        compiler_params=pltpu.CompilerParams(vmem_limit_bytes=32 * 2**20),
        cost_estimate=pl.CostEstimate(
            flops=count * depth * rows * 4, bytes_accessed=count * depth * rows * 6, transcendentals=0
        ),
        name="combine_line",
    )(mine, got)


def solution(mesh):
    return jax.shard_map(
        local,
        mesh=mesh,
        in_specs=(
            P("req", "tp"),
            P("req", "tp"),
            P("req", "tp"),
            P("req", "tp"),
            P("tp"),
            P("tp"),
            P("req", None, "tp"),
            P("req", None, "tp"),
            P(),
            P(),
            P(),
            P("tp", "req"),
            P("tp"),
            P(None, "tp"),
        ),
        out_specs=P("req", "tp"),
        check_vma=False,
    )
```

time: 1820 us -> 655 us (0.36)
  waiting for transfers between devices: 1040 us -> 234 us
  local copies, waits for them, and re-layouts: 489 us -> 30.6 us
  starting transfers between devices: 14.1 us -> 198 us
  Pallas kernels: 0 us -> 159 us
  matrix products: 127 us -> 9.58 us
  other arithmetic: 89.5 us -> 8.46 us
  loops' own time: 32.3 us -> 0 us
    all_gather x2 -> x0, waiting for transfers between devices: 460 us -> none  [the longest x1 289 us: local(): lax.all_gather(out_weight, 'req', axis=1, tiled=True)]
    reduce_scatter x3 -> x1, waiting for transfers between devices: 430 us -> 17.9 us  [local(): lax.psum_scatter(partial_proj, 'tp', scatter_dimension=0, tiled=True)]
    dynamic_update_slice x48 -> x4, local copies, waits for them, and re-layouts: 280 us -> 10.9 us  [local(): lax.dynamic_update_slice_in_dim(gathered, got, (place - k) % line * colum...]
    ppermute x4 -> x29, starting transfers between devices: 13.8 us -> 198 us  [the longest x15 170 us: send_line(): return lax.ppermute(value, 'req', pairs)]
    ppermute x4 -> x29, waiting for transfers between devices: 38.3 us -> 216 us  [the longest x14 150 us: send_xor(): return lax.ppermute(value, 'req', [(i, i ^ by) for i in range(size)])]
    pallas_call x0 -> x9, Pallas kernels: none -> 159 us  [the longest x2 149 us: attend(): pl.pallas_call(attend_kernel, grid_spec=pltpu.PrefetchScalarGridSpec(num_...]
    dynamic_slice x96 -> x1, local copies, waits for them, and re-layouts: 157 us -> 0.08 us  [local(): near_segs = lax.dynamic_slice_in_dim(padded_segs, first_row, 3 * tok_dev, 0)]
    dot_general x35 -> x1, matrix products: 124 us -> 7.96 us  [local(): partial_proj = jnp.dot(gathered, spread, preferred_element_type=jnp.float32)]
  transfers between devices with their start and end apart: 10 -> 30, of which waited for: 7 -> 15; matrix products, arithmetic and copies ran while one was open for 2% -> 4% of each run, Pallas kernels for 0% -> 24%
where the time goes in v1:
time: 655 us; the launch traced here: 658 us
  waiting for transfers between devices  234 us (36%)
  starting transfers between devices  198 us (30%)
  Pallas kernels  159 us (24%)
  local copies, waits for them, and re-layouts  30.6 us (5%)
  between operations  13.7 us (2%)
  matrix products  9.58 us (1%)
  other arithmetic  8.46 us (1%)
    ppermute x15, starting transfers between devices, send_line(): return lax.ppermute(value, 'req', pairs)  170 us
    ppermute x14, waiting for transfers between devices, send_xor(): return lax.ppermute(value, 'req', [(i, i ^ by) for i in range(size)])  150 us
    pallas_call x2, Pallas kernels, attend(): pl.pallas_call(attend_kernel, grid_spec=pltpu.PrefetchScalarGridSpec(num_...  149 us
    ppermute x15, waiting for transfers between devices, send_line(): return lax.ppermute(value, 'req', pairs)  66 us
    ppermute x14, starting transfers between devices, send_xor(): return lax.ppermute(value, 'req', [(i, i ^ by) for i in range(size)])  27.8 us
    reduce_scatter x1, waiting for transfers between devices, local(): lax.psum_scatter(partial_proj, 'tp', scatter_dimension=0, tiled=True)  17.9 us
  transfers between devices with their start and end apart: 30, of which 15 were waited for; matrix products, arithmetic and copies ran while one was open for 4% of the time, Pallas kernels for 24%

profile of v1, /device:TPU:0, one launch (start us, length us, event | category | flops | bytes accessed | tf_op | source)
XLA Modules:
  0.0 657.9 jit_solution(6543487157035947271)
XLA Ops:
  11.1 3.9 psum.7
  34.9 11.9 %collective-permute-done.4 = bf16[128,1280]{1,0:T(8,128)(2,1)S(1)} collective-permute-done((bf16[128,1280]{1,0:T(8,128)(2,1)S(1)}, bf16[128,1280]{1,0:T(8,128)(2,1)S(1)}, u32[]{:S(2)}, u32[]{:S(2)}) %collective-permute-start.4) | collective-permute-done | bytes 327712 | tf_op jit(solution)/shard_map/ppermute | solution.py:28
  51.1 26.5 %collective-permute-done.6 = bf16[4,128,1280]{2,1,0:T(8,128)(2,1)S(1)} collective-permute-done((bf16[4,128,1280]{2,1,0:T(8,128)(2,1)S(1)}, bf16[4,128,1280]{2,1,0:T(8,128)(2,1)S(1)}, u32[]{:S(2)}, u32[]{:S(2)}) %collective-permute-start.6) | collective-permute-done | bytes 1310752 | tf_op jit(solution)/shard_map/ppermute | solution.py:21
  83.3 81.5 %collective-permute-done.16 = bf16[4,128,1280]{2,1,0:T(8,128)(2,1)S(1)} collective-permute-done((bf16[4,128,1280]{2,1,0:T(8,128)(2,1)S(1)}, bf16[4,128,1280]{2,1,0:T(8,128)(2,1)S(1)}, u32[]{:S(2)}, u32[]{:S(2)}) %collective-permute-start.16) | collective-permute-done | bytes 1310752 | tf_op jit(solution)/shard_map/ppermute | solution.py:21
  170.3 74.7 %cache_attend.2 = (bf16[8,1328,128]{2,1,0:T(8,128)(2,1)}, bf16[8,1328,128]{2,1,0:T(8,128)(2,1)}) custom-call(s32[64]{0:T(128)} %reshape.367.table_ref, s32[18]{0:T(128)} %fusion.14.slot_ref, bf16[8,128,1280]{2,1,0:T(8,128)(2,1)} %constant_dynamic-update-slice_fusion.q_low_ref, bf16[8,128,1280]{2,1,0:T(8,128)(2,1)} %collective-permute-done.7.q_high_ref, ...), custom_call_target="tpu_custom_call" | custom-call | flops 21474836480 | bytes 20971520 | tf_op jit(solution)/shard_map/cache_attend/pallas_call | solution.py:215
  246.6 74.7 %cache_attend.3 = (bf16[8,1328,128]{2,1,0:T(8,128)(2,1)}, bf16[8,1328,128]{2,1,0:T(8,128)(2,1)}) custom-call(s32[64]{0:T(128)} %reshape.367.table_ref, s32[18]{0:T(128)} %fusion.15.slot_ref, bf16[8,128,1280]{2,1,0:T(8,128)(2,1)} %constant_dynamic-update-slice_fusion.5.q_low_ref, bf16[8,128,1280]{2,1,0:T(8,128)(2,1)} %collective-permute-done.17.q_high_ref, ...), custom_call_target="tpu_custom_call" | custom-call | flops 21474836480 | bytes 20971520 | tf_op jit(solution)/shard_map/cache_attend/pallas_call | solution.py:215
  321.3 11.5 %collective-permute-start.18 = (bf16[8,1328,128]{2,1,0:T(8,128)(2,1)}, bf16[8,1328,128]{2,1,0:T(8,128)(2,1)S(1)}, u32[]{:S(2)}, u32[]{:S(2)}) collective-permute-start(bf16[8,1328,128]{2,1,0:T(8,128)(2,1)} %get-tuple-element.36), channel_id=1, source_target_pairs={{0,4},{2,6},{4,0},{6,2},{8,12},{10,14},{12,8},{14,10},{16,20},{18,... | collective-permute-start | bytes 8159240 | tf_op jit(solution)/shard_map/ppermute | solution.py:21
  332.9 46.1 %collective-permute-start = (bf16[320,2560]{1,0:T(8,128)(2,1)}, bf16[320,2560]{1,0:T(8,128)(2,1)}, u32[]{:S(2)}, u32[]{:S(2)}) collective-permute-start(bf16[320,2560]{1,0:T(8,128)(2,1)} %bitcast), channel_id=1, source_target_pairs={{0,8},{2,10},{4,12},{6,14},{8,16},{10,18},{12,20},{14,22},{16,24},... | collective-permute-start | bytes 4915208 | tf_op jit(solution)/shard_map/ppermute | solution.py:28
  383.0 9.9 %collective-permute-done.18.got_low.got_high = bf16[8,1328,128]{2,1,0:T(8,128)(2,1)S(1)} collective-permute-done((bf16[8,1328,128]{2,1,0:T(8,128)(2,1)}, bf16[8,1328,128]{2,1,0:T(8,128)(2,1)S(1)}, u32[]{:S(2)}, u32[]{:S(2)}) %collective-permute-start.18) | collective-permute-done | bytes 2719776 | tf_op jit(solution)/shard_map/ppermute | solution.py:21
  395.1 20.5 %collective-permute-start.1 = (bf16[320,2560]{1,0:T(8,128)(2,1)}, bf16[320,2560]{1,0:T(8,128)(2,1)}, u32[]{:S(2)}, u32[]{:S(2)}) collective-permute-start(bf16[320,2560]{1,0:T(8,128)(2,1)} %bitcast), channel_id=1, source_target_pairs={{0,16},{2,18},{4,20},{6,22},{8,24},{10,26},{12,28},{14,30},{16,0},... | collective-permute-start | bytes 4915208 | tf_op jit(solution)/shard_map/ppermute | solution.py:28
  415.6 29.9 %collective-permute-start.2 = (bf16[320,2560]{1,0:T(8,128)(2,1)}, bf16[320,2560]{1,0:T(8,128)(2,1)}, u32[]{:S(2)}, u32[]{:S(2)}) collective-permute-start(bf16[320,2560]{1,0:T(8,128)(2,1)} %bitcast), channel_id=1, source_target_pairs={{0,24},{2,26},{4,28},{6,30},{8,0},{10,2},{12,4},{14,6},{16,8},{18,... | collective-permute-start | bytes 4915208 | tf_op jit(solution)/shard_map/ppermute | solution.py:28
  449.3 23.1 %collective-permute-start.11 = (bf16[1328,128]{1,0:T(8,128)(2,1)}, bf16[1328,128]{1,0:T(8,128)(2,1)}, u32[]{:S(2)}, u32[]{:S(2)}) collective-permute-start(bf16[1328,128]{1,0:T(8,128)(2,1)} %get-tuple-element.32), channel_id=1, source_target_pairs={{0,16},{2,18},{4,20},{6,22},{8,24},{10,26},{12,28},{14,30},{16,0},... | collective-permute-start | bytes 1019912 | tf_op jit(solution)/shard_map/ppermute | solution.py:28
  472.4 3.1 broadcast_in_dim.131
  478.8 15.8 %collective-permute-done.10.refs_1_ = bf16[1328,128]{1,0:T(8,128)(2,1)} collective-permute-done((bf16[1328,128]{1,0:T(8,128)(2,1)}, bf16[1328,128]{1,0:T(8,128)(2,1)}, u32[]{:S(2)}, u32[]{:S(2)}) %collective-permute-start.10) | collective-permute-done | bytes 340000 | tf_op jit(solution)/shard_map/ppermute | solution.py:28
  494.6 29.8 %collective-permute-start.20 = (bf16[1328,128]{1,0:T(8,128)(2,1)S(1)}, bf16[1328,128]{1,0:T(8,128)(2,1)S(1)}, u32[]{:S(2)}, u32[]{:S(2)}) collective-permute-start(bf16[1328,128]{1,0:T(8,128)(2,1)S(1)} %get-tuple-element.40), channel_id=1, source_target_pairs={{0,24},{2,26},{4,28},{6,30},{8,0},{10,2},{12,4},{14,6},{16,8},{18,... | collective-permute-start | bytes 1019912 | tf_op jit(solution)/shard_map/ppermute | solution.py:28
  524.4 27.7 %collective-permute-done.11.refs_2_ = bf16[1328,128]{1,0:T(8,128)(2,1)} collective-permute-done((bf16[1328,128]{1,0:T(8,128)(2,1)}, bf16[1328,128]{1,0:T(8,128)(2,1)}, u32[]{:S(2)}, u32[]{:S(2)}) %collective-permute-start.11) | collective-permute-done | bytes 340000 | tf_op jit(solution)/shard_map/ppermute | solution.py:28
  552.1 10.9 %collective-permute-start.22 = (bf16[1328,128]{1,0:T(8,128)(2,1)S(1)}, bf16[1328,128]{1,0:T(8,128)(2,1)S(1)}, u32[]{:S(2)}, u32[]{:S(2)}) collective-permute-start(bf16[1328,128]{1,0:T(8,128)(2,1)S(1)} %get-tuple-element.42), channel_id=1, source_target_pairs={{0,8},{2,10},{4,12},{6,14},{8,16},{10,18},{12,20},{14,22},{16,24},... | collective-permute-start | bytes 1019912 | tf_op jit(solution)/shard_map/ppermute | solution.py:28
  567.3 7.6 %collective-permute-done.21.refs_2_ = bf16[1328,128]{1,0:T(8,128)(2,1)S(1)} collective-permute-done((bf16[1328,128]{1,0:T(8,128)(2,1)S(1)}, bf16[1328,128]{1,0:T(8,128)(2,1)S(1)}, u32[]{:S(2)}, u32[]{:S(2)}) %collective-permute-start.21) | collective-permute-done | bytes 340000 | tf_op jit(solution)/shard_map/ppermute | solution.py:28
  584.2 8.7 %collective-permute-done.23 = bf16[2560,128]{1,0:T(8,128)(2,1)S(1)} collective-permute-done((bf16[2560,128]{1,0:T(8,128)(2,1)S(1)}, bf16[2560,128]{1,0:T(8,128)(2,1)S(1)}, u32[]{:S(2)}, u32[]{:S(2)}) %collective-permute-start.23) | collective-permute-done | bytes 655392 | tf_op jit(solution)/shard_map/ppermute | solution.py:21
  592.9 7.7 %collective-permute-done.24 = bf16[2560,128]{1,0:T(8,128)(2,1)S(1)} collective-permute-done((bf16[2560,128]{1,0:T(8,128)(2,1)S(1)}, bf16[2560,128]{1,0:T(8,128)(2,1)S(1)}, u32[]{:S(2)}, u32[]{:S(2)}) %collective-permute-start.24) | collective-permute-done | bytes 655392 | tf_op jit(solution)/shard_map/ppermute | solution.py:21
  601.9 8.0 %fusion.2 = f32[1280,512]{1,0:T(8,128)} fusion(bf16[1280,2560]{1,0:T(8,128)(2,1)} %constant_dynamic-update-slice_fusion.10, bf16[2560,128]{1,0:T(8,128)(2,1)S(1)} %collective-permute-done.25, bf16[2560,128]{1,0:T(8,128)(2,1)S(1)} %collective-permute-done.24, bf16[2560,128]{1,0:T(8,128)(2,1)S(1)} %collective-permute-done.23, ...), kind=kOutput, calls=%fused_computation.3 | convolution fusion | flops 3368550400 | bytes 11796480 | tf_op jit(solution)/shard_map/dot_general | solution.py:438
  609.9 17.9 %reduce-scatter.2.cloned.1.call-done = f32[640,512]{1,0:T(8,128)} async-done(((f32[1280,512]{1,0:T(8,128)}), f32[640,512]{1,0:T(8,128)}) %reduce-scatter.2.cloned.1.call-update) | async-done | bytes 1310736 | tf_op jit(solution)/shard_map/reduce_scatter | solution.py:439
  632.5 8.0 %collective-permute-done.26 = f32[640,128]{1,0:T(8,128)S(1)} collective-permute-done((f32[640,128]{1,0:T(8,128)S(1)}, f32[640,128]{1,0:T(8,128)S(1)}, u32[]{:S(2)}, u32[]{:S(2)}) %collective-permute-start.26) | collective-permute-done | bytes 327712 | tf_op jit(solution)/shard_map/ppermute | solution.py:21
  640.5 6.4 collective-permute-done.27
  (131 shorter events, 78.6 us)
Async XLA Ops:
  6.6 621.2 %reduce-scatter.2.cloned.1.call-start = ((), (), s32[]{:S(2)}) async-start(), calls=%async_computation.1 | async-start | bytes 3932160 | tf_op jit(solution)/shard_map/reduce_scatter | solution.py:439
  22.1 24.7 %collective-permute-start.4 = (bf16[128,1280]{1,0:T(8,128)(2,1)S(1)}, bf16[128,1280]{1,0:T(8,128)(2,1)S(1)}, u32[]{:S(2)}, u32[]{:S(2)}) collective-permute-start(bf16[128,1280]{1,0:T(8,128)(2,1)S(1)} %get-tuple-element.24), channel_id=1, source_target_pairs={{0,16},{2,18},{4,20},{6,22},{8,24},{10,26},{12,28},{14,30},{16,0},... | collective-permute-start | bytes 983048 | tf_op jit(solution)/shard_map/ppermute | solution.py:28
  26.0 54.4 %collective-permute-start.13 = (bf16[128,1280]{1,0:T(8,128)(2,1)S(1)}, bf16[128,1280]{1,0:T(8,128)(2,1)S(1)}, u32[]{:S(2)}, u32[]{:S(2)}) collective-permute-start(bf16[128,1280]{1,0:T(8,128)(2,1)S(1)} %get-tuple-element.34), channel_id=1, source_target_pairs={{0,8},{2,10},{4,12},{6,14},{8,16},{10,18},{12,20},{14,22},{16,24},... | collective-permute-start | bytes 983048 | tf_op jit(solution)/shard_map/ppermute | solution.py:28
  26.7 53.8 %collective-permute-start.14 = (bf16[128,1280]{1,0:T(8,128)(2,1)S(1)}, bf16[128,1280]{1,0:T(8,128)(2,1)S(1)}, u32[]{:S(2)}, u32[]{:S(2)}) collective-permute-start(bf16[128,1280]{1,0:T(8,128)(2,1)S(1)} %get-tuple-element.34), channel_id=1, source_target_pairs={{0,16},{2,18},{4,20},{6,22},{8,24},{10,26},{12,28},{14,30},{16,0},... | collective-permute-start | bytes 983048 | tf_op jit(solution)/shard_map/ppermute | solution.py:28
  32.7 47.7 %collective-permute-start.15 = (bf16[128,1280]{1,0:T(8,128)(2,1)S(1)}, bf16[128,1280]{1,0:T(8,128)(2,1)S(1)}, u32[]{:S(2)}, u32[]{:S(2)}) collective-permute-start(bf16[128,1280]{1,0:T(8,128)(2,1)S(1)} %get-tuple-element.34), channel_id=1, source_target_pairs={{0,24},{2,26},{4,28},{6,30},{8,0},{10,2},{12,4},{14,6},{16,8},{18,... | collective-permute-start | bytes 983048 | tf_op jit(solution)/shard_map/ppermute | solution.py:28
  47.0 30.6 %collective-permute-start.6 = (bf16[4,128,1280]{2,1,0:T(8,128)(2,1)S(1)}, bf16[4,128,1280]{2,1,0:T(8,128)(2,1)S(1)}, u32[]{:S(2)}, u32[]{:S(2)}) collective-permute-start(bf16[4,128,1280]{2,1,0:T(8,128)(2,1)S(1)} %pad_maximum_fusion), channel_id=1, source_target_pairs={{0,4},{2,6},{4,0},{6,2},{8,12},{10,14},{12,8},{14,10},{16,20},{18,... | collective-permute-start | bytes 3932168 | tf_op jit(solution)/shard_map/ppermute | solution.py:21
  78.7 91.6 %collective-permute-start.7 = (bf16[8,128,1280]{2,1,0:T(8,128)(2,1)}, bf16[8,128,1280]{2,1,0:T(8,128)(2,1)}, u32[]{:S(2)}, u32[]{:S(2)}) collective-permute-start(bf16[8,128,1280]{2,1,0:T(8,128)(2,1)} %constant_dynamic-update-slice_fusion.q_low_ref), channel_id=1, source_target_pairs={{0,2},{2,0},{4,6},{6,4},{8,10},{10,8},{12,14},{14,12},{16,18},{18,... | collective-permute-start | bytes 7864328 | tf_op jit(solution)/shard_map/ppermute | solution.py:21
  80.6 84.2 %collective-permute-start.16 = (bf16[4,128,1280]{2,1,0:T(8,128)(2,1)S(1)}, bf16[4,128,1280]{2,1,0:T(8,128)(2,1)S(1)}, u32[]{:S(2)}, u32[]{:S(2)}) collective-permute-start(bf16[4,128,1280]{2,1,0:T(8,128)(2,1)S(1)} %pad_maximum_fusion.1), channel_id=1, source_target_pairs={{0,2},{2,0},{4,6},{6,4},{8,10},{10,8},{12,14},{14,12},{16,18},{18,... | collective-permute-start | bytes 3932168 | tf_op jit(solution)/shard_map/ppermute | solution.py:21
  166.0 80.6 %collective-permute-start.17 = (bf16[8,128,1280]{2,1,0:T(8,128)(2,1)}, bf16[8,128,1280]{2,1,0:T(8,128)(2,1)}, u32[]{:S(2)}, u32[]{:S(2)}) collective-permute-start(bf16[8,128,1280]{2,1,0:T(8,128)(2,1)} %constant_dynamic-update-slice_fusion.5.q_low_ref), channel_id=1, source_target_pairs={{0,4},{2,6},{4,0},{6,2},{8,12},{10,14},{12,8},{14,10},{16,20},{18,... | collective-permute-start | bytes 7864328 | tf_op jit(solution)/shard_map/ppermute | solution.py:21
  245.1 133.9 %collective-permute-start.8 = (bf16[8,1328,128]{2,1,0:T(8,128)(2,1)}, bf16[8,1328,128]{2,1,0:T(8,128)(2,1)S(1)}, u32[]{:S(2)}, u32[]{:S(2)}) collective-permute-start(bf16[8,1328,128]{2,1,0:T(8,128)(2,1)} %get-tuple-element.27), channel_id=1, source_target_pairs={{0,2},{2,0},{4,6},{6,4},{8,10},{10,8},{12,14},{14,12},{16,18},{18,... | collective-permute-start | bytes 8159240 | tf_op jit(solution)/shard_map/ppermute | solution.py:21
  321.3 71.6 %collective-permute-start.18 = (bf16[8,1328,128]{2,1,0:T(8,128)(2,1)}, bf16[8,1328,128]{2,1,0:T(8,128)(2,1)S(1)}, u32[]{:S(2)}, u32[]{:S(2)}) collective-permute-start(bf16[8,1328,128]{2,1,0:T(8,128)(2,1)} %get-tuple-element.36), channel_id=1, source_target_pairs={{0,4},{2,6},{4,0},{6,2},{8,12},{10,14},{12,8},{14,10},{16,20},{18,... | collective-permute-start | bytes 8159240 | tf_op jit(solution)/shard_map/ppermute | solution.py:21
  332.9 116.4 %collective-permute-start = (bf16[320,2560]{1,0:T(8,128)(2,1)}, bf16[320,2560]{1,0:T(8,128)(2,1)}, u32[]{:S(2)}, u32[]{:S(2)}) collective-permute-start(bf16[320,2560]{1,0:T(8,128)(2,1)} %bitcast), channel_id=1, source_target_pairs={{0,8},{2,10},{4,12},{6,14},{8,16},{10,18},{12,20},{14,22},{16,24},... | collective-permute-start | bytes 4915208 | tf_op jit(solution)/shard_map/ppermute | solution.py:28
  381.1 64.4 %collective-permute-start.9 = (bf16[4,1328,128]{2,1,0:T(8,128)(2,1)}, bf16[4,1328,128]{2,1,0:T(8,128)(2,1)}, u32[]{:S(2)}, u32[]{:S(2)}) collective-permute-start(bf16[4,1328,128]{2,1,0:T(8,128)(2,1)} %get-tuple-element.29), channel_id=1, source_target_pairs={{0,4},{2,6},{4,0},{6,2},{8,12},{10,14},{12,8},{14,10},{16,20},{18,... | collective-permute-start | bytes 4079624 | tf_op jit(solution)/shard_map/ppermute | solution.py:21
  395.1 77.3 %collective-permute-start.19 = (bf16[4,1328,128]{2,1,0:T(8,128)(2,1)}, bf16[4,1328,128]{2,1,0:T(8,128)(2,1)S(1)}, u32[]{:S(2)}, u32[]{:S(2)}) collective-permute-start(bf16[4,1328,128]{2,1,0:T(8,128)(2,1)} %get-tuple-element.38), channel_id=1, source_target_pairs={{0,2},{2,0},{4,6},{6,4},{8,10},{10,8},{12,14},{14,12},{16,18},{18,... | collective-permute-start | bytes 4079624 | tf_op jit(solution)/shard_map/ppermute | solution.py:21
  395.1 183.7 %collective-permute-start.1 = (bf16[320,2560]{1,0:T(8,128)(2,1)}, bf16[320,2560]{1,0:T(8,128)(2,1)}, u32[]{:S(2)}, u32[]{:S(2)}) collective-permute-start(bf16[320,2560]{1,0:T(8,128)(2,1)} %bitcast), channel_id=1, source_target_pairs={{0,16},{2,18},{4,20},{6,22},{8,24},{10,26},{12,28},{14,30},{16,0},... | collective-permute-start | bytes 4915208 | tf_op jit(solution)/shard_map/ppermute | solution.py:28
  415.6 165.9 %collective-permute-start.2 = (bf16[320,2560]{1,0:T(8,128)(2,1)}, bf16[320,2560]{1,0:T(8,128)(2,1)}, u32[]{:S(2)}, u32[]{:S(2)}) collective-permute-start(bf16[320,2560]{1,0:T(8,128)(2,1)} %bitcast), channel_id=1, source_target_pairs={{0,24},{2,26},{4,28},{6,30},{8,0},{10,2},{12,4},{14,6},{16,8},{18,... | collective-permute-start | bytes 4915208 | tf_op jit(solution)/shard_map/ppermute | solution.py:28
  449.3 45.3 %collective-permute-start.10 = (bf16[1328,128]{1,0:T(8,128)(2,1)}, bf16[1328,128]{1,0:T(8,128)(2,1)}, u32[]{:S(2)}, u32[]{:S(2)}) collective-permute-start(bf16[1328,128]{1,0:T(8,128)(2,1)} %get-tuple-element.31), channel_id=1, source_target_pairs={{0,24},{2,26},{4,28},{6,30},{8,0},{10,2},{12,4},{14,6},{16,8},{18,... | collective-permute-start | bytes 1019912 | tf_op jit(solution)/shard_map/ppermute | solution.py:28
  449.3 102.8 %collective-permute-start.11 = (bf16[1328,128]{1,0:T(8,128)(2,1)}, bf16[1328,128]{1,0:T(8,128)(2,1)}, u32[]{:S(2)}, u32[]{:S(2)}) collective-permute-start(bf16[1328,128]{1,0:T(8,128)(2,1)} %get-tuple-element.32), channel_id=1, source_target_pairs={{0,16},{2,18},{4,20},{6,22},{8,24},{10,26},{12,28},{14,30},{16,0},... | collective-permute-start | bytes 1019912 | tf_op jit(solution)/shard_map/ppermute | solution.py:28
  472.4 79.7 %collective-permute-start.12 = (bf16[1328,128]{1,0:T(8,128)(2,1)}, bf16[1328,128]{1,0:T(8,128)(2,1)}, u32[]{:S(2)}, u32[]{:S(2)}) collective-permute-start(bf16[1328,128]{1,0:T(8,128)(2,1)} %get-tuple-element.33), channel_id=1, source_target_pairs={{0,8},{2,10},{4,12},{6,14},{8,16},{10,18},{12,20},{14,22},{16,24},... | collective-permute-start | bytes 1019912 | tf_op jit(solution)/shard_map/ppermute | solution.py:28
  494.6 72.6 %collective-permute-start.20 = (bf16[1328,128]{1,0:T(8,128)(2,1)S(1)}, bf16[1328,128]{1,0:T(8,128)(2,1)S(1)}, u32[]{:S(2)}, u32[]{:S(2)}) collective-permute-start(bf16[1328,128]{1,0:T(8,128)(2,1)S(1)} %get-tuple-element.40), channel_id=1, source_target_pairs={{0,24},{2,26},{4,28},{6,30},{8,0},{10,2},{12,4},{14,6},{16,8},{18,... | collective-permute-start | bytes 1019912 | tf_op jit(solution)/shard_map/ppermute | solution.py:28
  552.1 22.7 %collective-permute-start.21 = (bf16[1328,128]{1,0:T(8,128)(2,1)S(1)}, bf16[1328,128]{1,0:T(8,128)(2,1)S(1)}, u32[]{:S(2)}, u32[]{:S(2)}) collective-permute-start(bf16[1328,128]{1,0:T(8,128)(2,1)S(1)} %get-tuple-element.41), channel_id=1, source_target_pairs={{0,16},{2,18},{4,20},{6,22},{8,24},{10,26},{12,28},{14,30},{16,0},... | collective-permute-start | bytes 1019912 | tf_op jit(solution)/shard_map/ppermute | solution.py:28
  552.1 22.7 %collective-permute-start.22 = (bf16[1328,128]{1,0:T(8,128)(2,1)S(1)}, bf16[1328,128]{1,0:T(8,128)(2,1)S(1)}, u32[]{:S(2)}, u32[]{:S(2)}) collective-permute-start(bf16[1328,128]{1,0:T(8,128)(2,1)S(1)} %get-tuple-element.42), channel_id=1, source_target_pairs={{0,8},{2,10},{4,12},{6,14},{8,16},{10,18},{12,20},{14,22},{16,24},... | collective-permute-start | bytes 1019912 | tf_op jit(solution)/shard_map/ppermute | solution.py:28
  577.0 23.6 %collective-permute-start.24 = (bf16[2560,128]{1,0:T(8,128)(2,1)S(1)}, bf16[2560,128]{1,0:T(8,128)(2,1)S(1)}, u32[]{:S(2)}, u32[]{:S(2)}) collective-permute-start(bf16[2560,128]{1,0:T(8,128)(2,1)S(1)} %pad_maximum_fusion.3), channel_id=1, source_target_pairs={{0,4},{2,6},{4,0},{6,2},{8,12},{10,14},{12,8},{14,10},{16,20},{18,... | collective-permute-start | bytes 1966088 | tf_op jit(solution)/shard_map/ppermute | solution.py:21
  578.5 23.4 %collective-permute-start.25 = (bf16[2560,128]{1,0:T(8,128)(2,1)S(1)}, bf16[2560,128]{1,0:T(8,128)(2,1)S(1)}, u32[]{:S(2)}, u32[]{:S(2)}) collective-permute-start(bf16[2560,128]{1,0:T(8,128)(2,1)S(1)} %pad_maximum_fusion.3), channel_id=1, source_target_pairs={{0,6},{2,4},{4,2},{6,0},{8,14},{10,12},{12,10},{14,8},{16,22},{18,... | collective-permute-start | bytes 1966088 | tf_op jit(solution)/shard_map/ppermute | solution.py:21
  (19 other events, 992.0 us)
Sparse Core Ops, SparseCore 0:
  610.0 17.6 reduce-scatter.1

commit v2 on v1

v2 whole, which is shorter than its diff:
```python
import functools
import math

import jax
import jax.numpy as jnp
from jax import lax
from jax.experimental import pallas as pl
from jax.experimental.pallas import tpu as pltpu
from jax.sharding import PartitionSpec as P

HEAD_DIM = 128
EPSILON = 1e-06
LOW_SCORE = -1e30
PLANE = 4
PIECE = 16
LEVEL_ROWS = 32
SCORE_SCALE = math.log2(math.e) / math.sqrt(HEAD_DIM)


def send_xor(value, by):
    size = lax.axis_size("req")
    return lax.ppermute(value, "req", [(i, i ^ by) for i in range(size)])


def send_line(value, by):
    size = lax.axis_size("req")
    line = size // PLANE
    pairs = [(i, ((i // PLANE + by) % line) * PLANE + i % PLANE) for i in range(size)]
    return lax.ppermute(value, "req", pairs)


def group_count(width):
    return 4 if width // HEAD_DIM % 4 == 0 else 1


def send_tp(value, by):
    size = lax.axis_size("tp")
    return lax.ppermute(value, "tp", [(i, (i + by) % size) for i in range(size)])


def place_kernel(spots_ref, *refs):
    *blocks, out, sems = refs
    copies = [
        pltpu.make_async_copy(ref, out.at[spots_ref[i]], sems.at[i]) for i, ref in enumerate(blocks)
    ]
    for copy in copies:
        copy.start()
    for copy in copies:
        copy.wait()


def place_blocks(spots, blocks):
    return pl.pallas_call(
        place_kernel,
        grid_spec=pltpu.PrefetchScalarGridSpec(
            num_scalar_prefetch=1,
            grid=(1,),
            in_specs=[pl.BlockSpec(memory_space=pl.ANY)] * len(blocks),
            out_specs=pl.BlockSpec(memory_space=pl.ANY),
            scratch_shapes=[pltpu.SemaphoreType.DMA((len(blocks),))],
        ),
        out_shape=jax.ShapeDtypeStruct((len(blocks),) + blocks[0].shape, blocks[0].dtype),
        name="place_weights",
    )(spots, *blocks)


def turn_kernel(q_ref, k_ref, scale_ref, gain_q_ref, gain_k_ref, cos_ref, sin_ref, _, q_out, k_out):
    cosine = cos_ref[...]
    sine = sin_ref[...]
    sides = ((q_ref, gain_q_ref, q_out), (k_ref, gain_k_ref, k_out))
    for side, (ref, gain, out) in enumerate(sides):
        scale = scale_ref[:, side : side + 1]
        for col in range(0, ref.shape[1], HEAD_DIM):
            cols = slice(col, col + HEAD_DIM)
            x = ref[:, cols].astype(jnp.float32) * scale * gain[:, cols]
            y = x * cosine + pltpu.roll(x, HEAD_DIM // 2, 1) * sine
            out[:, cols] = y.astype(jnp.bfloat16)


def turn(group, queries, new_keys, scales, gain_q, gain_k, cosine, sine, after):
    rows, width = queries.shape
    width = width // group_count(width)
    part = jax.ShapeDtypeStruct((rows, width), jnp.bfloat16)
    part_spec = pl.BlockSpec((rows, width), lambda i: (0, group))
    gain_spec = pl.BlockSpec((1, width), lambda i: (0, group))
    whole = lambda shape: pl.BlockSpec(shape, lambda i: (0, 0))
    return pl.pallas_call(
        turn_kernel,
        grid=(1,),
        in_specs=[
            part_spec,
            part_spec,
            whole(scales.shape),
            gain_spec,
            gain_spec,
            whole(cosine.shape),
            whole(sine.shape),
            pl.BlockSpec(memory_space=pl.ANY),
        ],
        out_specs=[whole(part.shape), whole(part.shape)],
        out_shape=[part, part],
        compiler_params=pltpu.CompilerParams(vmem_limit_bytes=16 * 2**20),
        name="norm_turn",
    )(queries, new_keys, scales, gain_q[None], gain_k[None], cosine, sine, after)


def attend_kernel(
    table_ref,
    slot_ref,
    q_low_ref,
    q_high_ref,
    keys_ref,
    values_ref,
    near_keys_ref,
    near_values_ref,
    near_starts_ref,
    keep_ref,
    send_ref,
    q_all,
    acc,
    peak,
    total,
    sems,
):
    step = pl.program_id(0)
    half, rows, width = q_low_ref.shape
    blocks = 2 * half
    heads = width // HEAD_DIM
    lane = lax.broadcasted_iota(jnp.int32, (1, rows), 1)

    def update(slots, keys_ref, values_ref, masks, allowed):
        ones = jnp.ones((PIECE, keys_ref.shape[0]), jnp.bfloat16)
        mask = jnp.concatenate(masks, axis=1)
        old_peak = jnp.concatenate([peak[s] for s in slots], axis=1)
        old_total = jnp.concatenate([total[s] for s in slots], axis=1)
        scores, weights, tops, fades = {}, {}, {}, {}

        def score(h):
            cols = slice(h * HEAD_DIM, (h + 1) * HEAD_DIM)
            q = jnp.concatenate([q_all[s, :, cols] for s in slots], axis=0)
            scores[h] = lax.dot_general(
                keys_ref[:, cols], q, (((1,), (1,)), ((), ())), preferred_element_type=jnp.float32
            )

        def weigh(h):
            found = scores.pop(h)
            if allowed is not None:
                found = jnp.where(allowed, found, LOW_SCORE)
            before = old_peak[h : h + 1]
            top = jnp.maximum(jnp.max(found, axis=0, keepdims=True), before)
            tops[h] = jnp.where(mask, top, before)
            fades[h] = jnp.where(mask, jnp.exp2(before - top), 1.0)
            weights[h] = jnp.exp2(found - jnp.where(mask, top, -LOW_SCORE)).astype(jnp.bfloat16)

        def blend(h):
            cols = slice(h * HEAD_DIM, (h + 1) * HEAD_DIM)
            values = jnp.concatenate([values_ref[:, cols].T, ones], axis=0)
            blended = jnp.dot(values, weights.pop(h), preferred_element_type=jnp.float32)
            fade = fades.pop(h)
            held = [acc[s, cols, :] for s in slots]
            sums = old_total[h : h + 1] * fade + blended[HEAD_DIM : HEAD_DIM + 1]
            for i, s in enumerate(slots):
                span = slice(i * rows, (i + 1) * rows)
                acc[s, cols, :] = held[i] * fade[:, span] + blended[:HEAD_DIM, span]
                peak[s, h : h + 1, :] = tops[h][:, span]
                total[s, h : h + 1, :] = sums[:, span]

        for h in range(heads + 2):
            if h < heads:
                score(h)
            if 1 <= h <= heads:
                weigh(h - 1)
            if h >= 2:
                blend(h - 2)

    @pl.when(step == 0)
    def _():
        low = pltpu.make_async_copy(q_low_ref, q_all.at[pl.ds(0, half)], sems.at[0])
        high = pltpu.make_async_copy(q_high_ref, q_all.at[pl.ds(half, half)], sems.at[1])
        low.start()
        high.start()
        q_all[blocks] = jnp.zeros((rows, width), jnp.bfloat16)
        acc[...] = jnp.zeros_like(acc)
        peak[...] = jnp.full(peak.shape, LOW_SCORE, jnp.float32)
        total[...] = jnp.zeros_like(total)
        low.wait()
        high.wait()
        first = slot_ref[blocks + 1]

        def near_pair(j, carry):
            low = first + 2 * j
            row = low * rows + jnp.concatenate([lane, lane + rows], axis=1)
            begin = near_starts_ref[j]
            key = first * rows + lax.broadcasted_iota(jnp.int32, (rows, 2 * rows), 0)
            allowed = (key >= begin) & (key <= row)
            some = begin < (first + 1) * rows
            slots = [slot_ref[jnp.minimum(low + i, blocks)] for i in range(2)]
            masks = [some[:, :rows], some[:, rows:]]
            update(slots, near_keys_ref, near_values_ref, masks, allowed)
            return carry

        lax.fori_loop(0, 2, near_pair, 0)

    @pl.when(step > 0)
    def _():
        begin = table_ref[4 * step - 4]
        end = table_ref[4 * step - 3]
        first = table_ref[4 * step - 2]
        count = table_ref[4 * step - 1]

        def pair(j, carry):
            low = first + 2 * j
            row = low * rows + lane
            masks = [(r >= begin) & (r < end) for r in (row, row + rows)]
            slots = [slot_ref[low], slot_ref[low + 1]]
            update(slots, keys_ref.at[0], values_ref.at[0], masks, None)
            return carry

        lax.fori_loop(0, count, pair, 0)

    @pl.when(step == pl.num_programs(0) - 1)
    def _():
        for at, out in ((0, keep_ref), (half, send_ref)):

            def finish(i, carry, at=at, out=out):
                sums = jnp.maximum(total[at + i], 1.0)
                write_block(
                    out.at[i],
                    lambda h: acc[at + i, h * HEAD_DIM : (h + 1) * HEAD_DIM, :],
                    1.0 / sums,
                    peak[at + i] + jnp.log2(sums),
                    heads,
                )
                return carry

            lax.fori_loop(0, half, finish, 0)


def write_block(out, block, factors, levels, heads):
    for h in range(heads):
        out[h * HEAD_DIM : (h + 1) * HEAD_DIM, :] = (block(h) * factors[h : h + 1]).astype(jnp.bfloat16)
    first = levels.astype(jnp.bfloat16).astype(jnp.float32)
    second = (levels - first).astype(jnp.bfloat16).astype(jnp.float32)
    third = levels - first - second
    stacked = jnp.concatenate([first, second, third, jnp.zeros_like(levels)], axis=0)
    out[heads * HEAD_DIM :, :] = stacked.astype(jnp.bfloat16)


def read_levels(ref, heads):
    stacked = ref[heads * HEAD_DIM :, :].astype(jnp.float32)
    return stacked[:8] + (stacked[8:16] + stacked[16:24])


def attend(group, table, slots, q_low, q_high, cache_keys, cache_values, near_keys, near_values, near_starts):
    half, rows, width = q_low.shape
    pages, page_len, _ = cache_keys.shape
    heads = width // HEAD_DIM
    blocks = 2 * half
    assert heads <= 8
    out = jax.ShapeDtypeStruct((half, width + LEVEL_ROWS, rows), jnp.bfloat16)
    page_spec = pl.BlockSpec((1, page_len, width), lambda i, *_: (jnp.maximum(i - 1, 0), 0, group))
    near_spec = pl.BlockSpec((rows, width), lambda i, *_: (0, group))
    own_spec = pl.BlockSpec((rows, width), lambda i, *_: (0, 0))
    whole = lambda shape: pl.BlockSpec(shape, lambda i, *_: (0,) * len(shape))
    return pl.pallas_call(
        attend_kernel,
        grid_spec=pltpu.PrefetchScalarGridSpec(
            num_scalar_prefetch=2,
            grid=(pages + 1,),
            in_specs=[
                pl.BlockSpec(memory_space=pl.ANY),
                pl.BlockSpec(memory_space=pl.ANY),
                page_spec,
                page_spec,
                own_spec,
                near_spec,
                whole((2, 1, 2 * rows)),
            ],
            out_specs=[whole(out.shape), whole(out.shape)],
            scratch_shapes=[
                pltpu.VMEM((blocks + 1, rows, width), jnp.bfloat16),
                pltpu.VMEM((blocks + 1, width, rows), jnp.float32),
                pltpu.VMEM((blocks + 1, 8, rows), jnp.float32),
                pltpu.VMEM((blocks + 1, 8, rows), jnp.float32),
                pltpu.SemaphoreType.DMA((2,)),
            ],
        ),
        out_shape=[out, out],
        compiler_params=pltpu.CompilerParams(
            dimension_semantics=("arbitrary",), vmem_limit_bytes=56 * 2**20
        ),
        cost_estimate=pl.CostEstimate(
            flops=pages * heads * 256 * page_len * HEAD_DIM * 8,
            bytes_accessed=pages * page_len * width * 4,
            transcendentals=pages * heads * 256 * page_len,
        ),
        name="cache_attend",
    )(table, slots, q_low, q_high, cache_keys, cache_values, near_keys, near_values, near_starts)


def merged(refs, heads):
    levels = [read_levels(ref, heads) for ref in refs]
    top = functools.reduce(jnp.maximum, levels)
    weights = [jnp.exp2(level - top) for level in levels]
    total = functools.reduce(jnp.add, weights)
    factors = [w / total for w in weights]

    def block(h):
        cols = slice(h * HEAD_DIM, (h + 1) * HEAD_DIM)
        return functools.reduce(
            jnp.add, [ref[cols, :].astype(jnp.float32) * f[h : h + 1] for ref, f in zip(refs, factors)]
        )

    return block, top + jnp.log2(total)


def combine_kernel(mine_low, mine_high, got_low, got_high, keep_ref, send_ref):
    heads = (mine_low.shape[1] - LEVEL_ROWS) // HEAD_DIM
    for mine, got, out in ((mine_low, got_low, keep_ref), (mine_high, got_high, send_ref)):
        block, levels = merged([mine.at[0], got.at[0]], heads)
        write_block(out.at[0], block, jnp.ones_like(levels), levels, heads)


def combine(mine, got):
    count, depth, rows = mine.shape
    half = count // 2
    low = pl.BlockSpec((1, depth, rows), lambda i: (i, 0, 0))
    high = pl.BlockSpec((1, depth, rows), lambda i: (i + half, 0, 0))
    out = jax.ShapeDtypeStruct((half, depth, rows), jnp.bfloat16)
    return pl.pallas_call(
        combine_kernel,
        grid=(half,),
        in_specs=[low, high, low, high],
        out_specs=[low, low],
        out_shape=[out, out],
        compiler_params=pltpu.CompilerParams(vmem_limit_bytes=24 * 2**20),
        cost_estimate=pl.CostEstimate(
            flops=count * depth * rows * 4, bytes_accessed=count * depth * rows * 6, transcendentals=0
        ),
        name="combine_pairs",
    )(mine, mine, got, got)


def last_kernel(*refs):
    out_ref = refs[-1]
    heads = out_ref.shape[0] // HEAD_DIM
    block, _ = merged(refs[:-1], heads)
    for h in range(heads):
        out_ref[h * HEAD_DIM : (h + 1) * HEAD_DIM, :] = block(h).astype(jnp.bfloat16)


def combine_last(parts):
    depth, rows = parts[0].shape
    return pl.pallas_call(
        last_kernel,
        out_shape=jax.ShapeDtypeStruct((depth - LEVEL_ROWS, rows), jnp.bfloat16),
        compiler_params=pltpu.CompilerParams(vmem_limit_bytes=24 * 2**20),
        cost_estimate=pl.CostEstimate(
            flops=len(parts) * depth * rows * 2,
            bytes_accessed=(len(parts) + 1) * depth * rows * 2,
            transcendentals=0,
        ),
        name="combine_last",
    )(*parts)


def local(
    hidden_in,
    queries,
    new_keys,
    new_values,
    query_gain,
    key_gain,
    cache_keys,
    cache_values,
    seg_ids,
    cache_pages,
    page_table,
    out_weight,
    out_bias,
    gate_mod,
):
    tok_dev, local_width = queries.shape
    size = lax.axis_size("req")
    tp_size = lax.axis_size("tp")
    model_width = local_width * tp_size
    line = size // PLANE
    device = lax.axis_index("req")
    spot = device % PLANE
    place = device // PLANE
    slot_count, page_len, _ = cache_keys.shape
    request_count = cache_pages.shape[0]
    total_pages = page_table.shape[0]
    first_row = device * tok_dev
    own_rows = first_row + jnp.arange(tok_dev, dtype=jnp.int32)
    own_segs = lax.dynamic_slice_in_dim(seg_ids, first_row, tok_dev, 0)
    req_ids = jnp.arange(request_count, dtype=jnp.int32)
    starts = jnp.sum((seg_ids[None, :] < req_ids[:, None]).astype(jnp.int32), axis=1)
    ends = jnp.sum((seg_ids[None, :] <= req_ids[:, None]).astype(jnp.int32), axis=1)
    own_pick = own_segs[:, None] == req_ids[None, :]
    own_start = jnp.sum(jnp.where(own_pick, starts[None, :], 0), axis=1)
    own_cache = jnp.sum(jnp.where(own_pick, cache_pages[None, :], 0), axis=1)
    positions = own_cache * page_len + own_rows - own_start

    wide_q = queries.astype(jnp.float32)
    wide_k = new_keys.astype(jnp.float32)
    sums = lax.psum(
        jnp.stack([jnp.sum(wide_q * wide_q, axis=1), jnp.sum(wide_k * wide_k, axis=1)], axis=1), "tp"
    )
    scales = lax.rsqrt(sums / model_width + EPSILON) * jnp.array([[SCORE_SCALE, 1.0]], jnp.float32)
    halfway = HEAD_DIM // 2
    frequency = 10000.0 ** (-jnp.arange(halfway, dtype=jnp.float32) / halfway)
    angles = positions.astype(jnp.float32)[:, None] * frequency[None, :]
    cosine = jnp.cos(angles)
    sine = jnp.sin(angles)
    cosine = jnp.concatenate([cosine, cosine], axis=1)
    sine = jnp.concatenate([-sine, sine], axis=1)

    physical = device * slot_count + jnp.arange(slot_count, dtype=jnp.int32)
    logical = jnp.sum(
        jnp.where(
            page_table[None, :] == physical[:, None],
            jnp.arange(total_pages, dtype=jnp.int32)[None, :],
            0,
        ),
        axis=1,
    )
    page_ends = jnp.cumsum(cache_pages)
    owners = jnp.sum((page_ends[None, :] <= logical[:, None]).astype(jnp.int32), axis=1)
    owner_pick = owners[:, None] == req_ids[None, :]
    owner_starts = jnp.sum(jnp.where(owner_pick, starts[None, :], 0), axis=1)
    owner_ends = jnp.sum(jnp.where(owner_pick, ends[None, :], 0), axis=1)
    owner_first = owner_starts // tok_dev
    owner_pairs = ((owner_ends - 1) // tok_dev - owner_first + 2) // 2
    table = jnp.stack([owner_starts, owner_ends, owner_first, owner_pairs], axis=1).reshape(-1)

    near_blocks = device + jnp.arange(4, dtype=jnp.int32)
    near_rows = (near_blocks[:, None] * tok_dev + jnp.arange(tok_dev, dtype=jnp.int32)[None, :]).reshape(-1)
    padded_segs = jnp.concatenate([seg_ids, jnp.full((3 * tok_dev,), -1, jnp.int32)])
    near_segs = lax.dynamic_slice_in_dim(padded_segs, first_row, 4 * tok_dev, 0)
    near_starts = jnp.sum(
        jnp.where(near_segs[:, None] == req_ids[None, :], starts[None, :], 0), axis=1
    )
    near_starts = jnp.where(near_segs < 0, near_rows + size * tok_dev, near_starts)
    near_starts = near_starts.reshape(2, 1, 2 * tok_dev)

    block = jnp.arange(size, dtype=jnp.int32)
    back = (place - block // PLANE) % line
    across = (block % PLANE) ^ spot

    def order_of(group):
        return (2, 1) if group % 2 == 0 else (1, 2)

    groups = group_count(local_width)
    near, near_keys = [], []
    after = scales
    for group in range(groups):
        part, key_part = turn(
            group, queries, new_keys, scales, query_gain, key_gain, cosine, sine, after
        )
        got = [part[None]] + [send_line(part, k)[None] for k in range(1, line)]
        near.append(jnp.concatenate(got, axis=0))
        near_keys.append(key_part)
        after = near[-1]

    weight, _ = lax.optimization_barrier((out_weight.T, after))
    columns = weight.shape[0]
    blocks_each = line // tp_size
    tp_device = lax.axis_index("tp")
    from_place = (place - jnp.arange(line, dtype=jnp.int32)) % line
    weight_spots = ((from_place // blocks_each - tp_device) % tp_size) * blocks_each
    weight_spots = weight_spots + from_place % blocks_each
    weights = place_blocks(weight_spots, [weight] + [send_line(weight, k) for k in range(1, line)])
    weights = weights.reshape(tp_size, blocks_each * columns, local_width)
    weights = [weights[0]] + [send_tp(weights[k], k) for k in range(1, tp_size)]

    attended = []
    for group in range(groups):
        order = order_of(group)
        low = jnp.concatenate([near[group], send_xor(near[group], order[0])], axis=0)
        high = send_xor(low, order[1])
        slot = jnp.where((across & order[1]) > 0, 2 * line, 0)
        slot = slot + jnp.where((across & order[0]) > 0, line, 0) + back
        slots = jnp.concatenate([slot, jnp.stack([jnp.int32(size), device])])
        keep, send = attend(
            group, table, slots, low, high, cache_keys, cache_values, near_keys[group], new_values, near_starts
        )
        keep, send = combine(keep, send_xor(send, order[1]))
        parts = combine_line(keep, send_xor(send, order[0]))
        attended.append(combine_last([parts[0]] + [send_line(parts[k], -k) for k in range(1, line)]))

    projected = 0.0
    depth = 0
    for some in ([attended[:-1], attended[-1:]] if groups > 1 else [attended]):
        some = jnp.concatenate(some, axis=0)
        spread = jnp.concatenate([some] + [send_xor(some, k) for k in range(1, PLANE)], axis=1)
        for k in range(tp_size):
            part = spread if k == 0 else send_tp(spread, k)
            projected = projected + jnp.dot(
                weights[k][:, depth : depth + some.shape[0]], part, preferred_element_type=jnp.float32
            )
        depth += some.shape[0]
    sent = projected.astype(jnp.bfloat16)
    mine = [projected[:, :tok_dev]] + [
        send_xor(sent[:, k * tok_dev : (k + 1) * tok_dev], k).astype(jnp.float32) for k in range(1, PLANE)
    ]
    mine = [part.reshape(blocks_each, columns, tok_dev) for part in mine]
    swapped = [jnp.where((spot & 1) > 0, mine[i ^ 1], mine[i]) for i in range(PLANE)]
    swapped = [jnp.where((spot & 2) > 0, swapped[i ^ 2], swapped[i]) for i in range(PLANE)]
    projected = jnp.stack(swapped, axis=1).reshape(local_width, tok_dev).T

    gate_rows = jnp.dot(own_pick.astype(jnp.float32), gate_mod, precision=lax.Precision.HIGHEST)
    return (hidden_in.astype(jnp.float32) + gate_rows * (projected + out_bias[None, :])).astype(
        jnp.bfloat16
    )


def pair_kernel(mine, got, *outs):
    heads = (mine.shape[1] - LEVEL_ROWS) // HEAD_DIM
    for i, out in enumerate(outs):
        block, levels = merged([mine.at[i], got.at[i]], heads)
        write_block(out, block, jnp.ones_like(levels), levels, heads)


def combine_line(mine, got):
    count, depth, rows = mine.shape
    out = jax.ShapeDtypeStruct((depth, rows), jnp.bfloat16)
    return pl.pallas_call(
        pair_kernel,
        out_shape=[out] * count,
        compiler_params=pltpu.CompilerParams(vmem_limit_bytes=32 * 2**20),
        cost_estimate=pl.CostEstimate(
            flops=count * depth * rows * 4, bytes_accessed=count * depth * rows * 6, transcendentals=0
        ),
        name="combine_line",
    )(mine, got)


def solution(mesh):
    return jax.shard_map(
        local,
        mesh=mesh,
        in_specs=(
            P("req", "tp"),
            P("req", "tp"),
            P("req", "tp"),
            P("req", "tp"),
            P("tp"),
            P("tp"),
            P("req", None, "tp"),
            P("req", None, "tp"),
            P(),
            P(),
            P(),
            P("tp", "req"),
            P("tp"),
            P(None, "tp"),
        ),
        out_specs=P("req", "tp"),
        check_vma=False,
    )
```

time: 655 us -> 611 us (0.933)
  Pallas kernels: 159 us -> 298 us
  starting transfers between devices: 198 us -> 70.2 us
  waiting for transfers between devices: 234 us -> 202 us
  local copies, waits for them, and re-layouts: 30.6 us -> 12.5 us
  between operations: 13.7 us -> 0.84 us
    pallas_call x3 -> x9, Pallas kernels: 2.69 us -> 202 us  [the longest x1 200 us: place_blocks(): pl.pallas_call(place_kernel, grid_spec=pltpu.PrefetchScalarGridSpec(num_s...]
    ppermute x15 -> x27, starting transfers between devices: 170 us -> 32.7 us  [send_line(): return lax.ppermute(value, 'req', pairs)]
    ppermute x14 -> x25, waiting for transfers between devices: 150 us -> 82.1 us  [send_xor(): return lax.ppermute(value, 'req', [(i, i ^ by) for i in range(size)])]
    pallas_call x2 -> x4, Pallas kernels: 149 us -> 89.3 us  [attend(): pl.pallas_call(attend_kernel, grid_spec=pltpu.PrefetchScalarGridSpec(num_...]
    ppermute x15 -> x27, waiting for transfers between devices: 66 us -> 119 us  [send_line(): return lax.ppermute(value, 'req', pairs)]
    reduce_scatter x1 -> x0, waiting for transfers between devices: 17.9 us -> none  [local(): lax.psum_scatter(partial_proj, 'tp', scatter_dimension=0, tiled=True)]
    dynamic_update_slice x4 -> x0, local copies, waits for them, and re-layouts: 10.9 us -> none  [local(): lax.dynamic_update_slice_in_dim(gathered, got, (place - k) % line * colum...]
    ppermute x14 -> x25, starting transfers between devices: 27.8 us -> 37.3 us  [send_xor(): return lax.ppermute(value, 'req', [(i, i ^ by) for i in range(size)])]
  transfers between devices with their start and end apart: 30 -> 55, of which waited for: 15 -> 27; matrix products, arithmetic and copies ran while one was open for 4% -> 3% of each run, Pallas kernels for 24% -> 49%
where the time goes in v2:
time: 611 us; the launch traced here: 608 us
  Pallas kernels  298 us (49%)
  waiting for transfers between devices  202 us (33%)
  starting transfers between devices  70.2 us (11%)
  other arithmetic  14.4 us (2%)
  local copies, waits for them, and re-layouts  12.5 us (2%)
  matrix products  6.11 us (1%)
    pallas_call x1, Pallas kernels, place_blocks(): pl.pallas_call(place_kernel, grid_spec=pltpu.PrefetchScalarGridSpec(num_s...  200 us
    ppermute x27, waiting for transfers between devices, send_line(): return lax.ppermute(value, 'req', pairs)  119 us
    pallas_call x4, Pallas kernels, attend(): pl.pallas_call(attend_kernel, grid_spec=pltpu.PrefetchScalarGridSpec(num_...  89.3 us
    ppermute x25, waiting for transfers between devices, send_xor(): return lax.ppermute(value, 'req', [(i, i ^ by) for i in range(size)])  82.1 us
    ppermute x25, starting transfers between devices, send_xor(): return lax.ppermute(value, 'req', [(i, i ^ by) for i in range(size)])  37.3 us
    ppermute x27, starting transfers between devices, send_line(): return lax.ppermute(value, 'req', pairs)  32.7 us
  transfers between devices with their start and end apart: 55, of which 27 were waited for; matrix products, arithmetic and copies ran while one was open for 3% of the time, Pallas kernels for 49%

profile of v2, /device:TPU:0, one launch (start us, length us, event | category | flops | bytes accessed | tf_op | source)
XLA Modules:
  0.0 607.9 jit_solution(2818568411075675671)
XLA Ops:
  4.6 3.9 psum.7
  10.1 4.8 collective-permute-start.2
  21.0 8.3 %collective-permute-done.1 = bf16[128,640]{1,0:T(8,128)(2,1)S(1)} collective-permute-done((bf16[128,640]{1,0:T(8,128)(2,1)S(1)}, bf16[128,640]{1,0:T(8,128)(2,1)S(1)}, u32[]{:S(2)}, u32[]{:S(2)}) %collective-permute-start.1) | collective-permute-done | bytes 163872 | tf_op jit(solution)/shard_map/ppermute | solution.py:29
  38.2 9.6 %collective-permute-done.4 = bf16[128,640]{1,0:T(8,128)(2,1)S(1)} collective-permute-done((bf16[128,640]{1,0:T(8,128)(2,1)S(1)}, bf16[128,640]{1,0:T(8,128)(2,1)S(1)}, u32[]{:S(2)}, u32[]{:S(2)}) %collective-permute-start.4) | collective-permute-done | bytes 163872 | tf_op jit(solution)/shard_map/ppermute | solution.py:29
  54.3 9.6 %collective-permute-done.7 = bf16[128,640]{1,0:T(8,128)(2,1)S(1)} collective-permute-done((bf16[128,640]{1,0:T(8,128)(2,1)S(1)}, bf16[128,640]{1,0:T(8,128)(2,1)S(1)}, u32[]{:S(2)}, u32[]{:S(2)}) %collective-permute-start.7) | collective-permute-done | bytes 163872 | tf_op jit(solution)/shard_map/ppermute | solution.py:29
  72.3 8.1 %collective-permute-done.10 = bf16[128,640]{1,0:T(8,128)(2,1)S(1)} collective-permute-done((bf16[128,640]{1,0:T(8,128)(2,1)S(1)}, bf16[128,640]{1,0:T(8,128)(2,1)S(1)}, u32[]{:S(2)}, u32[]{:S(2)}) %collective-permute-start.10) | collective-permute-done | bytes 163872 | tf_op jit(solution)/shard_map/ppermute | solution.py:29
  88.4 11.7 %collective-permute-done.16.q_high_ref = bf16[8,128,640]{2,1,0:T(8,128)(2,1)S(1)} collective-permute-done((bf16[8,128,640]{2,1,0:T(8,128)(2,1)S(1)}, bf16[8,128,640]{2,1,0:T(8,128)(2,1)S(1)}, u32[]{:S(2)}, u32[]{:S(2)}) %collective-permute-start.16) | collective-permute-done | bytes 1310752 | tf_op jit(solution)/shard_map/ppermute | solution.py:22
  101.2 22.2 %cache_attend.4 = (bf16[8,672,128]{2,1,0:T(8,128)(2,1)}, bf16[8,672,128]{2,1,0:T(8,128)(2,1)}) custom-call(s32[64]{0:T(128)} %reshape.372.table_ref, s32[18]{0:T(128)} %fusion.26.slot_ref, bf16[8,128,640]{2,1,0:T(8,128)(2,1)} %copy-done.14, bf16[8,128,640]{2,1,0:T(8,128)(2,1)} %copy-done.18, bf16[16,256,2560]{2,1,0:T(8,128)(2,1)} %keys_ref.7, ...), custom_call_target="tpu_custom_call" | custom-call | flops 5368709120 | bytes 10485760 | tf_op jit(solution)/shard_map/cache_attend/pallas_call | solution.py:265
  133.1 22.3 %cache_attend.5 = (bf16[8,672,128]{2,1,0:T(8,128)(2,1)}, bf16[8,672,128]{2,1,0:T(8,128)(2,1)}) custom-call(s32[64]{0:T(128)} %reshape.372.table_ref, s32[18]{0:T(128)} %fusion.27.slot_ref, bf16[8,128,640]{2,1,0:T(8,128)(2,1)} %copy-done.16, bf16[8,128,640]{2,1,0:T(8,128)(2,1)} %collective-permute-done.23.q_high_ref, bf16[16,256,2560]{2,1,0:T(8,128)(2,1)} %keys_ref.7, ...), custom_call_target="tpu_custom_call" | custom-call | flops 5368709120 | bytes 10485760 | tf_op jit(solution)/shard_map/cache_attend/pallas_call | solution.py:265
  159.2 22.4 %cache_attend.6 = (bf16[8,672,128]{2,1,0:T(8,128)(2,1)}, bf16[8,672,128]{2,1,0:T(8,128)(2,1)}) custom-call(s32[64]{0:T(128)} %reshape.372.table_ref, s32[18]{0:T(128)} %fusion.26.slot_ref, bf16[8,128,640]{2,1,0:T(8,128)(2,1)} %copy-done.15, bf16[8,128,640]{2,1,0:T(8,128)(2,1)} %collective-permute-done.30.q_high_ref, bf16[16,256,2560]{2,1,0:T(8,128)(2,1)} %keys_ref.7, ...), custom_call_target="tpu_custom_call" | custom-call | flops 5368709120 | bytes 10485760 | tf_op jit(solution)/shard_map/cache_attend/pallas_call | solution.py:265
  187.2 45.3 %collective-permute-done.13.refs_2_ = bf16[320,2560]{1,0:T(8,128)(2,1)} collective-permute-done((bf16[320,2560]{1,0:T(8,128)(2,1)}, bf16[320,2560]{1,0:T(8,128)(2,1)}, u32[]{:S(2)}, u32[]{:S(2)}) %collective-permute-start.13) | collective-permute-done | bytes 1638432 | tf_op jit(solution)/shard_map/ppermute | solution.py:29
  235.1 200.3 %place_weights.1 = bf16[4,320,2560]{2,1,0:T(8,128)(2,1)} custom-call(s32[4]{0:T(128)} %fusion.25.spots_ref, bf16[320,2560]{1,0:T(8,128)(2,1)} %bitcast.refs_0_, bf16[320,2560]{1,0:T(8,128)(2,1)} %collective-permute-done.12.refs_1_, bf16[320,2560]{1,0:T(8,128)(2,1)} %collective-permute-done.13.refs_2_, bf16[320,2560]{1,0:T(8,128)(2,1)} %copy-done.17), custom_call_target="tpu_custom_call" | custom-call | tf_op jit(solution)/shard_map/place_weights/pallas_call | solution.py:53
  435.5 22.5 %cache_attend.7 = (bf16[8,672,128]{2,1,0:T(8,128)(2,1)}, bf16[8,672,128]{2,1,0:T(8,128)(2,1)}) custom-call(s32[64]{0:T(128)} %reshape.372.table_ref, s32[18]{0:T(128)} %fusion.27.slot_ref, bf16[8,128,640]{2,1,0:T(8,128)(2,1)} %constant_dynamic-update-slice_fusion.15.q_low_ref, bf16[8,128,640]{2,1,0:T(8,128)(2,1)} %collective-permute-done.42.q_high_ref, ...), custom_call_target="tpu_custom_call" | custom-call | flops 5368709120 | bytes 10485760 | tf_op jit(solution)/shard_map/cache_attend/pallas_call | solution.py:265
  465.2 12.2 %collective-permute-done.25.got = bf16[4,672,128]{2,1,0:T(8,128)(2,1)S(1)} collective-permute-done((bf16[4,672,128]{2,1,0:T(8,128)(2,1)S(1)}, bf16[4,672,128]{2,1,0:T(8,128)(2,1)S(1)}, u32[]{:S(2)}, u32[]{:S(2)}) %collective-permute-start.25) | collective-permute-done | bytes 688160 | tf_op jit(solution)/shard_map/ppermute | solution.py:22
  478.1 10.7 %collective-permute-done.20.refs_2_ = bf16[672,128]{1,0:T(8,128)(2,1)S(1)} collective-permute-done((bf16[672,128]{1,0:T(8,128)(2,1)S(1)}, bf16[672,128]{1,0:T(8,128)(2,1)S(1)}, u32[]{:S(2)}, u32[]{:S(2)}) %collective-permute-start.20) | collective-permute-done | bytes 172064 | tf_op jit(solution)/shard_map/ppermute | solution.py:29
  488.9 15.9 %collective-permute-done.32.got = bf16[4,672,128]{2,1,0:T(8,128)(2,1)S(1)} collective-permute-done((bf16[4,672,128]{2,1,0:T(8,128)(2,1)S(1)}, bf16[4,672,128]{2,1,0:T(8,128)(2,1)S(1)}, u32[]{:S(2)}, u32[]{:S(2)}) %collective-permute-start.32) | collective-permute-done | bytes 688160 | tf_op jit(solution)/shard_map/ppermute | solution.py:22
  505.2 3.9 collective-permute-start.33
  509.0 4.9 collective-permute-done.28.refs_3_
  514.0 5.1 collective-permute-start.35
  519.4 7.1 %collective-permute-done.34.refs_2_ = bf16[672,128]{1,0:T(8,128)(2,1)S(1)} collective-permute-done((bf16[672,128]{1,0:T(8,128)(2,1)S(1)}, bf16[672,128]{1,0:T(8,128)(2,1)S(1)}, u32[]{:S(2)}, u32[]{:S(2)}) %collective-permute-start.34) | collective-permute-done | bytes 172064 | tf_op jit(solution)/shard_map/ppermute | solution.py:29
  531.6 10.2 %collective-permute-done.38 = bf16[1920,128]{1,0:T(8,128)(2,1)S(1)} collective-permute-done((bf16[1920,128]{1,0:T(8,128)(2,1)S(1)}, bf16[1920,128]{1,0:T(8,128)(2,1)S(1)}, u32[]{:S(2)}, u32[]{:S(2)}) %collective-permute-start.38) | collective-permute-done | bytes 491552 | tf_op jit(solution)/shard_map/ppermute | solution.py:22
  541.8 8.6 %collective-permute-done.37 = bf16[1920,128]{1,0:T(8,128)(2,1)S(1)} collective-permute-done((bf16[1920,128]{1,0:T(8,128)(2,1)S(1)}, bf16[1920,128]{1,0:T(8,128)(2,1)S(1)}, u32[]{:S(2)}, u32[]{:S(2)}) %collective-permute-start.37) | collective-permute-done | bytes 491552 | tf_op jit(solution)/shard_map/ppermute | solution.py:22
  554.5 9.5 %collective-permute-done.44.got = bf16[4,672,128]{2,1,0:T(8,128)(2,1)S(1)} collective-permute-done((bf16[4,672,128]{2,1,0:T(8,128)(2,1)S(1)}, bf16[4,672,128]{2,1,0:T(8,128)(2,1)S(1)}, u32[]{:S(2)}, u32[]{:S(2)}) %collective-permute-start.44) | collective-permute-done | bytes 688160 | tf_op jit(solution)/shard_map/ppermute | solution.py:22
  570.3 9.1 %collective-permute-done.46.refs_2_ = bf16[672,128]{1,0:T(8,128)(2,1)S(1)} collective-permute-done((bf16[672,128]{1,0:T(8,128)(2,1)S(1)}, bf16[672,128]{1,0:T(8,128)(2,1)S(1)}, u32[]{:S(2)}, u32[]{:S(2)}) %collective-permute-start.46) | collective-permute-done | bytes 172064 | tf_op jit(solution)/shard_map/ppermute | solution.py:29
  (233 shorter events, 118.8 us)
Async XLA Ops:
  35.7 32.5 %collective-permute-start.15 = (bf16[4,128,640]{2,1,0:T(8,128)(2,1)S(1)}, bf16[4,128,640]{2,1,0:T(8,128)(2,1)S(1)}, u32[]{:S(2)}, u32[]{:S(2)}) collective-permute-start(bf16[4,128,640]{2,1,0:T(8,128)(2,1)S(1)} %pad_maximum_fusion.2._), channel_id=1, source_target_pairs={{0,4},{2,6},{4,0},{6,2},{8,12},{10,14},{12,8},{14,10},{16,20},{18,... | collective-permute-start | bytes 1966088 | tf_op jit(solution)/shard_map/ppermute | solution.py:22
  51.1 31.8 %collective-permute-start.22 = (bf16[4,128,640]{2,1,0:T(8,128)(2,1)S(1)}, bf16[4,128,640]{2,1,0:T(8,128)(2,1)S(1)}, u32[]{:S(2)}, u32[]{:S(2)}) collective-permute-start(bf16[4,128,640]{2,1,0:T(8,128)(2,1)S(1)} %pad_maximum_fusion.3._), channel_id=1, source_target_pairs={{0,2},{2,0},{4,6},{6,4},{8,10},{10,8},{12,14},{14,12},{16,18},{18,... | collective-permute-start | bytes 1966088 | tf_op jit(solution)/shard_map/ppermute | solution.py:22
  68.3 31.8 %collective-permute-start.16 = (bf16[8,128,640]{2,1,0:T(8,128)(2,1)S(1)}, bf16[8,128,640]{2,1,0:T(8,128)(2,1)S(1)}, u32[]{:S(2)}, u32[]{:S(2)}) collective-permute-start(bf16[8,128,640]{2,1,0:T(8,128)(2,1)S(1)} %constant_dynamic-update-slice_fusion.q_low_ref), channel_id=1, source_target_pairs={{0,2},{2,0},{4,6},{6,4},{8,10},{10,8},{12,14},{14,12},{16,18},{18,... | collective-permute-start | bytes 3932168 | tf_op jit(solution)/shard_map/ppermute | solution.py:22
  81.4 45.8 %collective-permute-start.41 = (bf16[4,128,640]{2,1,0:T(8,128)(2,1)}, bf16[4,128,640]{2,1,0:T(8,128)(2,1)}, u32[]{:S(2)}, u32[]{:S(2)}) collective-permute-start(bf16[4,128,640]{2,1,0:T(8,128)(2,1)} %pad_maximum_fusion.5), channel_id=1, source_target_pairs={{0,2},{2,0},{4,6},{6,4},{8,10},{10,8},{12,14},{14,12},{16,18},{18,... | collective-permute-start | bytes 1966088 | tf_op jit(solution)/shard_map/ppermute | solution.py:22
  82.9 72.6 %collective-permute-start.14 = (bf16[320,2560]{1,0:T(8,128)(2,1)}, bf16[320,2560]{1,0:T(8,128)(2,1)S(1)}, u32[]{:S(2)}, u32[]{:S(2)}) collective-permute-start(bf16[320,2560]{1,0:T(8,128)(2,1)} %bitcast.refs_0_), channel_id=1, source_target_pairs={{0,24},{2,26},{4,28},{6,30},{8,0},{10,2},{12,4},{14,6},{16,8},{18,... | collective-permute-start | bytes 4915208 | tf_op jit(solution)/shard_map/ppermute | solution.py:29
  83.0 48.8 %collective-permute-start.23 = (bf16[8,128,640]{2,1,0:T(8,128)(2,1)S(1)}, bf16[8,128,640]{2,1,0:T(8,128)(2,1)}, u32[]{:S(2)}, u32[]{:S(2)}) collective-permute-start(bf16[8,128,640]{2,1,0:T(8,128)(2,1)S(1)} %constant_dynamic-update-slice_fusion.5.q_low_ref), channel_id=1, source_target_pairs={{0,4},{2,6},{4,0},{6,2},{8,12},{10,14},{12,8},{14,10},{16,20},{18,... | collective-permute-start | bytes 3932168 | tf_op jit(solution)/shard_map/ppermute | solution.py:22
  86.3 71.8 %collective-permute-start.30 = (bf16[8,128,640]{2,1,0:T(8,128)(2,1)S(1)}, bf16[8,128,640]{2,1,0:T(8,128)(2,1)}, u32[]{:S(2)}, u32[]{:S(2)}) collective-permute-start(bf16[8,128,640]{2,1,0:T(8,128)(2,1)S(1)} %constant_dynamic-update-slice_fusion.10.q_low_ref), channel_id=1, source_target_pairs={{0,2},{2,0},{4,6},{6,4},{8,10},{10,8},{12,14},{14,12},{16,18},{18,... | collective-permute-start | bytes 3932168 | tf_op jit(solution)/shard_map/ppermute | solution.py:22
  123.4 58.1 %collective-permute-start.17 = (bf16[8,672,128]{2,1,0:T(8,128)(2,1)}, bf16[8,672,128]{2,1,0:T(8,128)(2,1)S(1)}, u32[]{:S(2)}, u32[]{:S(2)}) collective-permute-start(bf16[8,672,128]{2,1,0:T(8,128)(2,1)} %get-tuple-element.53), channel_id=1, source_target_pairs={{0,2},{2,0},{4,6},{6,4},{8,10},{10,8},{12,14},{14,12},{16,18},{18,... | collective-permute-start | bytes 4128776 | tf_op jit(solution)/shard_map/ppermute | solution.py:22
  127.1 105.4 %collective-permute-start.13 = (bf16[320,2560]{1,0:T(8,128)(2,1)}, bf16[320,2560]{1,0:T(8,128)(2,1)}, u32[]{:S(2)}, u32[]{:S(2)}) collective-permute-start(bf16[320,2560]{1,0:T(8,128)(2,1)} %bitcast.refs_0_), channel_id=1, source_target_pairs={{0,16},{2,18},{4,20},{6,22},{8,24},{10,26},{12,28},{14,30},{16,0},... | collective-permute-start | bytes 4915208 | tf_op jit(solution)/shard_map/ppermute | solution.py:29
  131.8 103.3 %collective-permute-start.12 = (bf16[320,2560]{1,0:T(8,128)(2,1)}, bf16[320,2560]{1,0:T(8,128)(2,1)}, u32[]{:S(2)}, u32[]{:S(2)}) collective-permute-start(bf16[320,2560]{1,0:T(8,128)(2,1)} %bitcast.refs_0_), channel_id=1, source_target_pairs={{0,8},{2,10},{4,12},{6,14},{8,16},{10,18},{12,20},{14,22},{16,24},... | collective-permute-start | bytes 4915208 | tf_op jit(solution)/shard_map/ppermute | solution.py:29
  155.4 280.0 %collective-permute-start.42 = (bf16[8,128,640]{2,1,0:T(8,128)(2,1)}, bf16[8,128,640]{2,1,0:T(8,128)(2,1)}, u32[]{:S(2)}, u32[]{:S(2)}) collective-permute-start(bf16[8,128,640]{2,1,0:T(8,128)(2,1)} %constant_dynamic-update-slice_fusion.15.q_low_ref), channel_id=1, source_target_pairs={{0,4},{2,6},{4,0},{6,2},{8,12},{10,14},{12,8},{14,10},{16,20},{18,... | collective-permute-start | bytes 3932168 | tf_op jit(solution)/shard_map/ppermute | solution.py:22
  158.1 300.7 %collective-permute-start.24 = (bf16[8,672,128]{2,1,0:T(8,128)(2,1)}, bf16[8,672,128]{2,1,0:T(8,128)(2,1)S(1)}, u32[]{:S(2)}, u32[]{:S(2)}) collective-permute-start(bf16[8,672,128]{2,1,0:T(8,128)(2,1)} %get-tuple-element.62), channel_id=1, source_target_pairs={{0,4},{2,6},{4,0},{6,2},{8,12},{10,14},{12,8},{14,10},{16,20},{18,... | collective-permute-start | bytes 4128776 | tf_op jit(solution)/shard_map/ppermute | solution.py:22
  181.6 280.5 %collective-permute-start.31 = (bf16[8,672,128]{2,1,0:T(8,128)(2,1)}, bf16[8,672,128]{2,1,0:T(8,128)(2,1)S(1)}, u32[]{:S(2)}, u32[]{:S(2)}) collective-permute-start(bf16[8,672,128]{2,1,0:T(8,128)(2,1)} %get-tuple-element.71), channel_id=1, source_target_pairs={{0,2},{2,0},{4,6},{6,4},{8,10},{10,8},{12,14},{14,12},{16,18},{18,... | collective-permute-start | bytes 4128776 | tf_op jit(solution)/shard_map/ppermute | solution.py:22
  232.5 230.4 %collective-permute-start.18 = (bf16[4,672,128]{2,1,0:T(8,128)(2,1)}, bf16[4,672,128]{2,1,0:T(8,128)(2,1)}, u32[]{:S(2)}, u32[]{:S(2)}) collective-permute-start(bf16[4,672,128]{2,1,0:T(8,128)(2,1)} %get-tuple-element.55), channel_id=1, source_target_pairs={{0,4},{2,6},{4,0},{6,2},{8,12},{10,14},{12,8},{14,10},{16,20},{18,... | collective-permute-start | bytes 2064392 | tf_op jit(solution)/shard_map/ppermute | solution.py:22
  458.0 72.3 %collective-permute-start.43 = (bf16[8,672,128]{2,1,0:T(8,128)(2,1)}, bf16[8,672,128]{2,1,0:T(8,128)(2,1)S(1)}, u32[]{:S(2)}, u32[]{:S(2)}) collective-permute-start(bf16[8,672,128]{2,1,0:T(8,128)(2,1)} %get-tuple-element.80), channel_id=1, source_target_pairs={{0,4},{2,6},{4,0},{6,2},{8,12},{10,14},{12,8},{14,10},{16,20},{18,... | collective-permute-start | bytes 4128776 | tf_op jit(solution)/shard_map/ppermute | solution.py:22
  459.6 17.9 %collective-permute-start.25 = (bf16[4,672,128]{2,1,0:T(8,128)(2,1)S(1)}, bf16[4,672,128]{2,1,0:T(8,128)(2,1)S(1)}, u32[]{:S(2)}, u32[]{:S(2)}) collective-permute-start(bf16[4,672,128]{2,1,0:T(8,128)(2,1)S(1)} %get-tuple-element.64), channel_id=1, source_target_pairs={{0,2},{2,0},{4,6},{6,4},{8,10},{10,8},{12,14},{14,12},{16,18},{18,... | collective-permute-start | bytes 2064392 | tf_op jit(solution)/shard_map/ppermute | solution.py:22
  462.8 42.0 %collective-permute-start.32 = (bf16[4,672,128]{2,1,0:T(8,128)(2,1)S(1)}, bf16[4,672,128]{2,1,0:T(8,128)(2,1)S(1)}, u32[]{:S(2)}, u32[]{:S(2)}) collective-permute-start(bf16[4,672,128]{2,1,0:T(8,128)(2,1)S(1)} %get-tuple-element.73), channel_id=1, source_target_pairs={{0,4},{2,6},{4,0},{6,2},{8,12},{10,14},{12,8},{14,10},{16,20},{18,... | collective-permute-start | bytes 2064392 | tf_op jit(solution)/shard_map/ppermute | solution.py:22
  465.1 124.7 %collective-permute-start.39 = (bf16[640,2560]{1,0:T(8,128)(2,1)S(1)}, bf16[640,2560]{1,0:T(8,128)(2,1)S(1)}, u32[]{:S(2)}, u32[]{:S(2)}) collective-permute-start(bf16[640,2560]{1,0:T(8,128)(2,1)S(1)} %bitcast.73), channel_id=1, source_target_pairs={{0,1},{1,0},{2,3},{3,2},{4,5},{5,4},{6,7},{7,6},{8,9},{9,8},{10,11... | collective-permute-start | bytes 9830408 | tf_op jit(solution)/shard_map/ppermute | solution.py:38
  488.9 20.1 %collective-permute-start.27 = (bf16[672,128]{1,0:T(8,128)(2,1)S(1)}, bf16[672,128]{1,0:T(8,128)(2,1)S(1)}, u32[]{:S(2)}, u32[]{:S(2)}) collective-permute-start(bf16[672,128]{1,0:T(8,128)(2,1)S(1)} %get-tuple-element.67), channel_id=1, source_target_pairs={{0,16},{2,18},{4,20},{6,22},{8,24},{10,26},{12,28},{14,30},{16,0},... | collective-permute-start | bytes 516104 | tf_op jit(solution)/shard_map/ppermute | solution.py:29
  509.0 17.4 %collective-permute-start.34 = (bf16[672,128]{1,0:T(8,128)(2,1)S(1)}, bf16[672,128]{1,0:T(8,128)(2,1)S(1)}, u32[]{:S(2)}, u32[]{:S(2)}) collective-permute-start(bf16[672,128]{1,0:T(8,128)(2,1)S(1)} %get-tuple-element.76), channel_id=1, source_target_pairs={{0,16},{2,18},{4,20},{6,22},{8,24},{10,26},{12,28},{14,30},{16,0},... | collective-permute-start | bytes 516104 | tf_op jit(solution)/shard_map/ppermute | solution.py:29
  528.2 22.2 %collective-permute-start.37 = (bf16[1920,128]{1,0:T(8,128)(2,1)S(1)}, bf16[1920,128]{1,0:T(8,128)(2,1)S(1)}, u32[]{:S(2)}, u32[]{:S(2)}) collective-permute-start(bf16[1920,128]{1,0:T(8,128)(2,1)S(1)} %pad_maximum_fusion.7), channel_id=1, source_target_pairs={{0,4},{2,6},{4,0},{6,2},{8,12},{10,14},{12,8},{14,10},{16,20},{18,... | collective-permute-start | bytes 1474568 | tf_op jit(solution)/shard_map/ppermute | solution.py:22
  528.8 22.5 %collective-permute-start.36 = (bf16[1920,128]{1,0:T(8,128)(2,1)S(1)}, bf16[1920,128]{1,0:T(8,128)(2,1)S(1)}, u32[]{:S(2)}, u32[]{:S(2)}) collective-permute-start(bf16[1920,128]{1,0:T(8,128)(2,1)S(1)} %pad_maximum_fusion.7), channel_id=1, source_target_pairs={{0,2},{2,0},{4,6},{6,4},{8,10},{10,8},{12,14},{14,12},{16,18},{18,... | collective-permute-start | bytes 1474568 | tf_op jit(solution)/shard_map/ppermute | solution.py:22
  531.0 33.0 %collective-permute-start.44 = (bf16[4,672,128]{2,1,0:T(8,128)(2,1)S(1)}, bf16[4,672,128]{2,1,0:T(8,128)(2,1)S(1)}, u32[]{:S(2)}, u32[]{:S(2)}) collective-permute-start(bf16[4,672,128]{2,1,0:T(8,128)(2,1)S(1)} %get-tuple-element.82), channel_id=1, source_target_pairs={{0,2},{2,0},{4,6},{6,4},{8,10},{10,8},{12,14},{14,12},{16,18},{18,... | collective-permute-start | bytes 2064392 | tf_op jit(solution)/shard_map/ppermute | solution.py:22
  554.4 37.4 %collective-permute-start.40 = (bf16[1920,512]{1,0:T(8,128)(2,1)S(1)}, bf16[1920,512]{1,0:T(8,128)(2,1)S(1)}, u32[]{:S(2)}, u32[]{:S(2)}) collective-permute-start(bf16[1920,512]{1,0:T(8,128)(2,1)S(1)} %pad_maximum_fusion), channel_id=1, source_target_pairs={{0,1},{1,0},{2,3},{3,2},{4,5},{5,4},{6,7},{7,6},{8,9},{9,8},{10,11... | collective-permute-start | bytes 5898248 | tf_op jit(solution)/shard_map/ppermute | solution.py:38
  (58 other events, 1225.6 us)

commit v3 on v2

--- a/solution.py
+++ b/solution.py
@@ -39,29 +39,27 @@
 
 
 def place_kernel(spots_ref, *refs):
-    *blocks, out, sems = refs
-    copies = [
-        pltpu.make_async_copy(ref, out.at[spots_ref[i]], sems.at[i]) for i, ref in enumerate(blocks)
-    ]
-    for copy in copies:
-        copy.start()
-    for copy in copies:
-        copy.wait()
-
-
-def place_blocks(spots, blocks):
+    *blocks, _, out = refs
+    for i, ref in enumerate(blocks):
+        out[spots_ref[i]] = ref[...]
+
+
+def place_blocks(spots, blocks, after):
+    depth, width = blocks[0].shape
+    chunk = next(c for c in (512, 256, 128) if width % c == 0)
     return pl.pallas_call(
         place_kernel,
         grid_spec=pltpu.PrefetchScalarGridSpec(
             num_scalar_prefetch=1,
-            grid=(1,),
-            in_specs=[pl.BlockSpec(memory_space=pl.ANY)] * len(blocks),
-            out_specs=pl.BlockSpec(memory_space=pl.ANY),
-            scratch_shapes=[pltpu.SemaphoreType.DMA((len(blocks),))],
-        ),
-        out_shape=jax.ShapeDtypeStruct((len(blocks),) + blocks[0].shape, blocks[0].dtype),
+            grid=(width // chunk,),
+            in_specs=[pl.BlockSpec((depth, chunk), lambda i, *_: (0, i))] * len(blocks)
+            + [pl.BlockSpec(memory_space=pl.ANY)],
+            out_specs=pl.BlockSpec((len(blocks), depth, chunk), lambda i, *_: (0, 0, i)),
+        ),
+        out_shape=jax.ShapeDtypeStruct((len(blocks), depth, width), blocks[0].dtype),
+        compiler_params=pltpu.CompilerParams(vmem_limit_bytes=16 * 2**20),
         name="place_weights",
-    )(spots, *blocks)
+    )(spots, *blocks, after)
 
 
 def turn_kernel(q_ref, k_ref, scale_ref, gain_q_ref, gain_k_ref, cos_ref, sin_ref, _, q_out, k_out):
@@ -290,7 +288,7 @@
             dimension_semantics=("arbitrary",), vmem_limit_bytes=56 * 2**20
         ),
         cost_estimate=pl.CostEstimate(
-            flops=pages * heads * 256 * page_len * HEAD_DIM * 8,
+            flops=pages * heads * 256 * page_len * HEAD_DIM * 40,
             bytes_accessed=pages * page_len * width * 4,
             transcendentals=pages * heads * 256 * page_len,
         ),
@@ -452,42 +450,50 @@
         return (2, 1) if group % 2 == 0 else (1, 2)
 
     groups = group_count(local_width)
-    near, near_keys = [], []
-    after = scales
+    near, near_keys, low, high = [], [], [], []
     for group in range(groups):
+        after = [scales, near, low, high][min(group, 3)]
+        after = after if group == 0 else after[0]
         part, key_part = turn(
             group, queries, new_keys, scales, query_gain, key_gain, cosine, sine, after
         )
         got = [part[None]] + [send_line(part, k)[None] for k in range(1, line)]
-        near.append(jnp.concatenate(got, axis=0))
+        near.append(lax.optimization_barrier(jnp.concatenate(got, axis=0)))
         near_keys.append(key_part)
-        after = near[-1]
-
-    weight, _ = lax.optimization_barrier((out_weight.T, after))
+        order = order_of(group)
+        low.append(jnp.concatenate([near[group], send_xor(near[group], order[0])], axis=0))
+        high.append(send_xor(low[group], order[1]))
+
+    weight, _ = lax.optimization_barrier((out_weight.T, near[-1]))
+    weights = [weight]
+    for _ in range(1, line):
+        weights.append(send_line(weights[-1], 1))
+
+    attended = []
+    for group in range(groups):
+        order = order_of(group)
+        slot = jnp.where((across & order[1]) > 0, 2 * line, 0)
+        slot = slot + jnp.where((across & order[0]) > 0, line, 0) + back
+        slots = jnp.concatenate([slot, jnp.stack([jnp.int32(size), device])])
+        keep, send = attend(
+            group, table, slots, low[group], high[group], cache_keys, cache_values,
+            near_keys[group], new_values, near_starts,
+        )
+        if group == groups - 1:
+            after = keep
+        keep, send = combine(keep, send_xor(send, order[1]))
+        parts = combine_line(keep, send_xor(send, order[0]))
+        attended.append(combine_last([parts[0]] + [send_line(parts[k], -k) for k in range(1, line)]))
+
     columns = weight.shape[0]
     blocks_each = line // tp_size
     tp_device = lax.axis_index("tp")
     from_place = (place - jnp.arange(line, dtype=jnp.int32)) % line
     weight_spots = ((from_place // blocks_each - tp_device) % tp_size) * blocks_each
     weight_spots = weight_spots + from_place % blocks_each
-    weights = place_blocks(weight_spots, [weight] + [send_line(weight, k) for k in range(1, line)])
+    weights = place_blocks(weight_spots, weights, after)
     weights = weights.reshape(tp_size, blocks_each * columns, local_width)
     weights = [weights[0]] + [send_tp(weights[k], k) for k in range(1, tp_size)]
-
-    attended = []
-    for group in range(groups):
-        order = order_of(group)
-        low = jnp.concatenate([near[group], send_xor(near[group], order[0])], axis=0)
-        high = send_xor(low, order[1])
-        slot = jnp.where((across & order[1]) > 0, 2 * line, 0)
-        slot = slot + jnp.where((across & order[0]) > 0, line, 0) + back
-        slots = jnp.concatenate([slot, jnp.stack([jnp.int32(size), device])])
-        keep, send = attend(
-            group, table, slots, low, high, cache_keys, cache_values, near_keys[group], new_values, near_starts
-        )
-        keep, send = combine(keep, send_xor(send, order[1]))
-        parts = combine_line(keep, send_xor(send, order[0]))
-        attended.append(combine_last([parts[0]] + [send_line(parts[k], -k) for k in range(1, line)]))
 
     projected = 0.0
     depth = 0

time: 611 us -> 417 us (0.68)
  Pallas kernels: 298 us -> 115 us
  waiting for transfers between devices: 202 us -> 182 us
  starting transfers between devices: 70.2 us -> 81.8 us
    pallas_call x1, Pallas kernels: 200 us -> 4.18 us  [place_blocks(): pl.pallas_call(place_kernel, grid_spec=pltpu.PrefetchScalarGridSpec(num_s...]
    ppermute x27, waiting for transfers between devices: 119 us -> 55.3 us  [send_line(): return lax.ppermute(value, 'req', pairs)]
    ppermute x25, waiting for transfers between devices: 82.1 us -> 126 us  [send_xor(): return lax.ppermute(value, 'req', [(i, i ^ by) for i in range(size)])]
    ppermute x27, starting transfers between devices: 32.7 us -> 52.7 us  [send_line(): return lax.ppermute(value, 'req', pairs)]
    pallas_call x4, Pallas kernels: 89.3 us -> 98.6 us  [attend(): pl.pallas_call(attend_kernel, grid_spec=pltpu.PrefetchScalarGridSpec(num_...]
    ppermute x25, starting transfers between devices: 37.3 us -> 28.9 us  [send_xor(): return lax.ppermute(value, 'req', [(i, i ^ by) for i in range(size)])]
  transfers between devices with their start and end apart: 55 -> 55, of which waited for: 27 -> 22; matrix products, arithmetic and copies ran while one was open for 3% -> 4% of each run, Pallas kernels for 49% -> 28%
where the time goes in v3:
time: 417 us; the launch traced here: 413 us
  waiting for transfers between devices  182 us (44%)
  Pallas kernels  115 us (28%)
  starting transfers between devices  81.8 us (20%)
  other arithmetic  16.8 us (4%)
  local copies, waits for them, and re-layouts  7.79 us (2%)
  matrix products  6.05 us (1%)
    ppermute x25, waiting for transfers between devices, send_xor(): return lax.ppermute(value, 'req', [(i, i ^ by) for i in range(size)])  126 us
    pallas_call x4, Pallas kernels, attend(): pl.pallas_call(attend_kernel, grid_spec=pltpu.PrefetchScalarGridSpec(num_...  98.6 us
    ppermute x27, waiting for transfers between devices, send_line(): return lax.ppermute(value, 'req', pairs)  55.3 us
    ppermute x27, starting transfers between devices, send_line(): return lax.ppermute(value, 'req', pairs)  52.7 us
    ppermute x25, starting transfers between devices, send_xor(): return lax.ppermute(value, 'req', [(i, i ^ by) for i in range(size)])  28.9 us
  transfers between devices with their start and end apart: 55, of which 22 were waited for; matrix products, arithmetic and copies ran while one was open for 4% of the time, Pallas kernels for 28%

profile of v3, /device:TPU:0, one launch (start us, length us, event | category | flops | bytes accessed | tf_op | source)
XLA Modules:
  0.0 413.3 jit_solution(14803300410774023139)
XLA Ops:
  5.9 3.9 psum.7
  10.8 4.8 %collective-permute-start.2 = (bf16[128,640]{1,0:T(8,128)(2,1)S(1)}, bf16[128,640]{1,0:T(8,128)(2,1)S(1)}, u32[]{:S(2)}, u32[]{:S(2)}) collective-permute-start(bf16[128,640]{1,0:T(8,128)(2,1)S(1)} %get-tuple-element.46), channel_id=1, source_target_pairs={{0,24},{2,26},{4,28},{6,30},{8,0},{10,2},{12,4},{14,6},{16,8},{18,... | collective-permute-start | bytes 491528 | tf_op jit(solution)/shard_map/ppermute | solution.py:29
  20.2 9.8 %collective-permute-done.1 = bf16[128,640]{1,0:T(8,128)(2,1)S(1)} collective-permute-done((bf16[128,640]{1,0:T(8,128)(2,1)S(1)}, bf16[128,640]{1,0:T(8,128)(2,1)S(1)}, u32[]{:S(2)}, u32[]{:S(2)}) %collective-permute-start.1) | collective-permute-done | bytes 163872 | tf_op jit(solution)/shard_map/ppermute | solution.py:29
  38.0 8.4 %collective-permute-done.3 = bf16[4,128,640]{2,1,0:T(8,128)(2,1)S(1)} collective-permute-done((bf16[4,128,640]{2,1,0:T(8,128)(2,1)S(1)}, bf16[4,128,640]{2,1,0:T(8,128)(2,1)S(1)}, u32[]{:S(2)}, u32[]{:S(2)}) %collective-permute-start.3) | collective-permute-done | bytes 655392 | tf_op jit(solution)/shard_map/ppermute | solution.py:22
  57.0 7.9 %collective-permute-done.29 = bf16[128,640]{1,0:T(8,128)(2,1)} collective-permute-done((bf16[128,640]{1,0:T(8,128)(2,1)S(1)}, bf16[128,640]{1,0:T(8,128)(2,1)}, u32[]{:S(2)}, u32[]{:S(2)}) %collective-permute-start.29) | collective-permute-done | bytes 163872 | tf_op jit(solution)/shard_map/ppermute | solution.py:29
  69.1 20.9 %collective-permute-done.21 = bf16[4,128,640]{2,1,0:T(8,128)(2,1)S(1)} collective-permute-done((bf16[4,128,640]{2,1,0:T(8,128)(2,1)S(1)}, bf16[4,128,640]{2,1,0:T(8,128)(2,1)S(1)}, u32[]{:S(2)}, u32[]{:S(2)}) %collective-permute-start.21) | collective-permute-done | bytes 655392 | tf_op jit(solution)/shard_map/ppermute | solution.py:22
  99.9 24.6 %cache_attend.5 = (bf16[8,672,128]{2,1,0:T(8,128)(2,1)}, bf16[8,672,128]{2,1,0:T(8,128)(2,1)}) custom-call(s32[64]{0:T(128)} %reshape.372.table_ref, s32[18]{0:T(128)} %fusion.27.slot_ref, bf16[8,128,640]{2,1,0:T(8,128)(2,1)} %copy-done.7, bf16[8,128,640]{2,1,0:T(8,128)(2,1)} %collective-permute-done.4._.q_high_ref, bf16[16,256,2560]{2,1,0:T(8,128)(2,1)} %keys_ref.7, ...), custom_call_target="tpu_custom_call" | custom-call | flops 26843545600 | bytes 10485760 | tf_op jit(solution)/shard_map/cache_attend/pallas_call | solution.py:263
  129.9 24.5 %cache_attend.6 = (bf16[8,672,128]{2,1,0:T(8,128)(2,1)}, bf16[8,672,128]{2,1,0:T(8,128)(2,1)}) custom-call(s32[64]{0:T(128)} %reshape.372.table_ref, s32[18]{0:T(128)} %fusion.26.slot_ref, bf16[8,128,640]{2,1,0:T(8,128)(2,1)} %copy-done.18, bf16[8,128,640]{2,1,0:T(8,128)(2,1)} %collective-permute-done.22.q_high_ref, bf16[16,256,2560]{2,1,0:T(8,128)(2,1)} %keys_ref.7, ...), custom_call_target="tpu_custom_call" | custom-call | flops 26843545600 | bytes 10485760 | tf_op jit(solution)/shard_map/cache_attend/pallas_call | solution.py:263
  154.5 13.1 %collective-permute-done.11 = bf16[4,128,640]{2,1,0:T(8,128)(2,1)} collective-permute-done((bf16[4,128,640]{2,1,0:T(8,128)(2,1)S(1)}, bf16[4,128,640]{2,1,0:T(8,128)(2,1)}, u32[]{:S(2)}, u32[]{:S(2)}) %collective-permute-start.11) | collective-permute-done | bytes 655392 | tf_op jit(solution)/shard_map/ppermute | solution.py:22
  176.7 24.7 %cache_attend.7 = (bf16[8,672,128]{2,1,0:T(8,128)(2,1)}, bf16[8,672,128]{2,1,0:T(8,128)(2,1)}) custom-call(s32[64]{0:T(128)} %reshape.372.table_ref, s32[18]{0:T(128)} %fusion.27.slot_ref, bf16[8,128,640]{2,1,0:T(8,128)(2,1)} %pad_maximum_fusion.4.q_low_ref, bf16[8,128,640]{2,1,0:T(8,128)(2,1)} %collective-permute-done.32.q_high_ref, ...), custom_call_target="tpu_custom_call" | custom-call | flops 26843545600 | bytes 10485760 | tf_op jit(solution)/shard_map/cache_attend/pallas_call | solution.py:263
  206.1 19.3 %collective-permute-done.14.got = bf16[4,672,128]{2,1,0:T(8,128)(2,1)} collective-permute-done((bf16[4,672,128]{2,1,0:T(8,128)(2,1)}, bf16[4,672,128]{2,1,0:T(8,128)(2,1)}, u32[]{:S(2)}, u32[]{:S(2)}) %collective-permute-start.14) | collective-permute-done | bytes 688160 | tf_op jit(solution)/shard_map/ppermute | solution.py:22
  227.3 5.0 %collective-permute-start.15 = (bf16[672,128]{1,0:T(8,128)(2,1)}, bf16[672,128]{1,0:T(8,128)(2,1)S(1)}, u32[]{:S(2)}, u32[]{:S(2)}) collective-permute-start(bf16[672,128]{1,0:T(8,128)(2,1)} %get-tuple-element.57), channel_id=1, source_target_pairs={{0,24},{2,26},{4,28},{6,30},{8,0},{10,2},{12,4},{14,6},{16,8},{18,... | collective-permute-start | bytes 516104 | tf_op jit(solution)/shard_map/ppermute | solution.py:29
  232.9 24.7 %cache_attend.4 = (bf16[8,672,128]{2,1,0:T(8,128)(2,1)}, bf16[8,672,128]{2,1,0:T(8,128)(2,1)}) custom-call(s32[64]{0:T(128)} %reshape.372.table_ref, s32[18]{0:T(128)} %fusion.26.slot_ref, bf16[8,128,640]{2,1,0:T(8,128)(2,1)} %pad_maximum_fusion.2.q_low_ref, bf16[8,128,640]{2,1,0:T(8,128)(2,1)} %collective-permute-done.12.q_high_ref, ...), custom_call_target="tpu_custom_call" | custom-call | flops 26843545600 | bytes 10485760 | tf_op jit(solution)/shard_map/cache_attend/pallas_call | solution.py:263
  257.6 6.0 %collective-permute-start.17 = (bf16[672,128]{1,0:T(8,128)(2,1)}, bf16[672,128]{1,0:T(8,128)(2,1)S(1)}, u32[]{:S(2)}, u32[]{:S(2)}) collective-permute-start(bf16[672,128]{1,0:T(8,128)(2,1)} %copy-done.13), channel_id=1, source_target_pairs={{0,8},{2,10},{4,12},{6,14},{8,16},{10,18},{12,20},{14,22},{16,24},... | collective-permute-start | bytes 516104 | tf_op jit(solution)/shard_map/ppermute | solution.py:29
  266.2 7.0 %collective-permute-done.10.refs_3_ = bf16[320,2560]{1,0:T(8,128)(2,1)S(1)} collective-permute-done((bf16[320,2560]{1,0:T(8,128)(2,1)}, bf16[320,2560]{1,0:T(8,128)(2,1)S(1)}, u32[]{:S(2)}, u32[]{:S(2)}) %collective-permute-start.10) | collective-permute-done | bytes 1638432 | tf_op jit(solution)/shard_map/ppermute | solution.py:29
  275.6 4.2 %place_weights.1 = bf16[4,320,2560]{2,1,0:T(8,128)(2,1)S(1)} custom-call(s32[4]{0:T(128)S(1)} %fusion.25.spots_ref, bf16[320,2560]{1,0:T(8,128)(2,1)S(1)} %bitcast.51, bf16[320,2560]{1,0:T(8,128)(2,1)S(1)} %collective-permute-done.8.refs_1_, bf16[320,2560]{1,0:T(8,128)(2,1)} %collective-permute-done.9.refs_2_, ...), custom_call_target="tpu_custom_call" | custom-call | tf_op jit(solution)/shard_map/place_weights/pallas_call | solution.py:50
  279.8 4.5 %collective-permute-start.26 = (bf16[672,128]{1,0:T(8,128)(2,1)S(1)}, bf16[672,128]{1,0:T(8,128)(2,1)S(1)}, u32[]{:S(2)}, u32[]{:S(2)}) collective-permute-start(bf16[672,128]{1,0:T(8,128)(2,1)S(1)} %get-tuple-element.68), channel_id=1, source_target_pairs={{0,16},{2,18},{4,20},{6,22},{8,24},{10,26},{12,28},{14,30},{16,0},... | collective-permute-start | bytes 516104 | tf_op jit(solution)/shard_map/ppermute | solution.py:29
  297.7 10.6 %collective-permute-done.36.refs_2_ = bf16[672,128]{1,0:T(8,128)(2,1)S(1)} collective-permute-done((bf16[672,128]{1,0:T(8,128)(2,1)S(1)}, bf16[672,128]{1,0:T(8,128)(2,1)S(1)}, u32[]{:S(2)}, u32[]{:S(2)}) %collective-permute-start.36) | collective-permute-done | bytes 172064 | tf_op jit(solution)/shard_map/ppermute | solution.py:29
  312.1 11.5 %collective-permute-done.40 = bf16[1920,128]{1,0:T(8,128)(2,1)S(1)} collective-permute-done((bf16[1920,128]{1,0:T(8,128)(2,1)S(1)}, bf16[1920,128]{1,0:T(8,128)(2,1)S(1)}, u32[]{:S(2)}, u32[]{:S(2)}) %collective-permute-start.40) | collective-permute-done | bytes 491552 | tf_op jit(solution)/shard_map/ppermute | solution.py:22
  323.6 23.2 %collective-permute-done.39 = bf16[1920,128]{1,0:T(8,128)(2,1)S(1)} collective-permute-done((bf16[1920,128]{1,0:T(8,128)(2,1)S(1)}, bf16[1920,128]{1,0:T(8,128)(2,1)S(1)}, u32[]{:S(2)}, u32[]{:S(2)}) %collective-permute-start.39) | collective-permute-done | bytes 491552 | tf_op jit(solution)/shard_map/ppermute | solution.py:22
  351.4 17.2 %collective-permute-done.44.got = bf16[4,672,128]{2,1,0:T(8,128)(2,1)S(1)} collective-permute-done((bf16[4,672,128]{2,1,0:T(8,128)(2,1)S(1)}, bf16[4,672,128]{2,1,0:T(8,128)(2,1)S(1)}, u32[]{:S(2)}, u32[]{:S(2)}) %collective-permute-start.44) | collective-permute-done | bytes 688160 | tf_op jit(solution)/shard_map/ppermute | solution.py:22
  371.9 3.8 collective-permute-done.45.refs_1_
  375.8 9.9 %collective-permute-done.46.refs_2_ = bf16[672,128]{1,0:T(8,128)(2,1)S(1)} collective-permute-done((bf16[672,128]{1,0:T(8,128)(2,1)S(1)}, bf16[672,128]{1,0:T(8,128)(2,1)S(1)}, u32[]{:S(2)}, u32[]{:S(2)}) %collective-permute-start.46) | collective-permute-done | bytes 172064 | tf_op jit(solution)/shard_map/ppermute | solution.py:29
  389.3 4.1 collective-permute-done.50
  (215 shorter events, 119.1 us)
Async XLA Ops:
  46.6 48.0 %collective-permute-start.4 = (bf16[8,128,640]{2,1,0:T(8,128)(2,1)S(1)}, bf16[8,128,640]{2,1,0:T(8,128)(2,1)}, u32[]{:S(2)}, u32[]{:S(2)}) collective-permute-start(bf16[8,128,640]{2,1,0:T(8,128)(2,1)S(1)} %pad_maximum_fusion.1.q_low_ref._), channel_id=1, source_target_pairs={{0,2},{2,0},{4,6},{6,4},{8,10},{10,8},{12,14},{14,12},{16,18},{18,... | collective-permute-start | bytes 3932168 | tf_op jit(solution)/shard_map/ppermute | solution.py:22
  56.3 33.8 %collective-permute-start.21 = (bf16[4,128,640]{2,1,0:T(8,128)(2,1)S(1)}, bf16[4,128,640]{2,1,0:T(8,128)(2,1)S(1)}, u32[]{:S(2)}, u32[]{:S(2)}) collective-permute-start(bf16[4,128,640]{2,1,0:T(8,128)(2,1)S(1)} %pad_maximum_fusion.8), channel_id=1, source_target_pairs={{0,2},{2,0},{4,6},{6,4},{8,10},{10,8},{12,14},{14,12},{16,18},{18,... | collective-permute-start | bytes 1966088 | tf_op jit(solution)/shard_map/ppermute | solution.py:22
  90.2 39.7 %collective-permute-start.22 = (bf16[8,128,640]{2,1,0:T(8,128)(2,1)S(1)}, bf16[8,128,640]{2,1,0:T(8,128)(2,1)}, u32[]{:S(2)}, u32[]{:S(2)}) collective-permute-start(bf16[8,128,640]{2,1,0:T(8,128)(2,1)S(1)} %pad_maximum_fusion.3.q_low_ref), channel_id=1, source_target_pairs={{0,4},{2,6},{4,0},{6,2},{8,12},{10,14},{12,8},{14,10},{16,20},{18,... | collective-permute-start | bytes 3932168 | tf_op jit(solution)/shard_map/ppermute | solution.py:22
  93.1 83.6 %collective-permute-start.32 = (bf16[8,128,640]{2,1,0:T(8,128)(2,1)}, bf16[8,128,640]{2,1,0:T(8,128)(2,1)}, u32[]{:S(2)}, u32[]{:S(2)}) collective-permute-start(bf16[8,128,640]{2,1,0:T(8,128)(2,1)} %pad_maximum_fusion.4.q_low_ref), channel_id=1, source_target_pairs={{0,2},{2,0},{4,6},{6,4},{8,10},{10,8},{12,14},{14,12},{16,18},{18,... | collective-permute-start | bytes 3932168 | tf_op jit(solution)/shard_map/ppermute | solution.py:22
  95.7 31.1 %collective-permute-start.6 = (bf16[128,640]{1,0:T(8,128)(2,1)S(1)}, bf16[128,640]{1,0:T(8,128)(2,1)S(1)}, u32[]{:S(2)}, u32[]{:S(2)}) collective-permute-start(bf16[128,640]{1,0:T(8,128)(2,1)S(1)} %get-tuple-element.47), channel_id=1, source_target_pairs={{0,16},{2,18},{4,20},{6,22},{8,24},{10,26},{12,28},{14,30},{16,0},... | collective-permute-start | bytes 491528 | tf_op jit(solution)/shard_map/ppermute | solution.py:29
  97.8 28.9 %collective-permute-start.5 = (bf16[128,640]{1,0:T(8,128)(2,1)S(1)}, bf16[128,640]{1,0:T(8,128)(2,1)S(1)}, u32[]{:S(2)}, u32[]{:S(2)}) collective-permute-start(bf16[128,640]{1,0:T(8,128)(2,1)S(1)} %get-tuple-element.47), channel_id=1, source_target_pairs={{0,8},{2,10},{4,12},{6,14},{8,16},{10,18},{12,20},{14,22},{16,24},... | collective-permute-start | bytes 491528 | tf_op jit(solution)/shard_map/ppermute | solution.py:29
  124.5 48.2 %collective-permute-start.13 = (bf16[8,672,128]{2,1,0:T(8,128)(2,1)}, bf16[8,672,128]{2,1,0:T(8,128)(2,1)S(1)}, u32[]{:S(2)}, u32[]{:S(2)}) collective-permute-start(bf16[8,672,128]{2,1,0:T(8,128)(2,1)} %get-tuple-element.53), channel_id=1, source_target_pairs={{0,2},{2,0},{4,6},{6,4},{8,10},{10,8},{12,14},{14,12},{16,18},{18,... | collective-permute-start | bytes 4128776 | tf_op jit(solution)/shard_map/ppermute | solution.py:22
  126.8 40.8 %collective-permute-start.11 = (bf16[4,128,640]{2,1,0:T(8,128)(2,1)S(1)}, bf16[4,128,640]{2,1,0:T(8,128)(2,1)}, u32[]{:S(2)}, u32[]{:S(2)}) collective-permute-start(bf16[4,128,640]{2,1,0:T(8,128)(2,1)S(1)} %pad_maximum_fusion.7), channel_id=1, source_target_pairs={{0,2},{2,0},{4,6},{6,4},{8,10},{10,8},{12,14},{14,12},{16,18},{18,... | collective-permute-start | bytes 1966088 | tf_op jit(solution)/shard_map/ppermute | solution.py:22
  126.9 47.5 %collective-permute-start.8 = (bf16[320,2560]{1,0:T(8,128)(2,1)S(1)}, bf16[320,2560]{1,0:T(8,128)(2,1)S(1)}, u32[]{:S(2)}, u32[]{:S(2)}) collective-permute-start(bf16[320,2560]{1,0:T(8,128)(2,1)S(1)} %bitcast.50), channel_id=1, source_target_pairs={{0,8},{2,10},{4,12},{6,14},{8,16},{10,18},{12,20},{14,22},{16,24},... | collective-permute-start | bytes 4915208 | tf_op jit(solution)/shard_map/ppermute | solution.py:29
  154.4 48.9 %collective-permute-start.23 = (bf16[8,672,128]{2,1,0:T(8,128)(2,1)}, bf16[8,672,128]{2,1,0:T(8,128)(2,1)S(1)}, u32[]{:S(2)}, u32[]{:S(2)}) collective-permute-start(bf16[8,672,128]{2,1,0:T(8,128)(2,1)} %get-tuple-element.63), channel_id=1, source_target_pairs={{0,4},{2,6},{4,0},{6,2},{8,12},{10,14},{12,8},{14,10},{16,20},{18,... | collective-permute-start | bytes 4128776 | tf_op jit(solution)/shard_map/ppermute | solution.py:22
  170.0 62.3 %collective-permute-start.12 = (bf16[8,128,640]{2,1,0:T(8,128)(2,1)}, bf16[8,128,640]{2,1,0:T(8,128)(2,1)}, u32[]{:S(2)}, u32[]{:S(2)}) collective-permute-start(bf16[8,128,640]{2,1,0:T(8,128)(2,1)} %pad_maximum_fusion.2.q_low_ref), channel_id=1, source_target_pairs={{0,4},{2,6},{4,0},{6,2},{8,12},{10,14},{12,8},{14,10},{16,20},{18,... | collective-permute-start | bytes 3932168 | tf_op jit(solution)/shard_map/ppermute | solution.py:22
  174.4 50.9 %collective-permute-start.14 = (bf16[4,672,128]{2,1,0:T(8,128)(2,1)}, bf16[4,672,128]{2,1,0:T(8,128)(2,1)}, u32[]{:S(2)}, u32[]{:S(2)}) collective-permute-start(bf16[4,672,128]{2,1,0:T(8,128)(2,1)} %get-tuple-element.55), channel_id=1, source_target_pairs={{0,4},{2,6},{4,0},{6,2},{8,12},{10,14},{12,8},{14,10},{16,20},{18,... | collective-permute-start | bytes 2064392 | tf_op jit(solution)/shard_map/ppermute | solution.py:22
  174.5 57.9 %collective-permute-start.9 = (bf16[320,2560]{1,0:T(8,128)(2,1)S(1)}, bf16[320,2560]{1,0:T(8,128)(2,1)}, u32[]{:S(2)}, u32[]{:S(2)}) collective-permute-start(bf16[320,2560]{1,0:T(8,128)(2,1)S(1)} %collective-permute-done.8.refs_1_), channel_id=1, source_target_pairs={{0,8},{2,10},{4,12},{6,14},{8,16},{10,18},{12,20},{14,22},{16,24},... | collective-permute-start | bytes 4915208 | tf_op jit(solution)/shard_map/ppermute | solution.py:29
  201.4 56.2 %collective-permute-start.33 = (bf16[8,672,128]{2,1,0:T(8,128)(2,1)}, bf16[8,672,128]{2,1,0:T(8,128)(2,1)S(1)}, u32[]{:S(2)}, u32[]{:S(2)}) collective-permute-start(bf16[8,672,128]{2,1,0:T(8,128)(2,1)} %get-tuple-element.73), channel_id=1, source_target_pairs={{0,2},{2,0},{4,6},{6,4},{8,10},{10,8},{12,14},{14,12},{16,18},{18,... | collective-permute-start | bytes 4128776 | tf_op jit(solution)/shard_map/ppermute | solution.py:22
  205.9 58.4 %collective-permute-start.24 = (bf16[4,672,128]{2,1,0:T(8,128)(2,1)}, bf16[4,672,128]{2,1,0:T(8,128)(2,1)}, u32[]{:S(2)}, u32[]{:S(2)}) collective-permute-start(bf16[4,672,128]{2,1,0:T(8,128)(2,1)} %get-tuple-element.65), channel_id=1, source_target_pairs={{0,2},{2,0},{4,6},{6,4},{8,10},{10,8},{12,14},{14,12},{16,18},{18,... | collective-permute-start | bytes 2064392 | tf_op jit(solution)/shard_map/ppermute | solution.py:22
  227.3 52.5 %collective-permute-start.15 = (bf16[672,128]{1,0:T(8,128)(2,1)}, bf16[672,128]{1,0:T(8,128)(2,1)S(1)}, u32[]{:S(2)}, u32[]{:S(2)}) collective-permute-start(bf16[672,128]{1,0:T(8,128)(2,1)} %get-tuple-element.57), channel_id=1, source_target_pairs={{0,24},{2,26},{4,28},{6,30},{8,0},{10,2},{12,4},{14,6},{16,8},{18,... | collective-permute-start | bytes 516104 | tf_op jit(solution)/shard_map/ppermute | solution.py:29
  232.3 52.9 %collective-permute-start.16 = (bf16[672,128]{1,0:T(8,128)(2,1)}, bf16[672,128]{1,0:T(8,128)(2,1)}, u32[]{:S(2)}, u32[]{:S(2)}) collective-permute-start(bf16[672,128]{1,0:T(8,128)(2,1)} %get-tuple-element.58), channel_id=1, source_target_pairs={{0,16},{2,18},{4,20},{6,22},{8,24},{10,26},{12,28},{14,30},{16,0},... | collective-permute-start | bytes 516104 | tf_op jit(solution)/shard_map/ppermute | solution.py:29
  232.4 40.8 %collective-permute-start.10 = (bf16[320,2560]{1,0:T(8,128)(2,1)}, bf16[320,2560]{1,0:T(8,128)(2,1)S(1)}, u32[]{:S(2)}, u32[]{:S(2)}) collective-permute-start(bf16[320,2560]{1,0:T(8,128)(2,1)} %collective-permute-done.9.refs_2_), channel_id=1, source_target_pairs={{0,8},{2,10},{4,12},{6,14},{8,16},{10,18},{12,20},{14,22},{16,24},... | collective-permute-start | bytes 4915208 | tf_op jit(solution)/shard_map/ppermute | solution.py:29
  257.6 29.6 %collective-permute-start.17 = (bf16[672,128]{1,0:T(8,128)(2,1)}, bf16[672,128]{1,0:T(8,128)(2,1)S(1)}, u32[]{:S(2)}, u32[]{:S(2)}) collective-permute-start(bf16[672,128]{1,0:T(8,128)(2,1)} %copy-done.13), channel_id=1, source_target_pairs={{0,8},{2,10},{4,12},{6,14},{8,16},{10,18},{12,20},{14,22},{16,24},... | collective-permute-start | bytes 516104 | tf_op jit(solution)/shard_map/ppermute | solution.py:29
  284.8 111.3 %collective-permute-start.41 = (bf16[640,2560]{1,0:T(8,128)(2,1)S(1)}, bf16[640,2560]{1,0:T(8,128)(2,1)S(1)}, u32[]{:S(2)}, u32[]{:S(2)}) collective-permute-start(bf16[640,2560]{1,0:T(8,128)(2,1)S(1)} %bitcast.59), channel_id=1, source_target_pairs={{0,1},{1,0},{2,3},{3,2},{4,5},{5,4},{6,7},{7,6},{8,9},{9,8},{10,11... | collective-permute-start | bytes 9830408 | tf_op jit(solution)/shard_map/ppermute | solution.py:38
  294.3 55.7 %collective-permute-start.43 = (bf16[8,672,128]{2,1,0:T(8,128)(2,1)S(1)}, bf16[8,672,128]{2,1,0:T(8,128)(2,1)S(1)}, u32[]{:S(2)}, u32[]{:S(2)}) collective-permute-start(bf16[8,672,128]{2,1,0:T(8,128)(2,1)S(1)} %copy-done.25), channel_id=1, source_target_pairs={{0,4},{2,6},{4,0},{6,2},{8,12},{10,14},{12,8},{14,10},{16,20},{18,... | collective-permute-start | bytes 4128776 | tf_op jit(solution)/shard_map/ppermute | solution.py:22
  310.1 36.7 %collective-permute-start.39 = (bf16[1920,128]{1,0:T(8,128)(2,1)S(1)}, bf16[1920,128]{1,0:T(8,128)(2,1)S(1)}, u32[]{:S(2)}, u32[]{:S(2)}) collective-permute-start(bf16[1920,128]{1,0:T(8,128)(2,1)S(1)} %pad_maximum_fusion.11), channel_id=1, source_target_pairs={{0,4},{2,6},{4,0},{6,2},{8,12},{10,14},{12,8},{14,10},{16,20},{18,... | collective-permute-start | bytes 1474568 | tf_op jit(solution)/shard_map/ppermute | solution.py:22
  310.6 36.1 %collective-permute-start.38 = (bf16[1920,128]{1,0:T(8,128)(2,1)S(1)}, bf16[1920,128]{1,0:T(8,128)(2,1)S(1)}, u32[]{:S(2)}, u32[]{:S(2)}) collective-permute-start(bf16[1920,128]{1,0:T(8,128)(2,1)S(1)} %pad_maximum_fusion.11), channel_id=1, source_target_pairs={{0,2},{2,0},{4,6},{6,4},{8,10},{10,8},{12,14},{14,12},{16,18},{18,... | collective-permute-start | bytes 1474568 | tf_op jit(solution)/shard_map/ppermute | solution.py:22
  349.9 46.1 %collective-permute-start.42 = (bf16[1920,512]{1,0:T(8,128)(2,1)S(1)}, bf16[1920,512]{1,0:T(8,128)(2,1)S(1)}, u32[]{:S(2)}, u32[]{:S(2)}) collective-permute-start(bf16[1920,512]{1,0:T(8,128)(2,1)S(1)} %pad_maximum_fusion), channel_id=1, source_target_pairs={{0,1},{1,0},{2,3},{3,2},{4,5},{5,4},{6,7},{7,6},{8,9},{9,8},{10,11... | collective-permute-start | bytes 5898248 | tf_op jit(solution)/shard_map/ppermute | solution.py:38
  (57 other events, 1117.3 us)

commit v4 on v2

--- a/solution.py
+++ b/solution.py
@@ -22,13 +22,6 @@
     return lax.ppermute(value, "req", [(i, i ^ by) for i in range(size)])
 
 
-def send_line(value, by):
-    size = lax.axis_size("req")
-    line = size // PLANE
-    pairs = [(i, ((i // PLANE + by) % line) * PLANE + i % PLANE) for i in range(size)]
-    return lax.ppermute(value, "req", pairs)
-
-
 def group_count(width):
     return 4 if width // HEAD_DIM % 4 == 0 else 1
 
@@ -36,32 +29,6 @@
 def send_tp(value, by):
     size = lax.axis_size("tp")
     return lax.ppermute(value, "tp", [(i, (i + by) % size) for i in range(size)])
-
-
-def place_kernel(spots_ref, *refs):
-    *blocks, out, sems = refs
-    copies = [
-        pltpu.make_async_copy(ref, out.at[spots_ref[i]], sems.at[i]) for i, ref in enumerate(blocks)
-    ]
-    for copy in copies:
-        copy.start()
-    for copy in copies:
-        copy.wait()
-
-
-def place_blocks(spots, blocks):
-    return pl.pallas_call(
-        place_kernel,
-        grid_spec=pltpu.PrefetchScalarGridSpec(
-            num_scalar_prefetch=1,
-            grid=(1,),
-            in_specs=[pl.BlockSpec(memory_space=pl.ANY)] * len(blocks),
-            out_specs=pl.BlockSpec(memory_space=pl.ANY),
-            scratch_shapes=[pltpu.SemaphoreType.DMA((len(blocks),))],
-        ),
-        out_shape=jax.ShapeDtypeStruct((len(blocks),) + blocks[0].shape, blocks[0].dtype),
-        name="place_weights",
-    )(spots, *blocks)
 
 
 def turn_kernel(q_ref, k_ref, scale_ref, gain_q_ref, gain_k_ref, cos_ref, sin_ref, _, q_out, k_out):
@@ -107,28 +74,19 @@
 def attend_kernel(
     table_ref,
     slot_ref,
-    q_low_ref,
-    q_high_ref,
-    keys_ref,
-    values_ref,
-    near_keys_ref,
-    near_values_ref,
-    near_starts_ref,
-    keep_ref,
-    send_ref,
-    q_all,
-    acc,
-    peak,
-    total,
-    sems,
+    q_slot_ref,
+    *refs,
 ):
+    *q_refs, keys_ref, values_ref, near_keys_ref, near_values_ref, near_starts_ref, _, _ = refs[:-7]
+    keep_ref, send_ref, q_all, acc, peak, total, sems = refs[-7:]
     step = pl.program_id(0)
-    half, rows, width = q_low_ref.shape
+    half, _, rows = keep_ref.shape
+    width = acc.shape[1]
     blocks = 2 * half
     heads = width // HEAD_DIM
     lane = lax.broadcasted_iota(jnp.int32, (1, rows), 1)
 
-    def update(slots, keys_ref, values_ref, masks, allowed):
+    def update(slots, q_slots, keys_ref, values_ref, masks, allowed):
         ones = jnp.ones((PIECE, keys_ref.shape[0]), jnp.bfloat16)
         mask = jnp.concatenate(masks, axis=1)
         old_peak = jnp.concatenate([peak[s] for s in slots], axis=1)
@@ -137,7 +95,7 @@
 
         def score(h):
             cols = slice(h * HEAD_DIM, (h + 1) * HEAD_DIM)
-            q = jnp.concatenate([q_all[s, :, cols] for s in slots], axis=0)
+            q = jnp.concatenate([q_all[s, :, cols] for s in q_slots], axis=0)
             scores[h] = lax.dot_general(
                 keys_ref[:, cols], q, (((1,), (1,)), ((), ())), preferred_element_type=jnp.float32
             )
@@ -175,16 +133,19 @@
 
     @pl.when(step == 0)
     def _():
-        low = pltpu.make_async_copy(q_low_ref, q_all.at[pl.ds(0, half)], sems.at[0])
-        high = pltpu.make_async_copy(q_high_ref, q_all.at[pl.ds(half, half)], sems.at[1])
-        low.start()
-        high.start()
+        share = blocks // len(q_refs)
+        copies = [
+            pltpu.make_async_copy(ref, q_all.at[pl.ds(i * share, share)], sems.at[i])
+            for i, ref in enumerate(q_refs)
+        ]
+        for copy in copies:
+            copy.start()
         q_all[blocks] = jnp.zeros((rows, width), jnp.bfloat16)
         acc[...] = jnp.zeros_like(acc)
         peak[...] = jnp.full(peak.shape, LOW_SCORE, jnp.float32)
         total[...] = jnp.zeros_like(total)
-        low.wait()
-        high.wait()
+        for copy in copies:
+            copy.wait()
         first = slot_ref[blocks + 1]
 
         def near_pair(j, carry):
@@ -194,9 +155,10 @@
             key = first * rows + lax.broadcasted_iota(jnp.int32, (rows, 2 * rows), 0)
             allowed = (key >= begin) & (key <= row)
             some = begin < (first + 1) * rows
-            slots = [slot_ref[jnp.minimum(low + i, blocks)] for i in range(2)]
+            at = [jnp.minimum(low + i, blocks) for i in range(2)]
+            slots, q_slots = [slot_ref[i] for i in at], [q_slot_ref[i] for i in at]
             masks = [some[:, :rows], some[:, rows:]]
-            update(slots, near_keys_ref, near_values_ref, masks, allowed)
+            update(slots, q_slots, near_keys_ref, near_values_ref, masks, allowed)
             return carry
 
         lax.fori_loop(0, 2, near_pair, 0)
@@ -213,7 +175,8 @@
             row = low * rows + lane
             masks = [(r >= begin) & (r < end) for r in (row, row + rows)]
             slots = [slot_ref[low], slot_ref[low + 1]]
-            update(slots, keys_ref.at[0], values_ref.at[0], masks, None)
+            q_slots = [q_slot_ref[low], q_slot_ref[low + 1]]
+            update(slots, q_slots, keys_ref.at[0], values_ref.at[0], masks, None)
             return carry
 
         lax.fori_loop(0, count, pair, 0)
@@ -251,8 +214,11 @@
     return stacked[:8] + (stacked[8:16] + stacked[16:24])
 
 
-def attend(group, table, slots, q_low, q_high, cache_keys, cache_values, near_keys, near_values, near_starts):
-    half, rows, width = q_low.shape
+def attend(
+    group, table, slots, q_slots, q_parts, cache_keys, cache_values, near_keys, near_values, near_starts, after
+):
+    rows, width = near_keys.shape
+    half = sum(part.shape[0] for part in q_parts) // 2
     pages, page_len, _ = cache_keys.shape
     heads = width // HEAD_DIM
     blocks = 2 * half
@@ -265,16 +231,17 @@
     return pl.pallas_call(
         attend_kernel,
         grid_spec=pltpu.PrefetchScalarGridSpec(
-            num_scalar_prefetch=2,
+            num_scalar_prefetch=3,
             grid=(pages + 1,),
-            in_specs=[
-                pl.BlockSpec(memory_space=pl.ANY),
-                pl.BlockSpec(memory_space=pl.ANY),
+            in_specs=[pl.BlockSpec(memory_space=pl.ANY)] * len(q_parts)
+            + [
                 page_spec,
                 page_spec,
                 own_spec,
                 near_spec,
                 whole((2, 1, 2 * rows)),
+                pl.BlockSpec(memory_space=pl.ANY),
+                pl.BlockSpec(memory_space=pl.ANY),
             ],
             out_specs=[whole(out.shape), whole(out.shape)],
             scratch_shapes=[
@@ -290,12 +257,12 @@
             dimension_semantics=("arbitrary",), vmem_limit_bytes=56 * 2**20
         ),
         cost_estimate=pl.CostEstimate(
-            flops=pages * heads * 256 * page_len * HEAD_DIM * 8,
+            flops=pages * heads * 256 * page_len * HEAD_DIM * 40,
             bytes_accessed=pages * page_len * width * 4,
             transcendentals=pages * heads * 256 * page_len,
         ),
         name="cache_attend",
-    )(table, slots, q_low, q_high, cache_keys, cache_values, near_keys, near_values, near_starts)
+    )(table, slots, q_slots, *q_parts, cache_keys, cache_values, near_keys, near_values, near_starts, *after)
 
 
 def merged(refs, heads):
@@ -314,14 +281,14 @@
     return block, top + jnp.log2(total)
 
 
-def combine_kernel(mine_low, mine_high, got_low, got_high, keep_ref, send_ref):
+def combine_kernel(mine_low, mine_high, got_low, got_high, _, keep_ref, send_ref):
     heads = (mine_low.shape[1] - LEVEL_ROWS) // HEAD_DIM
     for mine, got, out in ((mine_low, got_low, keep_ref), (mine_high, got_high, send_ref)):
         block, levels = merged([mine.at[0], got.at[0]], heads)
         write_block(out.at[0], block, jnp.ones_like(levels), levels, heads)
 
 
-def combine(mine, got):
+def combine(mine, got, after):
     count, depth, rows = mine.shape
     half = count // 2
     low = pl.BlockSpec((1, depth, rows), lambda i: (i, 0, 0))
@@ -330,7 +297,7 @@
     return pl.pallas_call(
         combine_kernel,
         grid=(half,),
-        in_specs=[low, high, low, high],
+        in_specs=[low, high, low, high, pl.BlockSpec(memory_space=pl.ANY)],
         out_specs=[low, low],
         out_shape=[out, out],
         compiler_params=pltpu.CompilerParams(vmem_limit_bytes=24 * 2**20),
@@ -338,21 +305,23 @@
             flops=count * depth * rows * 4, bytes_accessed=count * depth * rows * 6, transcendentals=0
         ),
         name="combine_pairs",
-    )(mine, mine, got, got)
+    )(mine, mine, got, got, after)
 
 
 def last_kernel(*refs):
     out_ref = refs[-1]
     heads = out_ref.shape[0] // HEAD_DIM
-    block, _ = merged(refs[:-1], heads)
+    block, _ = merged(refs[:-2], heads)
     for h in range(heads):
         out_ref[h * HEAD_DIM : (h + 1) * HEAD_DIM, :] = block(h).astype(jnp.bfloat16)
 
 
-def combine_last(parts):
+def combine_last(parts, after):
     depth, rows = parts[0].shape
+    whole = pl.BlockSpec(memory_space=pltpu.VMEM)
     return pl.pallas_call(
         last_kernel,
+        in_specs=[whole] * len(parts) + [pl.BlockSpec(memory_space=pl.ANY)],
         out_shape=jax.ShapeDtypeStruct((depth - LEVEL_ROWS, rows), jnp.bfloat16),
         compiler_params=pltpu.CompilerParams(vmem_limit_bytes=24 * 2**20),
         cost_estimate=pl.CostEstimate(
@@ -361,7 +330,7 @@
             transcendentals=0,
         ),
         name="combine_last",
-    )(*parts)
+    )(*parts, after)
 
 
 def local(
@@ -387,7 +356,6 @@
     line = size // PLANE
     device = lax.axis_index("req")
     spot = device % PLANE
-    place = device // PLANE
     slot_count, page_len, _ = cache_keys.shape
     request_count = cache_pages.shape[0]
     total_pages = page_table.shape[0]
@@ -444,62 +412,101 @@
     near_starts = jnp.where(near_segs < 0, near_rows + size * tok_dev, near_starts)
     near_starts = near_starts.reshape(2, 1, 2 * tok_dev)
 
-    block = jnp.arange(size, dtype=jnp.int32)
-    back = (place - block // PLANE) % line
-    across = (block % PLANE) ^ spot
-
-    def order_of(group):
-        return (2, 1) if group % 2 == 0 else (1, 2)
+    apart = jnp.arange(size, dtype=jnp.int32) ^ device
+    beyond = jnp.stack([jnp.int32(size), device])
+    natural = jnp.concatenate([jnp.arange(size, dtype=jnp.int32), beyond])
+    masks = [1 << i for i in range((size - 1).bit_length())]
+    columns = out_weight.shape[1]
+    blocks_each = line // tp_size
+    tp_device = lax.axis_index("tp")
 
     groups = group_count(local_width)
-    near, near_keys = [], []
+    orders = [masks if group in (0, 3) else [2, 1] + masks[2:] for group in range(groups)]
+    slots = []
+    for order in orders:
+        slot = sum(jnp.where((apart & m) > 0, size >> (i + 1), 0) for i, m in enumerate(order))
+        slots.append(jnp.concatenate([slot, beyond]))
+    gathered, near_keys = [], []
     after = scales
     for group in range(groups):
         part, key_part = turn(
             group, queries, new_keys, scales, query_gain, key_gain, cosine, sine, after
         )
-        got = [part[None]] + [send_line(part, k)[None] for k in range(1, line)]
-        near.append(jnp.concatenate(got, axis=0))
         near_keys.append(key_part)
-        after = near[-1]
-
-    weight, _ = lax.optimization_barrier((out_weight.T, after))
-    columns = weight.shape[0]
-    blocks_each = line // tp_size
-    tp_device = lax.axis_index("tp")
-    from_place = (place - jnp.arange(line, dtype=jnp.int32)) % line
-    weight_spots = ((from_place // blocks_each - tp_device) % tp_size) * blocks_each
-    weight_spots = weight_spots + from_place % blocks_each
-    weights = place_blocks(weight_spots, [weight] + [send_line(weight, k) for k in range(1, line)])
-    weights = weights.reshape(tp_size, blocks_each * columns, local_width)
-    weights = [weights[0]] + [send_tp(weights[k], k) for k in range(1, tp_size)]
-
-    attended = []
-    for group in range(groups):
-        order = order_of(group)
-        low = jnp.concatenate([near[group], send_xor(near[group], order[0])], axis=0)
-        high = send_xor(low, order[1])
-        slot = jnp.where((across & order[1]) > 0, 2 * line, 0)
-        slot = slot + jnp.where((across & order[0]) > 0, line, 0) + back
-        slots = jnp.concatenate([slot, jnp.stack([jnp.int32(size), device])])
-        keep, send = attend(
-            group, table, slots, low, high, cache_keys, cache_values, near_keys[group], new_values, near_starts
-        )
-        keep, send = combine(keep, send_xor(send, order[1]))
-        parts = combine_line(keep, send_xor(send, order[0]))
-        attended.append(combine_last([parts[0]] + [send_line(parts[k], -k) for k in range(1, line)]))
+        after = along_line if group == 2 else key_part
+        if group % 2 == 0:
+            gathered.append([lax.all_gather(part[None], "req", axis=0, tiled=True)])
+            continue
+        held, stages = part[None], []
+        for m in orders[group][:0:-1]:
+            held = lax.optimization_barrier(jnp.concatenate([held, send_xor(held, m)], axis=0))
+            stages.append(held)
+            if held.shape[0] == line and group == 1:
+                along_line = held
+        gathered.append([held, send_xor(held, orders[group][0])])
+    weight, _ = lax.optimization_barrier((out_weight.T, near_keys[-1]))
+    lines = [[z * PLANE + p for z in range(line)] for p in range(PLANE)]
+    weight = lax.all_gather(weight, "req", axis=0, tiled=True, axis_index_groups=lines)
+
+    weight = weight.reshape(tp_size, blocks_each * columns, local_width)
+    weights = []
+    for k in range(tp_size):
+        part = lax.dynamic_index_in_dim(weight, (tp_device + k) % tp_size, 0, keepdims=False)
+        weights.append(part if k == 0 else send_tp(part, k))
+
+    waits = [near_starts] * 4
+    if groups > 1:
+        waits[:2] = stages[-2:]
+    if groups > 1:
+        turns = ((0, "a"), (1, "a"), (0, "c"), (3, "a"), (0, "c"), (1, "c"), (2, "a"))
+        turns += ((3, "c"), (0, "c"), (1, "c"), (2, "c"), (0, "l"), (3, "c"), (1, "c"), (2, "c"))
+        turns += ((1, "l"), (3, "c"), (2, "c"), (3, "l"), (2, "l"))
+    else:
+        turns = ((0, "a"),) + ((0, "c"),) * (len(masks) - 1) + ((0, "l"),)
+    attended, state, left = [None] * groups, [None] * groups, [list(order) for order in orders]
+    before = near_starts
+    for group, step in turns:
+        if step == "a":
+            state[group] = attend(
+                group, table, slots[group], natural if group % 2 == 0 else slots[group], gathered[group],
+                cache_keys, cache_values, near_keys[group], new_values, near_starts, (before, waits[group]),
+            )
+            before = state[group][0]
+        elif step == "c":
+            keep, send = state[group]
+            state[group] = combine(keep, send_xor(send, left[group].pop(0)), before)
+            before = latest = state[group][0]
+        else:
+            if group == 3:
+                before = weights[-1]
+            keep, send = state[group]
+            attended[group] = combine_last([keep[0], send_xor(send, left[group].pop(0))[0]], before)
+            before = attended[group]
+    if groups > 1:
+        attended = [attended[group] for group in (0, 1, 3, 2)]
+        attended[0], _ = lax.optimization_barrier((attended[0], latest))
 
     projected = 0.0
-    depth = 0
-    for some in ([attended[:-1], attended[-1:]] if groups > 1 else [attended]):
+    share = local_width // groups
+    if groups > 1:
+        weight_sets = [[(0, 2 * share), (3 * share, 4 * share)], [(2 * share, 3 * share)]]
+    else:
+        weight_sets = [[(0, local_width)]]
+    for some, spans in zip([attended[:-1], attended[-1:]] if groups > 1 else [attended], weight_sets):
         some = jnp.concatenate(some, axis=0)
-        spread = jnp.concatenate([some] + [send_xor(some, k) for k in range(1, PLANE)], axis=1)
+        got = [send_xor(some, k) for k in range(1, PLANE)]
+        *got, _ = lax.optimization_barrier((*got, attended[-1]))
+        spread = jnp.concatenate([some] + got, axis=1)
         for k in range(tp_size):
             part = spread if k == 0 else send_tp(spread, k)
-            projected = projected + jnp.dot(
-                weights[k][:, depth : depth + some.shape[0]], part, preferred_element_type=jnp.float32
-            )
-        depth += some.shape[0]
+            at = 0
+            for low, high in spans:
+                projected = projected + jnp.dot(
+                    weights[k][:, low:high],
+                    part[at : at + high - low],
+                    preferred_element_type=jnp.float32,
+                )
+                at += high - low
     sent = projected.astype(jnp.bfloat16)
     mine = [projected[:, :tok_dev]] + [
         send_xor(sent[:, k * tok_dev : (k + 1) * tok_dev], k).astype(jnp.float32) for k in range(1, PLANE)
@@ -513,27 +520,6 @@
     return (hidden_in.astype(jnp.float32) + gate_rows * (projected + out_bias[None, :])).astype(
         jnp.bfloat16
     )
-
-
-def pair_kernel(mine, got, *outs):
-    heads = (mine.shape[1] - LEVEL_ROWS) // HEAD_DIM
-    for i, out in enumerate(outs):
-        block, levels = merged([mine.at[i], got.at[i]], heads)
-        write_block(out, block, jnp.ones_like(levels), levels, heads)
-
-
-def combine_line(mine, got):
-    count, depth, rows = mine.shape
-    out = jax.ShapeDtypeStruct((depth, rows), jnp.bfloat16)
-    return pl.pallas_call(
-        pair_kernel,
-        out_shape=[out] * count,
-        compiler_params=pltpu.CompilerParams(vmem_limit_bytes=32 * 2**20),
-        cost_estimate=pl.CostEstimate(
-            flops=count * depth * rows * 4, bytes_accessed=count * depth * rows * 6, transcendentals=0
-        ),
-        name="combine_line",
-    )(mine, got)
 
 
 def solution(mesh):

time: 611 us -> 449 us (0.73)
  Pallas kernels: 298 us -> 127 us
  starting transfers between devices: 70.2 us -> 40 us
  waiting for transfers between devices: 202 us -> 224 us
  between operations: 0.84 us -> 13.8 us
    pallas_call x9 -> x4, Pallas kernels: 203 us -> 0.32 us  [combine_last(): pl.pallas_call(last_kernel, in_specs=[whole] * len(parts) + [pl.BlockSpec...]
    ppermute x27 -> x0, waiting for transfers between devices: 119 us -> none  [send_line(): return lax.ppermute(value, 'req', pairs)]
    ppermute x25 -> x33, waiting for transfers between devices: 82.1 us -> 158 us  [send_xor(): return lax.ppermute(value, 'req', [(i, i ^ by) for i in range(size)])]
    all_gather x0 -> x3, waiting for transfers between devices: none -> 66 us  [the longest x2 59.9 us: local(): gathered.append([lax.all_gather(part[None], 'req', axis=0, tiled=True)])]
    ppermute x27 -> x0, starting transfers between devices: 32.7 us -> none  [send_line(): return lax.ppermute(value, 'req', pairs)]
    pallas_call x4, Pallas kernels: 89.3 us -> 120 us  [attend(): pl.pallas_call(attend_kernel, grid_spec=pltpu.PrefetchScalarGridSpec(num_...]
    squeeze x0 -> x1, local copies, waits for them, and re-layouts: none -> 6.13 us  [local(): lax.dynamic_index_in_dim(weight, (tp_device + k) % tp_size, 0, keepdims=F...]
    ppermute x25 -> x33, starting transfers between devices: 37.3 us -> 39.7 us  [send_xor(): return lax.ppermute(value, 'req', [(i, i ^ by) for i in range(size)])]
  transfers between devices with their start and end apart: 55 -> 39, of which waited for: 27 -> 27; matrix products, arithmetic and copies ran while one was open for 3% -> 4% of each run, Pallas kernels for 49% -> 28%
where the time goes in v4:
time: 449 us; the launch traced here: 450 us
  waiting for transfers between devices  224 us (50%)
  Pallas kernels  127 us (28%)
  starting transfers between devices  40 us (9%)
  local copies, waits for them, and re-layouts  17.6 us (4%)
  between operations  13.8 us (3%)
  other arithmetic  12.5 us (3%)
  matrix products  10.2 us (2%)
    ppermute x33, waiting for transfers between devices, send_xor(): return lax.ppermute(value, 'req', [(i, i ^ by) for i in range(size)])  158 us
    pallas_call x4, Pallas kernels, attend(): pl.pallas_call(attend_kernel, grid_spec=pltpu.PrefetchScalarGridSpec(num_...  120 us
    all_gather x2, waiting for transfers between devices, local(): gathered.append([lax.all_gather(part[None], 'req', axis=0, tiled=True)])  59.9 us
    ppermute x33, starting transfers between devices, send_xor(): return lax.ppermute(value, 'req', [(i, i ^ by) for i in range(size)])  39.7 us
    unnamed x60, local copies, waits for them, and re-layouts  9.18 us
  transfers between devices with their start and end apart: 39, of which 27 were waited for; matrix products, arithmetic and copies ran while one was open for 4% of the time, Pallas kernels for 28%

profile of v4, /device:TPU:0, one launch (start us, length us, event | category | flops | bytes accessed | tf_op | source)
XLA Modules:
  0.0 449.8 jit_solution(7805550032875397514)
XLA Ops:
  11.1 3.9 psum.7
  20.8 8.2 %collective-permute-done = bf16[1,128,640]{2,1,0:T(8,128)(2,1)S(1)} collective-permute-done((bf16[1,128,640]{2,1,0:T(8,128)(2,1)S(1)}, bf16[1,128,640]{2,1,0:T(8,128)(2,1)S(1)}, u32[]{:S(2)}, u32[]{:S(2)}) %collective-permute-start) | collective-permute-done | bytes 163872 | tf_op jit(solution)/shard_map/ppermute | solution.py:22
  29.9 11.6 %collective-permute-done.1 = bf16[2,128,640]{2,1,0:T(8,128)(2,1)S(1)} collective-permute-done((bf16[2,128,640]{2,1,0:T(8,128)(2,1)S(1)}, bf16[2,128,640]{2,1,0:T(8,128)(2,1)S(1)}, u32[]{:S(2)}, u32[]{:S(2)}) %collective-permute-start.1) | collective-permute-done | bytes 327712 | tf_op jit(solution)/shard_map/ppermute | solution.py:22
  47.4 13.8 %collective-permute-done.2 = bf16[1,128,640]{2,1,0:T(8,128)(2,1)S(1)} collective-permute-done((bf16[1,128,640]{2,1,0:T(8,128)(2,1)S(1)}, bf16[1,128,640]{2,1,0:T(8,128)(2,1)S(1)}, u32[]{:S(2)}, u32[]{:S(2)}) %collective-permute-start.2) | collective-permute-done | bytes 163872 | tf_op jit(solution)/shard_map/ppermute | solution.py:22
  62.9 6.4 %collective-permute-done.3 = bf16[2,128,640]{2,1,0:T(8,128)(2,1)S(1)} collective-permute-done((bf16[2,128,640]{2,1,0:T(8,128)(2,1)S(1)}, bf16[2,128,640]{2,1,0:T(8,128)(2,1)S(1)}, u32[]{:S(2)}, u32[]{:S(2)}) %collective-permute-start.3) | collective-permute-done | bytes 327712 | tf_op jit(solution)/shard_map/ppermute | solution.py:22
  71.1 15.6 %collective-permute-done.5 = bf16[4,128,640]{2,1,0:T(8,128)(2,1)S(1)} collective-permute-done((bf16[4,128,640]{2,1,0:T(8,128)(2,1)S(1)}, bf16[4,128,640]{2,1,0:T(8,128)(2,1)S(1)}, u32[]{:S(2)}, u32[]{:S(2)}) %collective-permute-start.5) | collective-permute-done | bytes 655392 | tf_op jit(solution)/shard_map/ppermute | solution.py:22
  88.6 5.9 %collective-permute-done.7 = bf16[4,128,640]{2,1,0:T(8,128)(2,1)S(1)} collective-permute-done((bf16[4,128,640]{2,1,0:T(8,128)(2,1)S(1)}, bf16[4,128,640]{2,1,0:T(8,128)(2,1)S(1)}, u32[]{:S(2)}, u32[]{:S(2)}) %collective-permute-start.7) | collective-permute-done | bytes 655392 | tf_op jit(solution)/shard_map/ppermute | solution.py:22
  97.0 30.0 %cache_attend.4 = (bf16[8,672,128]{2,1,0:T(8,128)(2,1)}, bf16[8,672,128]{2,1,0:T(8,128)(2,1)}) custom-call(s32[64]{0:T(128)} %reshape.371.table_ref, s32[18]{0:T(128)} %fusion.35.slot_ref.q_slot_ref, s32[18]{0:T(128)} %fusion.36.q_slot_ref, bf16[16,128,640]{2,1,0:T(8,128)(2,1)} %bitcast.80, bf16[16,256,2560]{2,1,0:T(8,128)(2,1)} %refs_1_.3, ...), custom_call_target="tpu_custom_call" | custom-call | flops 26843545600 | bytes 10485760 | tf_op jit(solution)/shard_map/cache_attend/pallas_call | solution.py:231
  130.5 29.9 %cache_attend.5 = (bf16[8,672,128]{2,1,0:T(8,128)(2,1)}, bf16[8,672,128]{2,1,0:T(8,128)(2,1)}) custom-call(s32[64]{0:T(128)} %reshape.371.table_ref, s32[18]{0:T(128)} %fusion.37.slot_ref.q_slot_ref, s32[18]{0:T(128)} %fusion.37.slot_ref.q_slot_ref, bf16[8,128,640]{2,1,0:T(8,128)(2,1)} %pad_maximum_fusion.1.refs_0_, bf16[8,128,640]{2,1,0:T(8,128)(2,1)} %copy-done.29, ...), custom_call_target="tpu_custom_call" | custom-call | flops 26843545600 | bytes 10485760 | tf_op jit(solution)/shard_map/cache_attend/pallas_call | solution.py:231
  165.4 29.9 %cache_attend.6 = (bf16[8,672,128]{2,1,0:T(8,128)(2,1)}, bf16[8,672,128]{2,1,0:T(8,128)(2,1)}) custom-call(s32[64]{0:T(128)} %reshape.371.table_ref, s32[18]{0:T(128)} %fusion.35.slot_ref.q_slot_ref, s32[18]{0:T(128)} %fusion.35.slot_ref.q_slot_ref, bf16[8,128,640]{2,1,0:T(8,128)(2,1)} %copy-done.20, bf16[8,128,640]{2,1,0:T(8,128)(2,1)} %collective-permute-done.9.refs_1_, ...), custom_call_target="tpu_custom_call" | custom-call | flops 26843545600 | bytes 10485760 | tf_op jit(solution)/shard_map/cache_attend/pallas_call | solution.py:231
  197.0 9.8 %collective-permute-done.8.got_low.got_high = bf16[4,672,128]{2,1,0:T(8,128)(2,1)S(1)} collective-permute-done((bf16[4,672,128]{2,1,0:T(8,128)(2,1)S(1)}, bf16[4,672,128]{2,1,0:T(8,128)(2,1)S(1)}, u32[]{:S(2)}, u32[]{:S(2)}) %collective-permute-start.8) | collective-permute-done | bytes 688160 | tf_op jit(solution)/shard_map/ppermute | solution.py:22
  211.1 6.1 %all-gather.6.cloned.1.call-done = bf16[1280,2560]{1,0:T(8,128)(2,1)} async-done(((bf16[320,2560]{1,0:T(8,128)(2,1)}), bf16[1280,2560]{1,0:T(8,128)(2,1)}) %all-gather.6.cloned.1.call-update) | async-done | bytes 6553616 | tf_op jit(solution)/shard_map/all_gather | solution.py:449
  217.2 6.1 %dynamic-slice_bitcast_fusion = (bf16[640,2560]{1,0:T(8,128)(2,1)}, bf16[640,2560]{1,0:T(8,128)(2,1)}) fusion(bf16[2,640,2560]{2,1,0:T(8,128)(2,1)} %bitcast.60, s32[]{:T(128)S(6)} %select_n.269, s32[]{:T(128)S(6)} %select_n.252), kind=kLoop, calls=%fused_computation.3 | loop fusion | bytes 13107208 | tf_op jit(solution)/shard_map/jit(dynamic_index_in_dim)/squeeze | solution.py:454
  223.4 58.8 %all-gather.10.cloned.1.call-done = bf16[2048,640]{1,0:T(8,128)(2,1)} async-done(((bf16[128,640]{1,0:T(8,128)(2,1)}), bf16[2048,640]{1,0:T(8,128)(2,1)}) %all-gather.10.cloned.1.call-update) | async-done | bytes 2621456 | tf_op jit(solution)/shard_map/all_gather | solution.py:438
  282.2 29.9 %cache_attend.7 = (bf16[8,672,128]{2,1,0:T(8,128)(2,1)}, bf16[8,672,128]{2,1,0:T(8,128)(2,1)}) custom-call(s32[64]{0:T(128)} %reshape.371.table_ref, s32[18]{0:T(128)} %fusion.37.slot_ref.q_slot_ref, s32[18]{0:T(128)} %fusion.36.q_slot_ref, bf16[16,128,640]{2,1,0:T(8,128)(2,1)} %bitcast.79, bf16[16,256,2560]{2,1,0:T(8,128)(2,1)} %refs_1_.3, ...), custom_call_target="tpu_custom_call" | custom-call | flops 26843545600 | bytes 10485760 | tf_op jit(solution)/shard_map/cache_attend/pallas_call | solution.py:231
  318.5 5.5 %collective-permute-done.10.got_low.got_high = bf16[2,672,128]{2,1,0:T(8,128)(2,1)S(1)} collective-permute-done((bf16[2,672,128]{2,1,0:T(8,128)(2,1)S(1)}, bf16[2,672,128]{2,1,0:T(8,128)(2,1)S(1)}, u32[]{:S(2)}, u32[]{:S(2)}) %collective-permute-start.10) | collective-permute-done | bytes 344096 | tf_op jit(solution)/shard_map/ppermute | solution.py:22
  324.1 5.7 %collective-permute-done.15.got_low.got_high = bf16[4,672,128]{2,1,0:T(8,128)(2,1)S(1)} collective-permute-done((bf16[4,672,128]{2,1,0:T(8,128)(2,1)S(1)}, bf16[4,672,128]{2,1,0:T(8,128)(2,1)S(1)}, u32[]{:S(2)}, u32[]{:S(2)}) %collective-permute-start.15) | collective-permute-done | bytes 688160 | tf_op jit(solution)/shard_map/ppermute | solution.py:22
  330.2 15.2 %collective-permute-done.14.got_low.got_high = bf16[8,672,128]{2,1,0:T(8,128)(2,1)S(1)} collective-permute-done((bf16[8,672,128]{2,1,0:T(8,128)(2,1)}, bf16[8,672,128]{2,1,0:T(8,128)(2,1)S(1)}, u32[]{:S(2)}, u32[]{:S(2)}) %collective-permute-start.14) | collective-permute-done | bytes 1376288 | tf_op jit(solution)/shard_map/ppermute | solution.py:22
  348.5 7.5 %collective-permute-done.13 = bf16[1,672,128]{2,1,0:T(8,128)(2,1)S(1)} collective-permute-done((bf16[1,672,128]{2,1,0:T(8,128)(2,1)S(1)}, bf16[1,672,128]{2,1,0:T(8,128)(2,1)S(1)}, u32[]{:S(2)}, u32[]{:S(2)}) %collective-permute-start.13) | collective-permute-done | bytes 172064 | tf_op jit(solution)/shard_map/ppermute | solution.py:22
  362.6 9.5 %collective-permute-done.21 = bf16[1,672,128]{2,1,0:T(8,128)(2,1)S(1)} collective-permute-done((bf16[1,672,128]{2,1,0:T(8,128)(2,1)S(1)}, bf16[1,672,128]{2,1,0:T(8,128)(2,1)S(1)}, u32[]{:S(2)}, u32[]{:S(2)}) %collective-permute-start.21) | collective-permute-done | bytes 172064 | tf_op jit(solution)/shard_map/ppermute | solution.py:22
  375.8 5.7 %collective-permute-done.19.got_low.got_high = bf16[2,672,128]{2,1,0:T(8,128)(2,1)S(1)} collective-permute-done((bf16[2,672,128]{2,1,0:T(8,128)(2,1)S(1)}, bf16[2,672,128]{2,1,0:T(8,128)(2,1)S(1)}, u32[]{:S(2)}, u32[]{:S(2)}) %collective-permute-start.19) | collective-permute-done | bytes 344096 | tf_op jit(solution)/shard_map/ppermute | solution.py:22
  387.4 6.9 %collective-permute-done.27 = bf16[1,672,128]{2,1,0:T(8,128)(2,1)S(1)} collective-permute-done((bf16[1,672,128]{2,1,0:T(8,128)(2,1)S(1)}, bf16[1,672,128]{2,1,0:T(8,128)(2,1)S(1)}, u32[]{:S(2)}, u32[]{:S(2)}) %collective-permute-start.27) | collective-permute-done | bytes 172064 | tf_op jit(solution)/shard_map/ppermute | solution.py:22
  397.0 9.5 %collective-permute-done.25 = bf16[1920,128]{1,0:T(8,128)(2,1)S(1)} collective-permute-done((bf16[1920,128]{1,0:T(8,128)(2,1)S(1)}, bf16[1920,128]{1,0:T(8,128)(2,1)S(1)}, u32[]{:S(2)}, u32[]{:S(2)}) %collective-permute-start.25) | collective-permute-done | bytes 491552 | tf_op jit(solution)/shard_map/ppermute | solution.py:22
  432.8 4.4 collective-permute-done.33
  (198 shorter events, 100.3 us)
Async XLA Ops:
  6.6 90.4 %all-gather.8.cloned.1.call-start = ((), (), s32[]{:S(2)}) async-start(), calls=%async_computation.1 | async-start | bytes 2785280 | tf_op jit(solution)/shard_map/all_gather | solution.py:438
  16.5 200.7 %all-gather.6.cloned.1.call-start = ((), (), s32[]{:S(2)}) async-start(), calls=%async_computation | async-start | bytes 8192000 | tf_op jit(solution)/shard_map/all_gather | solution.py:449
  29.1 12.4 %collective-permute-start.1 = (bf16[2,128,640]{2,1,0:T(8,128)(2,1)S(1)}, bf16[2,128,640]{2,1,0:T(8,128)(2,1)S(1)}, u32[]{:S(2)}, u32[]{:S(2)}) collective-permute-start(bf16[2,128,640]{2,1,0:T(8,128)(2,1)S(1)} %pad_maximum_fusion.8), channel_id=1, source_target_pairs={{0,8},{2,10},{4,12},{6,14},{8,0},{10,2},{12,4},{14,6},{16,24},{18,... | collective-permute-start | bytes 983048 | tf_op jit(solution)/shard_map/ppermute | solution.py:22
  42.7 239.5 %all-gather.10.cloned.1.call-start = ((), (), s32[]{:S(2)}) async-start(), calls=%async_computation.2 | async-start | bytes 2785280 | tf_op jit(solution)/shard_map/all_gather | solution.py:438
  44.5 16.6 %collective-permute-start.2 = (bf16[1,128,640]{2,1,0:T(8,128)(2,1)S(1)}, bf16[1,128,640]{2,1,0:T(8,128)(2,1)S(1)}, u32[]{:S(2)}, u32[]{:S(2)}) collective-permute-start(bf16[1,128,640]{2,1,0:T(8,128)(2,1)S(1)} %bitcast.56), channel_id=1, source_target_pairs={{0,16},{2,18},{4,20},{6,22},{8,24},{10,26},{12,28},{14,30},{16,0},... | collective-permute-start | bytes 491528 | tf_op jit(solution)/shard_map/ppermute | solution.py:22
  62.5 24.2 %collective-permute-start.5 = (bf16[4,128,640]{2,1,0:T(8,128)(2,1)S(1)}, bf16[4,128,640]{2,1,0:T(8,128)(2,1)S(1)}, u32[]{:S(2)}, u32[]{:S(2)}) collective-permute-start(bf16[4,128,640]{2,1,0:T(8,128)(2,1)S(1)} %pad_maximum_fusion.4._), channel_id=1, source_target_pairs={{0,2},{2,0},{4,6},{6,4},{8,10},{10,8},{12,14},{14,12},{16,18},{18,... | collective-permute-start | bytes 1966088 | tf_op jit(solution)/shard_map/ppermute | solution.py:22
  69.4 25.2 %collective-permute-start.7 = (bf16[4,128,640]{2,1,0:T(8,128)(2,1)S(1)}, bf16[4,128,640]{2,1,0:T(8,128)(2,1)S(1)}, u32[]{:S(2)}, u32[]{:S(2)}) collective-permute-start(bf16[4,128,640]{2,1,0:T(8,128)(2,1)S(1)} %pad_maximum_fusion.5.refs_7_), channel_id=1, source_target_pairs={{0,4},{2,6},{4,0},{6,2},{8,12},{10,14},{12,8},{14,10},{16,20},{18,... | collective-permute-start | bytes 1966088 | tf_op jit(solution)/shard_map/ppermute | solution.py:22
  87.9 41.5 %collective-permute-start.6 = (bf16[8,128,640]{2,1,0:T(8,128)(2,1)}, bf16[8,128,640]{2,1,0:T(8,128)(2,1)S(1)}, u32[]{:S(2)}, u32[]{:S(2)}) collective-permute-start(bf16[8,128,640]{2,1,0:T(8,128)(2,1)} %pad_maximum_fusion.1.refs_0_), channel_id=1, source_target_pairs={{0,4},{2,6},{4,0},{6,2},{8,12},{10,14},{12,8},{14,10},{16,20},{18,... | collective-permute-start | bytes 3932168 | tf_op jit(solution)/shard_map/ppermute | solution.py:22
  94.7 70.7 %collective-permute-start.9 = (bf16[8,128,640]{2,1,0:T(8,128)(2,1)S(1)}, bf16[8,128,640]{2,1,0:T(8,128)(2,1)}, u32[]{:S(2)}, u32[]{:S(2)}) collective-permute-start(bf16[8,128,640]{2,1,0:T(8,128)(2,1)S(1)} %pad_maximum_fusion.2.refs_8_.refs_0_), channel_id=1, source_target_pairs={{0,2},{2,0},{4,6},{6,4},{8,10},{10,8},{12,14},{14,12},{16,18},{18,... | collective-permute-start | bytes 3932168 | tf_op jit(solution)/shard_map/ppermute | solution.py:22
  127.0 33.5 %collective-permute-start.4 = (bf16[8,672,128]{2,1,0:T(8,128)(2,1)}, bf16[8,672,128]{2,1,0:T(8,128)(2,1)S(1)}, u32[]{:S(2)}, u32[]{:S(2)}) collective-permute-start(bf16[8,672,128]{2,1,0:T(8,128)(2,1)} %get-tuple-element.60), channel_id=1, source_target_pairs={{0,2},{2,0},{4,6},{6,4},{8,10},{10,8},{12,14},{14,12},{16,18},{18,... | collective-permute-start | bytes 4128776 | tf_op jit(solution)/shard_map/ppermute | solution.py:22
  160.4 48.2 %collective-permute-start.12 = (bf16[8,672,128]{2,1,0:T(8,128)(2,1)}, bf16[8,672,128]{2,1,0:T(8,128)(2,1)S(1)}, u32[]{:S(2)}, u32[]{:S(2)}) collective-permute-start(bf16[8,672,128]{2,1,0:T(8,128)(2,1)} %get-tuple-element.71), channel_id=1, source_target_pairs={{0,4},{2,6},{4,0},{6,2},{8,12},{10,14},{12,8},{14,10},{16,20},{18,... | collective-permute-start | bytes 4128776 | tf_op jit(solution)/shard_map/ppermute | solution.py:22
  163.4 43.4 %collective-permute-start.8 = (bf16[4,672,128]{2,1,0:T(8,128)(2,1)S(1)}, bf16[4,672,128]{2,1,0:T(8,128)(2,1)S(1)}, u32[]{:S(2)}, u32[]{:S(2)}) collective-permute-start(bf16[4,672,128]{2,1,0:T(8,128)(2,1)S(1)} %get-tuple-element.64), channel_id=1, source_target_pairs={{0,4},{2,6},{4,0},{6,2},{8,12},{10,14},{12,8},{14,10},{16,20},{18,... | collective-permute-start | bytes 2064392 | tf_op jit(solution)/shard_map/ppermute | solution.py:22
  195.3 120.1 %collective-permute-start.11 = (bf16[8,672,128]{2,1,0:T(8,128)(2,1)}, bf16[8,672,128]{2,1,0:T(8,128)(2,1)S(1)}, u32[]{:S(2)}, u32[]{:S(2)}) collective-permute-start(bf16[8,672,128]{2,1,0:T(8,128)(2,1)} %get-tuple-element.68), channel_id=1, source_target_pairs={{0,2},{2,0},{4,6},{6,4},{8,10},{10,8},{12,14},{14,12},{16,18},{18,... | collective-permute-start | bytes 4128776 | tf_op jit(solution)/shard_map/ppermute | solution.py:22
  223.3 159.3 %collective-permute-start.23 = (bf16[640,2560]{1,0:T(8,128)(2,1)}, bf16[640,2560]{1,0:T(8,128)(2,1)}, u32[]{:S(2)}, u32[]{:S(2)}) collective-permute-start(bf16[640,2560]{1,0:T(8,128)(2,1)} %get-tuple-element.107), channel_id=1, source_target_pairs={{0,1},{1,0},{2,3},{3,2},{4,5},{5,4},{6,7},{7,6},{8,9},{9,8},{10,11... | collective-permute-start | bytes 9830408 | tf_op jit(solution)/shard_map/ppermute | solution.py:31
  312.0 33.4 %collective-permute-start.14 = (bf16[8,672,128]{2,1,0:T(8,128)(2,1)}, bf16[8,672,128]{2,1,0:T(8,128)(2,1)S(1)}, u32[]{:S(2)}, u32[]{:S(2)}) collective-permute-start(bf16[8,672,128]{2,1,0:T(8,128)(2,1)} %get-tuple-element.77), channel_id=1, source_target_pairs={{0,4},{2,6},{4,0},{6,2},{8,12},{10,14},{12,8},{14,10},{16,20},{18,... | collective-permute-start | bytes 4128776 | tf_op jit(solution)/shard_map/ppermute | solution.py:22
  312.8 17.0 %collective-permute-start.15 = (bf16[4,672,128]{2,1,0:T(8,128)(2,1)S(1)}, bf16[4,672,128]{2,1,0:T(8,128)(2,1)S(1)}, u32[]{:S(2)}, u32[]{:S(2)}) collective-permute-start(bf16[4,672,128]{2,1,0:T(8,128)(2,1)S(1)} %get-tuple-element.78), channel_id=1, source_target_pairs={{0,2},{2,0},{4,6},{6,4},{8,10},{10,8},{12,14},{14,12},{16,18},{18,... | collective-permute-start | bytes 2064392 | tf_op jit(solution)/shard_map/ppermute | solution.py:22
  317.5 40.8 %collective-permute-start.18 = (bf16[4,672,128]{2,1,0:T(8,128)(2,1)S(1)}, bf16[4,672,128]{2,1,0:T(8,128)(2,1)S(1)}, u32[]{:S(2)}, u32[]{:S(2)}) collective-permute-start(bf16[4,672,128]{2,1,0:T(8,128)(2,1)S(1)} %get-tuple-element.83), channel_id=1, source_target_pairs={{0,4},{2,6},{4,0},{6,2},{8,12},{10,14},{12,8},{14,10},{16,20},{18,... | collective-permute-start | bytes 2064392 | tf_op jit(solution)/shard_map/ppermute | solution.py:22
  346.1 14.6 %collective-permute-start.16 = (bf16[4,672,128]{2,1,0:T(8,128)(2,1)S(1)}, bf16[4,672,128]{2,1,0:T(8,128)(2,1)S(1)}, u32[]{:S(2)}, u32[]{:S(2)}) collective-permute-start(bf16[4,672,128]{2,1,0:T(8,128)(2,1)S(1)} %get-tuple-element.81), channel_id=1, source_target_pairs={{0,2},{2,0},{4,6},{6,4},{8,10},{10,8},{12,14},{14,12},{16,18},{18,... | collective-permute-start | bytes 2064392 | tf_op jit(solution)/shard_map/ppermute | solution.py:22
  358.6 14.8 %collective-permute-start.20 = (bf16[2,672,128]{2,1,0:T(8,128)(2,1)S(1)}, bf16[2,672,128]{2,1,0:T(8,128)(2,1)S(1)}, u32[]{:S(2)}, u32[]{:S(2)}) collective-permute-start(bf16[2,672,128]{2,1,0:T(8,128)(2,1)S(1)} %get-tuple-element.88), channel_id=1, source_target_pairs={{0,8},{2,10},{4,12},{6,14},{8,0},{10,2},{12,4},{14,6},{16,24},{18,... | collective-permute-start | bytes 1032200 | tf_op jit(solution)/shard_map/ppermute | solution.py:22
  361.1 20.4 %collective-permute-start.19 = (bf16[2,672,128]{2,1,0:T(8,128)(2,1)S(1)}, bf16[2,672,128]{2,1,0:T(8,128)(2,1)S(1)}, u32[]{:S(2)}, u32[]{:S(2)}) collective-permute-start(bf16[2,672,128]{2,1,0:T(8,128)(2,1)S(1)} %get-tuple-element.87), channel_id=1, source_target_pairs={{0,8},{2,10},{4,12},{6,14},{8,0},{10,2},{12,4},{14,6},{16,24},{18,... | collective-permute-start | bytes 1032200 | tf_op jit(solution)/shard_map/ppermute | solution.py:22
  382.7 14.2 %collective-permute-start.24 = (bf16[1920,128]{1,0:T(8,128)(2,1)S(1)}, bf16[1920,128]{1,0:T(8,128)(2,1)S(1)}, u32[]{:S(2)}, u32[]{:S(2)}) collective-permute-start(bf16[1920,128]{1,0:T(8,128)(2,1)S(1)} %pad_maximum_fusion.7), channel_id=1, source_target_pairs={{0,2},{2,0},{4,6},{6,4},{8,10},{10,8},{12,14},{14,12},{16,18},{18,... | collective-permute-start | bytes 1474568 | tf_op jit(solution)/shard_map/ppermute | solution.py:22
  384.3 22.2 %collective-permute-start.25 = (bf16[1920,128]{1,0:T(8,128)(2,1)S(1)}, bf16[1920,128]{1,0:T(8,128)(2,1)S(1)}, u32[]{:S(2)}, u32[]{:S(2)}) collective-permute-start(bf16[1920,128]{1,0:T(8,128)(2,1)S(1)} %pad_maximum_fusion.7), channel_id=1, source_target_pairs={{0,4},{2,6},{4,0},{6,2},{8,12},{10,14},{12,8},{14,10},{16,20},{18,... | collective-permute-start | bytes 1474568 | tf_op jit(solution)/shard_map/ppermute | solution.py:22
  385.4 21.1 %collective-permute-start.26 = (bf16[1920,128]{1,0:T(8,128)(2,1)S(1)}, bf16[1920,128]{1,0:T(8,128)(2,1)S(1)}, u32[]{:S(2)}, u32[]{:S(2)}) collective-permute-start(bf16[1920,128]{1,0:T(8,128)(2,1)S(1)} %pad_maximum_fusion.7), channel_id=1, source_target_pairs={{0,6},{2,4},{4,2},{6,0},{8,14},{10,12},{12,10},{14,8},{16,22},{18,... | collective-permute-start | bytes 1474568 | tf_op jit(solution)/shard_map/ppermute | solution.py:22
  409.6 12.3 %collective-permute-start.28 = (bf16[1920,512]{1,0:T(8,128)(2,1)S(1)}, bf16[1920,512]{1,0:T(8,128)(2,1)S(1)}, u32[]{:S(2)}, u32[]{:S(2)}) collective-permute-start(bf16[1920,512]{1,0:T(8,128)(2,1)S(1)} %pad_maximum_fusion), channel_id=1, source_target_pairs={{0,1},{1,0},{2,3},{3,2},{4,5},{5,4},{6,7},{7,6},{8,9},{9,8},{10,11... | collective-permute-start | bytes 5898248 | tf_op jit(solution)/shard_map/ppermute | solution.py:31
  (45 other events, 956.6 us)
Sparse Core Ops, SparseCore 0:
  16.7 80.2 all-gather.7
  98.6 118.5 all-gather.5
  219.9 62.2 all-gather.9

commit v5 on v4

--- a/solution.py
+++ b/solution.py
@@ -71,7 +71,12 @@
     )(queries, new_keys, scales, gain_q[None], gain_k[None], cosine, sine, after)
 
 
+def joined(parts, axis):
+    return parts[0] if len(parts) == 1 else jnp.concatenate(parts, axis=axis)
+
+
 def attend_kernel(
+    q_column,
     table_ref,
     slot_ref,
     q_slot_ref,
@@ -88,14 +93,14 @@
 
     def update(slots, q_slots, keys_ref, values_ref, masks, allowed):
         ones = jnp.ones((PIECE, keys_ref.shape[0]), jnp.bfloat16)
-        mask = jnp.concatenate(masks, axis=1)
-        old_peak = jnp.concatenate([peak[s] for s in slots], axis=1)
-        old_total = jnp.concatenate([total[s] for s in slots], axis=1)
+        mask = joined(masks, 1)
+        old_peak = joined([peak[s] for s in slots], 1)
+        old_total = joined([total[s] for s in slots], 1)
         scores, weights, tops, fades = {}, {}, {}, {}
 
         def score(h):
             cols = slice(h * HEAD_DIM, (h + 1) * HEAD_DIM)
-            q = jnp.concatenate([q_all[s, :, cols] for s in q_slots], axis=0)
+            q = joined([q_all[s, :, cols] for s in q_slots], 0)
             scores[h] = lax.dot_general(
                 keys_ref[:, cols], q, (((1,), (1,)), ((), ())), preferred_element_type=jnp.float32
             )
@@ -135,7 +140,9 @@
     def _():
         share = blocks // len(q_refs)
         copies = [
-            pltpu.make_async_copy(ref, q_all.at[pl.ds(i * share, share)], sems.at[i])
+            pltpu.make_async_copy(
+                ref.at[:, :, pl.ds(q_column, width)], q_all.at[pl.ds(i * share, share)], sems.at[i]
+            )
             for i, ref in enumerate(q_refs)
         ]
         for copy in copies:
@@ -170,16 +177,20 @@
         first = table_ref[4 * step - 2]
         count = table_ref[4 * step - 1]
 
+        def visit(at):
+            masks = [(b * rows + lane >= begin) & (b * rows + lane < end) for b in at]
+            slots, q_slots = [slot_ref[b] for b in at], [q_slot_ref[b] for b in at]
+            update(slots, q_slots, keys_ref.at[0], values_ref.at[0], masks, None)
+
         def pair(j, carry):
-            low = first + 2 * j
-            row = low * rows + lane
-            masks = [(r >= begin) & (r < end) for r in (row, row + rows)]
-            slots = [slot_ref[low], slot_ref[low + 1]]
-            q_slots = [q_slot_ref[low], q_slot_ref[low + 1]]
-            update(slots, q_slots, keys_ref.at[0], values_ref.at[0], masks, None)
+            visit([first + 2 * j, first + 2 * j + 1])
             return carry
 
-        lax.fori_loop(0, count, pair, 0)
+        lax.fori_loop(0, count // 2, pair, 0)
+
+        @pl.when(count % 2 == 1)
+        def _():
+            visit([first + count - 1])
 
     @pl.when(step == pl.num_programs(0) - 1)
     def _():
@@ -228,8 +239,9 @@
     near_spec = pl.BlockSpec((rows, width), lambda i, *_: (0, group))
     own_spec = pl.BlockSpec((rows, width), lambda i, *_: (0, 0))
     whole = lambda shape: pl.BlockSpec(shape, lambda i, *_: (0,) * len(shape))
+    q_column = group // 2 * width if len(q_parts) == 1 else 0
     return pl.pallas_call(
-        attend_kernel,
+        functools.partial(attend_kernel, q_column),
         grid_spec=pltpu.PrefetchScalarGridSpec(
             num_scalar_prefetch=3,
             grid=(pages + 1,),
@@ -281,56 +293,63 @@
     return block, top + jnp.log2(total)
 
 
-def combine_kernel(mine_low, mine_high, got_low, got_high, _, keep_ref, send_ref):
-    heads = (mine_low.shape[1] - LEVEL_ROWS) // HEAD_DIM
-    for mine, got, out in ((mine_low, got_low, keep_ref), (mine_high, got_high, send_ref)):
-        block, levels = merged([mine.at[0], got.at[0]], heads)
-        write_block(out.at[0], block, jnp.ones_like(levels), levels, heads)
-
-
-def combine(mine, got, after):
-    count, depth, rows = mine.shape
+def combine_kernel(*refs):
+    *ins, _, keep_ref, send_ref = refs
+    heads = (keep_ref.shape[1] - LEVEL_ROWS) // HEAD_DIM
+    for g in range(len(ins) // 4):
+        mine_low, mine_high, got_low, got_high = ins[4 * g : 4 * g + 4]
+        for mine, got, out in ((mine_low, got_low, keep_ref), (mine_high, got_high, send_ref)):
+            block, levels = merged([mine.at[0], got.at[0]], heads)
+            write_block(out.at[g], block, jnp.ones_like(levels), levels, heads)
+
+
+def combine(pairs, after):
+    count, depth, rows = pairs[0][0].shape
+    groups = len(pairs)
     half = count // 2
     low = pl.BlockSpec((1, depth, rows), lambda i: (i, 0, 0))
     high = pl.BlockSpec((1, depth, rows), lambda i: (i + half, 0, 0))
-    out = jax.ShapeDtypeStruct((half, depth, rows), jnp.bfloat16)
+    into = pl.BlockSpec((groups, depth, rows), lambda i: (i, 0, 0))
+    out = jax.ShapeDtypeStruct((half * groups, depth, rows), jnp.bfloat16)
     return pl.pallas_call(
         combine_kernel,
         grid=(half,),
-        in_specs=[low, high, low, high, pl.BlockSpec(memory_space=pl.ANY)],
-        out_specs=[low, low],
+        in_specs=[low, high, low, high] * groups + [pl.BlockSpec(memory_space=pl.ANY)],
+        out_specs=[into, into],
         out_shape=[out, out],
         compiler_params=pltpu.CompilerParams(vmem_limit_bytes=24 * 2**20),
         cost_estimate=pl.CostEstimate(
-            flops=count * depth * rows * 4, bytes_accessed=count * depth * rows * 6, transcendentals=0
+            flops=groups * count * depth * rows * 4,
+            bytes_accessed=groups * count * depth * rows * 6,
+            transcendentals=0,
         ),
         name="combine_pairs",
-    )(mine, mine, got, got, after)
-
-
-def last_kernel(*refs):
-    out_ref = refs[-1]
-    heads = out_ref.shape[0] // HEAD_DIM
-    block, _ = merged(refs[:-2], heads)
-    for h in range(heads):
-        out_ref[h * HEAD_DIM : (h + 1) * HEAD_DIM, :] = block(h).astype(jnp.bfloat16)
-
-
-def combine_last(parts, after):
-    depth, rows = parts[0].shape
+    )(*[part for mine, got in pairs for part in (mine, mine, got, got)], after)
+
+
+def last_kernel(mine_ref, got_ref, _, out_ref):
+    groups, depth, _ = mine_ref.shape
+    heads = (depth - LEVEL_ROWS) // HEAD_DIM
+    for g in range(groups):
+        block, _ = merged([mine_ref.at[g], got_ref.at[g]], heads)
+        for h in range(heads):
+            at = (g * heads + h) * HEAD_DIM
+            out_ref[at : at + HEAD_DIM, :] = block(h).astype(jnp.bfloat16)
+
+
+def combine_last(mine, got, after):
+    groups, depth, rows = mine.shape
     whole = pl.BlockSpec(memory_space=pltpu.VMEM)
     return pl.pallas_call(
         last_kernel,
-        in_specs=[whole] * len(parts) + [pl.BlockSpec(memory_space=pl.ANY)],
-        out_shape=jax.ShapeDtypeStruct((depth - LEVEL_ROWS, rows), jnp.bfloat16),
+        in_specs=[whole, whole, pl.BlockSpec(memory_space=pl.ANY)],
+        out_shape=jax.ShapeDtypeStruct((groups * (depth - LEVEL_ROWS), rows), jnp.bfloat16),
         compiler_params=pltpu.CompilerParams(vmem_limit_bytes=24 * 2**20),
         cost_estimate=pl.CostEstimate(
-            flops=len(parts) * depth * rows * 2,
-            bytes_accessed=(len(parts) + 1) * depth * rows * 2,
-            transcendentals=0,
+            flops=groups * depth * rows * 4, bytes_accessed=groups * depth * rows * 6, transcendentals=0
         ),
         name="combine_last",
-    )(*parts, after)
+    )(mine, got, after)
 
 
 def local(
@@ -399,8 +418,8 @@
     owner_starts = jnp.sum(jnp.where(owner_pick, starts[None, :], 0), axis=1)
     owner_ends = jnp.sum(jnp.where(owner_pick, ends[None, :], 0), axis=1)
     owner_first = owner_starts // tok_dev
-    owner_pairs = ((owner_ends - 1) // tok_dev - owner_first + 2) // 2
-    table = jnp.stack([owner_starts, owner_ends, owner_first, owner_pairs], axis=1).reshape(-1)
+    owner_blocks = (owner_ends - 1) // tok_dev - owner_first + 1
+    table = jnp.stack([owner_starts, owner_ends, owner_first, owner_blocks], axis=1).reshape(-1)
 
     near_blocks = device + jnp.arange(4, dtype=jnp.int32)
     near_rows = (near_blocks[:, None] * tok_dev + jnp.arange(tok_dev, dtype=jnp.int32)[None, :]).reshape(-1)
@@ -426,77 +445,97 @@
     for order in orders:
         slot = sum(jnp.where((apart & m) > 0, size >> (i + 1), 0) for i, m in enumerate(order))
         slots.append(jnp.concatenate([slot, beyond]))
-    gathered, near_keys = [], []
+    gathered, near_keys, parts, stages = [None] * groups, [None] * groups, [None] * groups, []
     after = scales
-    for group in range(groups):
-        part, key_part = turn(
+    for group in [0, 2, 1, 3] if groups > 1 else [0]:
+        parts[group], near_keys[group] = turn(
             group, queries, new_keys, scales, query_gain, key_gain, cosine, sine, after
         )
-        near_keys.append(key_part)
-        after = along_line if group == 2 else key_part
+        after = near_keys[group]
         if group % 2 == 0:
-            gathered.append([lax.all_gather(part[None], "req", axis=0, tiled=True)])
             continue
-        held, stages = part[None], []
+        held = parts[group][None]
         for m in orders[group][:0:-1]:
             held = lax.optimization_barrier(jnp.concatenate([held, send_xor(held, m)], axis=0))
             stages.append(held)
-            if held.shape[0] == line and group == 1:
-                along_line = held
-        gathered.append([held, send_xor(held, orders[group][0])])
-    weight, _ = lax.optimization_barrier((out_weight.T, near_keys[-1]))
-    lines = [[z * PLANE + p for z in range(line)] for p in range(PLANE)]
-    weight = lax.all_gather(weight, "req", axis=0, tiled=True, axis_index_groups=lines)
-
-    weight = weight.reshape(tp_size, blocks_each * columns, local_width)
-    weights = []
-    for k in range(tp_size):
-        part = lax.dynamic_index_in_dim(weight, (tp_device + k) % tp_size, 0, keepdims=False)
-        weights.append(part if k == 0 else send_tp(part, k))
-
+            if held.shape[0] == line:
+                after = held
+        gathered[group] = held
+    whole_blocks = lax.all_gather(
+        jnp.concatenate(parts[::2], axis=1)[None], "req", axis=0, tiled=True
+    )
+
+    def gather_weights(after):
+        weight, _ = lax.optimization_barrier((out_weight.T, after))
+        lines = [[z * PLANE + p for z in range(line)] for p in range(PLANE)]
+        weight = lax.all_gather(weight, "req", axis=0, tiled=True, axis_index_groups=lines)
+        weight = weight.reshape(tp_size, blocks_each * columns, local_width)
+        weights = []
+        for k in range(tp_size):
+            part = lax.dynamic_index_in_dim(weight, (tp_device + k) % tp_size, 0, keepdims=False)
+            weights.append(part if k == 0 else send_tp(part, k))
+        return weights
+
+    last = len(masks) - 1
+    if groups > 1:
+        turns = ("a1", "a0", "c1", "a2", "c0", "a3", "c2", "c01", "c3", "c2", "c01", "c3", "c2", "l01")
+        turns += ("c3", "l2", "l3")
+    else:
+        turns = ("a0",) + ("c0",) * last + ("l0",)
+    state, stage, attended = {}, {}, []
+    before = near_starts
     waits = [near_starts] * 4
     if groups > 1:
-        waits[:2] = stages[-2:]
+        waits[:2] = stages[-1], stages[-2]
+    weights = None
+    for turn_name in turns:
+        step, names = turn_name[0], turn_name[1:]
+        if step == "a":
+            group = int(names)
+            order = orders[group]
+            if group % 2 == 0:
+                q_parts = [whole_blocks]
+            else:
+                q_parts = [gathered[group], send_xor(gathered[group], order[0])]
+            state[names] = attend(
+                group, table, slots[group], natural if group % 2 == 0 else slots[group], q_parts,
+                cache_keys, cache_values, near_keys[group], new_values, near_starts,
+                (before, waits[group]),
+            )
+            stage[names] = 0
+            before = state[names][0]
+            if weights is None:
+                weights = gather_weights(before)
+            continue
+        if names not in state:
+            parts = list(names)
+        else:
+            parts = [names]
+        pairs = []
+        for part in parts:
+            keep, send = state[part]
+            pairs.append((keep, send_xor(send, orders[int(part[0])][stage[part]])))
+        stage[names] = stage[parts[0]] + 1
+        if step == "c":
+            state[names] = combine(pairs, before)
+            before = latest = state[names][0]
+        else:
+            if names == "2":
+                before = weights[-1]
+            before = combine_last(*pairs[0], before)
+            attended.append((names, before))
     if groups > 1:
-        turns = ((0, "a"), (1, "a"), (0, "c"), (3, "a"), (0, "c"), (1, "c"), (2, "a"))
-        turns += ((3, "c"), (0, "c"), (1, "c"), (2, "c"), (0, "l"), (3, "c"), (1, "c"), (2, "c"))
-        turns += ((1, "l"), (3, "c"), (2, "c"), (3, "l"), (2, "l"))
-    else:
-        turns = ((0, "a"),) + ((0, "c"),) * (len(masks) - 1) + ((0, "l"),)
-    attended, state, left = [None] * groups, [None] * groups, [list(order) for order in orders]
-    before = near_starts
-    for group, step in turns:
-        if step == "a":
-            state[group] = attend(
-                group, table, slots[group], natural if group % 2 == 0 else slots[group], gathered[group],
-                cache_keys, cache_values, near_keys[group], new_values, near_starts, (before, waits[group]),
-            )
-            before = state[group][0]
-        elif step == "c":
-            keep, send = state[group]
-            state[group] = combine(keep, send_xor(send, left[group].pop(0)), before)
-            before = latest = state[group][0]
-        else:
-            if group == 3:
-                before = weights[-1]
-            keep, send = state[group]
-            attended[group] = combine_last([keep[0], send_xor(send, left[group].pop(0))[0]], before)
-            before = attended[group]
-    if groups > 1:
-        attended = [attended[group] for group in (0, 1, 3, 2)]
-        attended[0], _ = lax.optimization_barrier((attended[0], latest))
+        attended[0] = (attended[0][0], lax.optimization_barrier((attended[0][1], latest))[0])
 
     projected = 0.0
     share = local_width // groups
-    if groups > 1:
-        weight_sets = [[(0, 2 * share), (3 * share, 4 * share)], [(2 * share, 3 * share)]]
-    else:
-        weight_sets = [[(0, local_width)]]
-    for some, spans in zip([attended[:-1], attended[-1:]] if groups > 1 else [attended], weight_sets):
-        some = jnp.concatenate(some, axis=0)
+    for some in [attended[:-1], attended[-1:]] if groups > 1 else [attended]:
+        names = "".join(name for name, _ in some)
+        some = joined([part for _, part in some], 0)
         got = [send_xor(some, k) for k in range(1, PLANE)]
-        *got, _ = lax.optimization_barrier((*got, attended[-1]))
+        *got, _ = lax.optimization_barrier((*got, attended[-1][1]))
         spread = jnp.concatenate([some] + got, axis=1)
+        spans = [(int(names[0]) * share, int(names[-1]) * share + share)]
         for k in range(tp_size):
             part = spread if k == 0 else send_tp(spread, k)
             at = 0

time: 449 us -> 449 us (level)
  Pallas kernels: 127 us -> 102 us
  waiting for transfers between devices: 224 us -> 249 us
    ppermute x33 -> x31, waiting for transfers between devices: 158 us -> 203 us  [send_xor(): return lax.ppermute(value, 'req', [(i, i ^ by) for i in range(size)])]
    pallas_call x8 -> x7, Pallas kernels: 120 us -> 95.2 us  [the longest x4 94.9 us: attend(): pl.pallas_call(functools.partial(attend_kernel, q_column), grid_spec=pltp...]
    all_gather x3 -> x2, waiting for transfers between devices: 66 us -> 46 us  [the longest x1 46 us: gather_weights(): lax.all_gather(weight, 'req', axis=0, tiled=True, axis_index_groups=lines)]
    ppermute x33 -> x31, starting transfers between devices: 39.7 us -> 38.2 us  [send_xor(): return lax.ppermute(value, 'req', [(i, i ^ by) for i in range(size)])]
    unnamed x60 -> x58, local copies, waits for them, and re-layouts: 9.18 us -> 8.77 us
  transfers between devices with their start and end apart: 39 -> 36, of which waited for: 27 -> 23; matrix products, arithmetic and copies ran while one was open for 4% -> 4% of each run, Pallas kernels for 28% -> 23%
where the time goes in v5:
time: 449 us; the launch traced here: 446 us
  waiting for transfers between devices  249 us (55%)
  Pallas kernels  102 us (23%)
  starting transfers between devices  38.5 us (9%)
  local copies, waits for them, and re-layouts  17.2 us (4%)
  between operations  14.1 us (3%)
  other arithmetic  12.2 us (3%)
  matrix products  8.86 us (2%)
    ppermute x31, waiting for transfers between devices, send_xor(): return lax.ppermute(value, 'req', [(i, i ^ by) for i in range(size)])  203 us
    pallas_call x4, Pallas kernels, attend(): pl.pallas_call(functools.partial(attend_kernel, q_column), grid_spec=pltp...  94.9 us
    all_gather x1, waiting for transfers between devices, gather_weights(): lax.all_gather(weight, 'req', axis=0, tiled=True, axis_index_groups=lines)  46 us
    ppermute x31, starting transfers between devices, send_xor(): return lax.ppermute(value, 'req', [(i, i ^ by) for i in range(size)])  38.2 us
  transfers between devices with their start and end apart: 36, of which 23 were waited for; matrix products, arithmetic and copies ran while one was open for 4% of the time, Pallas kernels for 23%

profile of v5, /device:TPU:0, one launch (start us, length us, event | category | flops | bytes accessed | tf_op | source)
XLA Modules:
  0.0 445.7 jit_solution(5118002999048899131)
XLA Ops:
  11.1 3.9 psum.7
  17.7 3.8 collective-permute-start
  21.5 8.2 %collective-permute-done = bf16[1,128,640]{2,1,0:T(8,128)(2,1)S(1)} collective-permute-done((bf16[1,128,640]{2,1,0:T(8,128)(2,1)S(1)}, bf16[1,128,640]{2,1,0:T(8,128)(2,1)S(1)}, u32[]{:S(2)}, u32[]{:S(2)}) %collective-permute-start) | collective-permute-done | bytes 163872 | tf_op jit(solution)/shard_map/ppermute | solution.py:22
  30.6 14.8 %collective-permute-done.1 = bf16[2,128,640]{2,1,0:T(8,128)(2,1)S(1)} collective-permute-done((bf16[2,128,640]{2,1,0:T(8,128)(2,1)S(1)}, bf16[2,128,640]{2,1,0:T(8,128)(2,1)S(1)}, u32[]{:S(2)}, u32[]{:S(2)}) %collective-permute-start.1) | collective-permute-done | bytes 327712 | tf_op jit(solution)/shard_map/ppermute | solution.py:22
  47.7 23.7 %collective-permute-done.2 = bf16[4,128,640]{2,1,0:T(8,128)(2,1)S(1)} collective-permute-done((bf16[4,128,640]{2,1,0:T(8,128)(2,1)S(1)}, bf16[4,128,640]{2,1,0:T(8,128)(2,1)S(1)}, u32[]{:S(2)}, u32[]{:S(2)}) %collective-permute-start.2) | collective-permute-done | bytes 655392 | tf_op jit(solution)/shard_map/ppermute | solution.py:22
  78.4 7.5 %collective-permute-done.4 = bf16[1,128,640]{2,1,0:T(8,128)(2,1)S(1)} collective-permute-done((bf16[1,128,640]{2,1,0:T(8,128)(2,1)S(1)}, bf16[1,128,640]{2,1,0:T(8,128)(2,1)S(1)}, u32[]{:S(2)}, u32[]{:S(2)}) %collective-permute-start.4) | collective-permute-done | bytes 163872 | tf_op jit(solution)/shard_map/ppermute | solution.py:22
  87.4 21.9 %collective-permute-done.5 = bf16[2,128,640]{2,1,0:T(8,128)(2,1)S(1)} collective-permute-done((bf16[2,128,640]{2,1,0:T(8,128)(2,1)S(1)}, bf16[2,128,640]{2,1,0:T(8,128)(2,1)S(1)}, u32[]{:S(2)}, u32[]{:S(2)}) %collective-permute-start.5) | collective-permute-done | bytes 327712 | tf_op jit(solution)/shard_map/ppermute | solution.py:22
  110.2 6.6 %collective-permute-done.3.refs_1_ = bf16[8,128,640]{2,1,0:T(8,128)(2,1)} collective-permute-done((bf16[8,128,640]{2,1,0:T(8,128)(2,1)}, bf16[8,128,640]{2,1,0:T(8,128)(2,1)}, u32[]{:S(2)}, u32[]{:S(2)}) %collective-permute-start.3) | collective-permute-done | bytes 1310752 | tf_op jit(solution)/shard_map/ppermute | solution.py:22
  116.7 23.8 %cache_attend.4 = (bf16[8,672,128]{2,1,0:T(8,128)(2,1)}, bf16[8,672,128]{2,1,0:T(8,128)(2,1)}) custom-call(s32[64]{0:T(128)} %reshape.325.table_ref, s32[18]{0:T(128)} %fusion.15.slot_ref.q_slot_ref, s32[18]{0:T(128)} %fusion.15.slot_ref.q_slot_ref, bf16[8,128,640]{2,1,0:T(8,128)(2,1)} %pad_maximum_fusion.1.refs_0_, ...), custom_call_target="tpu_custom_call" | custom-call | flops 26843545600 | bytes 10485760 | tf_op jit(solution)/shard_map/cache_attend/pallas_call | solution.py:243
  145.1 9.9 %collective-permute-done.6 = bf16[4,128,640]{2,1,0:T(8,128)(2,1)S(1)} collective-permute-done((bf16[4,128,640]{2,1,0:T(8,128)(2,1)S(1)}, bf16[4,128,640]{2,1,0:T(8,128)(2,1)S(1)}, u32[]{:S(2)}, u32[]{:S(2)}) %collective-permute-start.6) | collective-permute-done | bytes 655392 | tf_op jit(solution)/shard_map/ppermute | solution.py:22
  158.7 23.7 %cache_attend.5 = (bf16[8,672,128]{2,1,0:T(8,128)(2,1)}, bf16[8,672,128]{2,1,0:T(8,128)(2,1)}) custom-call(s32[64]{0:T(128)} %reshape.325.table_ref, s32[18]{0:T(128)} %fusion.16.slot_ref.q_slot_ref, s32[18]{0:T(128)} %fusion.17.q_slot_ref, bf16[16,128,1280]{2,1,0:T(8,128)(2,1)} %bitcast.63, bf16[16,256,2560]{2,1,0:T(8,128)(2,1)} %refs_2_.7, ...), custom_call_target="tpu_custom_call" | custom-call | flops 26843545600 | bytes 10485760 | tf_op jit(solution)/shard_map/cache_attend/pallas_call | solution.py:243
  187.7 23.7 %cache_attend.6 = (bf16[8,672,128]{2,1,0:T(8,128)(2,1)}, bf16[8,672,128]{2,1,0:T(8,128)(2,1)}) custom-call(s32[64]{0:T(128)} %reshape.325.table_ref, s32[18]{0:T(128)} %fusion.15.slot_ref.q_slot_ref, s32[18]{0:T(128)} %fusion.17.q_slot_ref, bf16[16,128,1280]{2,1,0:T(8,128)(2,1)} %bitcast.64, bf16[16,256,2560]{2,1,0:T(8,128)(2,1)} %refs_2_.7, ...), custom_call_target="tpu_custom_call" | custom-call | flops 26843545600 | bytes 10485760 | tf_op jit(solution)/shard_map/cache_attend/pallas_call | solution.py:243
  214.7 46.0 %all-gather.4.cloned.1.call-done = bf16[1280,2560]{1,0:T(8,128)(2,1)} async-done(((bf16[320,2560]{1,0:T(8,128)(2,1)}), bf16[1280,2560]{1,0:T(8,128)(2,1)}) %all-gather.4.cloned.1.call-update) | async-done | bytes 6553616 | tf_op jit(solution)/shard_map/all_gather | solution.py:471
  260.8 6.2 %dynamic-slice_bitcast_fusion.1 = (bf16[640,2560]{1,0:T(8,128)(2,1)}, bf16[640,2560]{1,0:T(8,128)(2,1)}) fusion(bf16[2,640,2560]{2,1,0:T(8,128)(2,1)} %bitcast.44, s32[]{:T(128)S(6)} %select_n.254, s32[]{:T(128)S(6)} %select_n.258), kind=kLoop, calls=%fused_computation.4 | loop fusion | bytes 13107208 | tf_op jit(solution)/shard_map/jit(dynamic_index_in_dim)/squeeze | solution.py:475
  267.0 23.7 %cache_attend.7 = (bf16[8,672,128]{2,1,0:T(8,128)(2,1)}, bf16[8,672,128]{2,1,0:T(8,128)(2,1)}) custom-call(s32[64]{0:T(128)} %reshape.325.table_ref, s32[18]{0:T(128)} %fusion.16.slot_ref.q_slot_ref, s32[18]{0:T(128)} %fusion.16.slot_ref.q_slot_ref, bf16[8,128,640]{2,1,0:T(8,128)(2,1)} %pad_maximum_fusion.2.refs_7_.refs_0_, ...), custom_call_target="tpu_custom_call" | custom-call | flops 26843545600 | bytes 10485760 | tf_op jit(solution)/shard_map/cache_attend/pallas_call | solution.py:243
  296.9 41.8 %collective-permute-done.10.refs_6_.refs_7_ = bf16[4,672,128]{2,1,0:T(8,128)(2,1)S(1)} collective-permute-done((bf16[4,672,128]{2,1,0:T(8,128)(2,1)S(1)}, bf16[4,672,128]{2,1,0:T(8,128)(2,1)S(1)}, u32[]{:S(2)}, u32[]{:S(2)}) %collective-permute-start.10) | collective-permute-done | bytes 688160 | tf_op jit(solution)/shard_map/ppermute | solution.py:22
  342.7 10.3 %collective-permute-done.14.refs_2_.refs_3_ = bf16[4,672,128]{2,1,0:T(8,128)(2,1)S(1)} collective-permute-done((bf16[4,672,128]{2,1,0:T(8,128)(2,1)S(1)}, bf16[4,672,128]{2,1,0:T(8,128)(2,1)S(1)}, u32[]{:S(2)}, u32[]{:S(2)}) %collective-permute-start.14) | collective-permute-done | bytes 688160 | tf_op jit(solution)/shard_map/ppermute | solution.py:22
  360.1 9.9 %collective-permute-done.17.refs_2_.refs_3_ = bf16[2,672,128]{2,1,0:T(8,128)(2,1)S(1)} collective-permute-done((bf16[2,672,128]{2,1,0:T(8,128)(2,1)S(1)}, bf16[2,672,128]{2,1,0:T(8,128)(2,1)S(1)}, u32[]{:S(2)}, u32[]{:S(2)}) %collective-permute-start.17) | collective-permute-done | bytes 344096 | tf_op jit(solution)/shard_map/ppermute | solution.py:22
  370.2 4.1 collective-permute-done.16.got_ref
  374.5 7.4 %collective-permute-done.19.refs_2_.refs_3_ = bf16[2,672,128]{2,1,0:T(8,128)(2,1)S(1)} collective-permute-done((bf16[2,672,128]{2,1,0:T(8,128)(2,1)S(1)}, bf16[2,672,128]{2,1,0:T(8,128)(2,1)S(1)}, u32[]{:S(2)}, u32[]{:S(2)}) %collective-permute-start.19) | collective-permute-done | bytes 344096 | tf_op jit(solution)/shard_map/ppermute | solution.py:22
  386.7 8.2 %collective-permute-done.25.got_ref = bf16[1,672,128]{2,1,0:T(8,128)(2,1)S(1)} collective-permute-done((bf16[1,672,128]{2,1,0:T(8,128)(2,1)S(1)}, bf16[1,672,128]{2,1,0:T(8,128)(2,1)S(1)}, u32[]{:S(2)}, u32[]{:S(2)}) %collective-permute-start.25) | collective-permute-done | bytes 172064 | tf_op jit(solution)/shard_map/ppermute | solution.py:22
  396.4 10.1 %collective-permute-done.23 = bf16[1920,128]{1,0:T(8,128)(2,1)S(1)} collective-permute-done((bf16[1920,128]{1,0:T(8,128)(2,1)S(1)}, bf16[1920,128]{1,0:T(8,128)(2,1)S(1)}, u32[]{:S(2)}, u32[]{:S(2)}) %collective-permute-start.23) | collective-permute-done | bytes 491552 | tf_op jit(solution)/shard_map/ppermute | solution.py:22
  410.3 3.5 collective-permute-done.27
  428.3 4.4 collective-permute-done.31
  (185 shorter events, 84.6 us)
Async XLA Ops:
  6.6 152.1 %all-gather.6.cloned.1.call-start = ((), (), s32[]{:S(2)}) async-start(), calls=%async_computation.1 | async-start | bytes 5570560 | tf_op jit(solution)/shard_map/all_gather | solution.py:464
  17.2 243.5 %all-gather.4.cloned.1.call-start = ((), (), s32[]{:S(2)}) async-start(), calls=%async_computation | async-start | bytes 8192000 | tf_op jit(solution)/shard_map/all_gather | solution.py:471
  29.8 15.6 %collective-permute-start.1 = (bf16[2,128,640]{2,1,0:T(8,128)(2,1)S(1)}, bf16[2,128,640]{2,1,0:T(8,128)(2,1)S(1)}, u32[]{:S(2)}, u32[]{:S(2)}) collective-permute-start(bf16[2,128,640]{2,1,0:T(8,128)(2,1)S(1)} %pad_maximum_fusion.8), channel_id=1, source_target_pairs={{0,8},{2,10},{4,12},{6,14},{8,0},{10,2},{12,4},{14,6},{16,24},{18,... | collective-permute-start | bytes 983048 | tf_op jit(solution)/shard_map/ppermute | solution.py:22
  45.5 26.0 %collective-permute-start.2 = (bf16[4,128,640]{2,1,0:T(8,128)(2,1)S(1)}, bf16[4,128,640]{2,1,0:T(8,128)(2,1)S(1)}, u32[]{:S(2)}, u32[]{:S(2)}) collective-permute-start(bf16[4,128,640]{2,1,0:T(8,128)(2,1)S(1)} %pad_maximum_fusion.4._), channel_id=1, source_target_pairs={{0,2},{2,0},{4,6},{6,4},{8,10},{10,8},{12,14},{14,12},{16,18},{18,... | collective-permute-start | bytes 1966088 | tf_op jit(solution)/shard_map/ppermute | solution.py:22
  72.6 44.1 %collective-permute-start.3 = (bf16[8,128,640]{2,1,0:T(8,128)(2,1)}, bf16[8,128,640]{2,1,0:T(8,128)(2,1)}, u32[]{:S(2)}, u32[]{:S(2)}) collective-permute-start(bf16[8,128,640]{2,1,0:T(8,128)(2,1)} %pad_maximum_fusion.1.refs_0_), channel_id=1, source_target_pairs={{0,4},{2,6},{4,0},{6,2},{8,12},{10,14},{12,8},{14,10},{16,20},{18,... | collective-permute-start | bytes 3932168 | tf_op jit(solution)/shard_map/ppermute | solution.py:22
  86.0 23.3 %collective-permute-start.5 = (bf16[2,128,640]{2,1,0:T(8,128)(2,1)S(1)}, bf16[2,128,640]{2,1,0:T(8,128)(2,1)S(1)}, u32[]{:S(2)}, u32[]{:S(2)}) collective-permute-start(bf16[2,128,640]{2,1,0:T(8,128)(2,1)S(1)} %pad_maximum_fusion.9), channel_id=1, source_target_pairs={{0,8},{2,10},{4,12},{6,14},{8,0},{10,2},{12,4},{14,6},{16,24},{18,... | collective-permute-start | bytes 983048 | tf_op jit(solution)/shard_map/ppermute | solution.py:22
  141.6 13.4 %collective-permute-start.6 = (bf16[4,128,640]{2,1,0:T(8,128)(2,1)S(1)}, bf16[4,128,640]{2,1,0:T(8,128)(2,1)S(1)}, u32[]{:S(2)}, u32[]{:S(2)}) collective-permute-start(bf16[4,128,640]{2,1,0:T(8,128)(2,1)S(1)} %copy-done.19), channel_id=1, source_target_pairs={{0,4},{2,6},{4,0},{6,2},{8,12},{10,14},{12,8},{14,10},{16,20},{18,... | collective-permute-start | bytes 1966088 | tf_op jit(solution)/shard_map/ppermute | solution.py:22
  156.2 110.8 %collective-permute-start.12 = (bf16[8,128,640]{2,1,0:T(8,128)(2,1)}, bf16[8,128,640]{2,1,0:T(8,128)(2,1)}, u32[]{:S(2)}, u32[]{:S(2)}) collective-permute-start(bf16[8,128,640]{2,1,0:T(8,128)(2,1)} %pad_maximum_fusion.2.refs_7_.refs_0_), channel_id=1, source_target_pairs={{0,2},{2,0},{4,6},{6,4},{8,10},{10,8},{12,14},{14,12},{16,18},{18,... | collective-permute-start | bytes 3932168 | tf_op jit(solution)/shard_map/ppermute | solution.py:22
  158.4 26.4 %collective-permute-start.8 = (bf16[8,672,128]{2,1,0:T(8,128)(2,1)S(1)}, bf16[8,672,128]{2,1,0:T(8,128)(2,1)S(1)}, u32[]{:S(2)}, u32[]{:S(2)}) collective-permute-start(bf16[8,672,128]{2,1,0:T(8,128)(2,1)S(1)} %copy-done.28), channel_id=1, source_target_pairs={{0,4},{2,6},{4,0},{6,2},{8,12},{10,14},{12,8},{14,10},{16,20},{18,... | collective-permute-start | bytes 4128776 | tf_op jit(solution)/shard_map/ppermute | solution.py:22
  182.5 29.4 %collective-permute-start.7 = (bf16[8,672,128]{2,1,0:T(8,128)(2,1)}, bf16[8,672,128]{2,1,0:T(8,128)(2,1)S(1)}, u32[]{:S(2)}, u32[]{:S(2)}) collective-permute-start(bf16[8,672,128]{2,1,0:T(8,128)(2,1)} %get-tuple-element.59), channel_id=1, source_target_pairs={{0,2},{2,0},{4,6},{6,4},{8,10},{10,8},{12,14},{14,12},{16,18},{18,... | collective-permute-start | bytes 4128776 | tf_op jit(solution)/shard_map/ppermute | solution.py:22
  211.5 83.2 %collective-permute-start.11 = (bf16[8,672,128]{2,1,0:T(8,128)(2,1)}, bf16[8,672,128]{2,1,0:T(8,128)(2,1)S(1)}, u32[]{:S(2)}, u32[]{:S(2)}) collective-permute-start(bf16[8,672,128]{2,1,0:T(8,128)(2,1)} %get-tuple-element.66), channel_id=1, source_target_pairs={{0,4},{2,6},{4,0},{6,2},{8,12},{10,14},{12,8},{14,10},{16,20},{18,... | collective-permute-start | bytes 4128776 | tf_op jit(solution)/shard_map/ppermute | solution.py:22
  266.9 115.1 %collective-permute-start.21 = (bf16[640,2560]{1,0:T(8,128)(2,1)}, bf16[640,2560]{1,0:T(8,128)(2,1)}, u32[]{:S(2)}, u32[]{:S(2)}) collective-permute-start(bf16[640,2560]{1,0:T(8,128)(2,1)} %get-tuple-element.100), channel_id=1, source_target_pairs={{0,1},{1,0},{2,3},{3,2},{4,5},{5,4},{6,7},{7,6},{8,9},{9,8},{10,11... | collective-permute-start | bytes 9830408 | tf_op jit(solution)/shard_map/ppermute | solution.py:31
  290.7 48.8 %collective-permute-start.15 = (bf16[8,672,128]{2,1,0:T(8,128)(2,1)}, bf16[8,672,128]{2,1,0:T(8,128)(2,1)S(1)}, u32[]{:S(2)}, u32[]{:S(2)}) collective-permute-start(bf16[8,672,128]{2,1,0:T(8,128)(2,1)} %get-tuple-element.73), channel_id=1, source_target_pairs={{0,2},{2,0},{4,6},{6,4},{8,10},{10,8},{12,14},{14,12},{16,18},{18,... | collective-permute-start | bytes 4128776 | tf_op jit(solution)/shard_map/ppermute | solution.py:22
  292.4 46.2 %collective-permute-start.10 = (bf16[4,672,128]{2,1,0:T(8,128)(2,1)S(1)}, bf16[4,672,128]{2,1,0:T(8,128)(2,1)S(1)}, u32[]{:S(2)}, u32[]{:S(2)}) collective-permute-start(bf16[4,672,128]{2,1,0:T(8,128)(2,1)S(1)} %get-tuple-element.65), channel_id=1, source_target_pairs={{0,2},{2,0},{4,6},{6,4},{8,10},{10,8},{12,14},{14,12},{16,18},{18,... | collective-permute-start | bytes 2064392 | tf_op jit(solution)/shard_map/ppermute | solution.py:22
  292.8 45.9 %collective-permute-start.9 = (bf16[4,672,128]{2,1,0:T(8,128)(2,1)S(1)}, bf16[4,672,128]{2,1,0:T(8,128)(2,1)S(1)}, u32[]{:S(2)}, u32[]{:S(2)}) collective-permute-start(bf16[4,672,128]{2,1,0:T(8,128)(2,1)S(1)} %get-tuple-element.64), channel_id=1, source_target_pairs={{0,4},{2,6},{4,0},{6,2},{8,12},{10,14},{12,8},{14,10},{16,20},{18,... | collective-permute-start | bytes 2064392 | tf_op jit(solution)/shard_map/ppermute | solution.py:22
  296.7 56.3 %collective-permute-start.14 = (bf16[4,672,128]{2,1,0:T(8,128)(2,1)S(1)}, bf16[4,672,128]{2,1,0:T(8,128)(2,1)S(1)}, u32[]{:S(2)}, u32[]{:S(2)}) collective-permute-start(bf16[4,672,128]{2,1,0:T(8,128)(2,1)S(1)} %get-tuple-element.72), channel_id=1, source_target_pairs={{0,2},{2,0},{4,6},{6,4},{8,10},{10,8},{12,14},{14,12},{16,18},{18,... | collective-permute-start | bytes 2064392 | tf_op jit(solution)/shard_map/ppermute | solution.py:22
  339.4 16.9 %collective-permute-start.13 = (bf16[4,672,128]{2,1,0:T(8,128)(2,1)S(1)}, bf16[4,672,128]{2,1,0:T(8,128)(2,1)S(1)}, u32[]{:S(2)}, u32[]{:S(2)}) collective-permute-start(bf16[4,672,128]{2,1,0:T(8,128)(2,1)S(1)} %get-tuple-element.71), channel_id=1, source_target_pairs={{0,8},{2,10},{4,12},{6,14},{8,0},{10,2},{12,4},{14,6},{16,24},{18,... | collective-permute-start | bytes 2064392 | tf_op jit(solution)/shard_map/ppermute | solution.py:22
  340.7 16.9 %collective-permute-start.18 = (bf16[4,672,128]{2,1,0:T(8,128)(2,1)S(1)}, bf16[4,672,128]{2,1,0:T(8,128)(2,1)S(1)}, u32[]{:S(2)}, u32[]{:S(2)}) collective-permute-start(bf16[4,672,128]{2,1,0:T(8,128)(2,1)S(1)} %get-tuple-element.79), channel_id=1, source_target_pairs={{0,4},{2,6},{4,0},{6,2},{8,12},{10,14},{12,8},{14,10},{16,20},{18,... | collective-permute-start | bytes 2064392 | tf_op jit(solution)/shard_map/ppermute | solution.py:22
  353.3 16.6 %collective-permute-start.17 = (bf16[2,672,128]{2,1,0:T(8,128)(2,1)S(1)}, bf16[2,672,128]{2,1,0:T(8,128)(2,1)S(1)}, u32[]{:S(2)}, u32[]{:S(2)}) collective-permute-start(bf16[2,672,128]{2,1,0:T(8,128)(2,1)S(1)} %get-tuple-element.78), channel_id=1, source_target_pairs={{0,8},{2,10},{4,12},{6,14},{8,0},{10,2},{12,4},{14,6},{16,24},{18,... | collective-permute-start | bytes 1032200 | tf_op jit(solution)/shard_map/ppermute | solution.py:22
  356.7 17.6 %collective-permute-start.16 = (bf16[2,672,128]{2,1,0:T(8,128)(2,1)S(1)}, bf16[2,672,128]{2,1,0:T(8,128)(2,1)S(1)}, u32[]{:S(2)}, u32[]{:S(2)}) collective-permute-start(bf16[2,672,128]{2,1,0:T(8,128)(2,1)S(1)} %get-tuple-element.77), channel_id=1, source_target_pairs={{0,16},{2,18},{4,20},{6,22},{8,24},{10,26},{12,28},{14,30},{16,0},... | collective-permute-start | bytes 1032200 | tf_op jit(solution)/shard_map/ppermute | solution.py:22
  358.3 23.6 %collective-permute-start.19 = (bf16[2,672,128]{2,1,0:T(8,128)(2,1)S(1)}, bf16[2,672,128]{2,1,0:T(8,128)(2,1)S(1)}, u32[]{:S(2)}, u32[]{:S(2)}) collective-permute-start(bf16[2,672,128]{2,1,0:T(8,128)(2,1)S(1)} %get-tuple-element.82), channel_id=1, source_target_pairs={{0,8},{2,10},{4,12},{6,14},{8,0},{10,2},{12,4},{14,6},{16,24},{18,... | collective-permute-start | bytes 1032200 | tf_op jit(solution)/shard_map/ppermute | solution.py:22
  382.2 14.2 %collective-permute-start.22 = (bf16[1920,128]{1,0:T(8,128)(2,1)S(1)}, bf16[1920,128]{1,0:T(8,128)(2,1)S(1)}, u32[]{:S(2)}, u32[]{:S(2)}) collective-permute-start(bf16[1920,128]{1,0:T(8,128)(2,1)S(1)} %pad_maximum_fusion.7), channel_id=1, source_target_pairs={{0,2},{2,0},{4,6},{6,4},{8,10},{10,8},{12,14},{14,12},{16,18},{18,... | collective-permute-start | bytes 1474568 | tf_op jit(solution)/shard_map/ppermute | solution.py:22
  383.9 22.5 %collective-permute-start.23 = (bf16[1920,128]{1,0:T(8,128)(2,1)S(1)}, bf16[1920,128]{1,0:T(8,128)(2,1)S(1)}, u32[]{:S(2)}, u32[]{:S(2)}) collective-permute-start(bf16[1920,128]{1,0:T(8,128)(2,1)S(1)} %pad_maximum_fusion.7), channel_id=1, source_target_pairs={{0,4},{2,6},{4,0},{6,2},{8,12},{10,14},{12,8},{14,10},{16,20},{18,... | collective-permute-start | bytes 1474568 | tf_op jit(solution)/shard_map/ppermute | solution.py:22
  384.6 21.9 %collective-permute-start.24 = (bf16[1920,128]{1,0:T(8,128)(2,1)S(1)}, bf16[1920,128]{1,0:T(8,128)(2,1)S(1)}, u32[]{:S(2)}, u32[]{:S(2)}) collective-permute-start(bf16[1920,128]{1,0:T(8,128)(2,1)S(1)} %pad_maximum_fusion.7), channel_id=1, source_target_pairs={{0,6},{2,4},{4,2},{6,0},{8,14},{10,12},{12,10},{14,8},{16,22},{18,... | collective-permute-start | bytes 1474568 | tf_op jit(solution)/shard_map/ppermute | solution.py:22
  (41 other events, 894.9 us)
Sparse Core Ops, SparseCore 0:
  17.3 114.9 all-gather.5
  140.7 120.0 all-gather.3

commit v6 on v5

--- a/solution.py
+++ b/solution.py
@@ -269,7 +269,7 @@
             dimension_semantics=("arbitrary",), vmem_limit_bytes=56 * 2**20
         ),
         cost_estimate=pl.CostEstimate(
-            flops=pages * heads * 256 * page_len * HEAD_DIM * 40,
+            flops=pages * heads * 256 * page_len * HEAD_DIM * 8,
             bytes_accessed=pages * page_len * width * 4,
             transcendentals=pages * heads * 256 * page_len,
         ),
@@ -469,7 +469,10 @@
         weight, _ = lax.optimization_barrier((out_weight.T, after))
         lines = [[z * PLANE + p for z in range(line)] for p in range(PLANE)]
         weight = lax.all_gather(weight, "req", axis=0, tiled=True, axis_index_groups=lines)
-        weight = weight.reshape(tp_size, blocks_each * columns, local_width)
+        return weight.reshape(tp_size, blocks_each * columns, local_width)
+
+    def swap_weights(weight, after):
+        weight, _ = lax.optimization_barrier((weight, after))
         weights = []
         for k in range(tp_size):
             part = lax.dynamic_index_in_dim(weight, (tp_device + k) % tp_size, 0, keepdims=False)
@@ -478,16 +481,16 @@
 
     last = len(masks) - 1
     if groups > 1:
-        turns = ("a1", "a0", "c1", "a2", "c0", "a3", "c2", "c01", "c3", "c2", "c01", "c3", "c2", "l01")
-        turns += ("c3", "l2", "l3")
+        turns = ("a1", "a0", "c1", "a2", "c1", "c0", "a3", "c2", "c1", "c0", "c3", "c2", "l1", "c0", "c3")
+        turns += ("c2", "l0", "c3", "l2", "l3")
     else:
         turns = ("a0",) + ("c0",) * last + ("l0",)
     state, stage, attended = {}, {}, []
     before = near_starts
     waits = [near_starts] * 4
     if groups > 1:
-        waits[:2] = stages[-1], stages[-2]
-    weights = None
+        waits[1] = stages[-2]
+    weight, weights = None, None
     for turn_name in turns:
         step, names = turn_name[0], turn_name[1:]
         if step == "a":
@@ -504,8 +507,8 @@
             )
             stage[names] = 0
             before = state[names][0]
-            if weights is None:
-                weights = gather_weights(before)
+            if weight is None:
+                weight = gather_weights(before)
             continue
         if names not in state:
             parts = list(names)
@@ -519,12 +522,13 @@
         if step == "c":
             state[names] = combine(pairs, before)
             before = latest = state[names][0]
+            if weights is None and names in ("3", str(groups - 1)):
+                weights = swap_weights(weight, before)
         else:
-            if names == "2":
-                before = weights[-1]
             before = combine_last(*pairs[0], before)
             attended.append((names, before))
     if groups > 1:
+        attended[:2] = attended[1::-1]
         attended[0] = (attended[0][0], lax.optimization_barrier((attended[0][1], latest))[0])
 
     projected = 0.0

time: 449 us -> 409 us (0.911); the launches traced: 446 us -> 411 us
  waiting for transfers between devices: 249 us -> 196 us
  Pallas kernels: 102 us -> 114 us
  starting transfers between devices: 38.5 us -> 49.8 us
  local copies, waits for them, and re-layouts: 17.2 us -> 10.6 us
    all_gather x1, waiting for transfers between devices: 46 us -> 0.02 us  [gather_weights(): lax.all_gather(weight, 'req', axis=0, tiled=True, axis_index_groups=lines)]
    ppermute x31 -> x33, starting transfers between devices: 38.2 us -> 49.5 us  [send_xor(): return lax.ppermute(value, 'req', [(i, i ^ by) for i in range(size)])]
    ppermute x31 -> x33, waiting for transfers between devices: 203 us -> 196 us  [send_xor(): return lax.ppermute(value, 'req', [(i, i ^ by) for i in range(size)])]
    pallas_call x10 -> x12, Pallas kernels: 5.09 us -> 12 us  [combine(): pl.pallas_call(combine_kernel, grid=(half,), in_specs=[low, high, low, hi...]
    pallas_call x4, Pallas kernels: 94.9 us -> 99.6 us  [attend(): pl.pallas_call(functools.partial(attend_kernel, q_column), grid_spec=pltp...]
  transfers between devices with their start and end apart: 36 -> 38, of which waited for: 23 -> 22; matrix products, arithmetic and copies ran while one was open for 4% -> 5% of each run, Pallas kernels for 23% -> 28%
where the time goes in v6:
time: 409 us; the launch traced here: 411 us
  waiting for transfers between devices  196 us (48%)
  Pallas kernels  114 us (28%)
  starting transfers between devices  49.8 us (12%)
  other arithmetic  16.6 us (4%)
  between operations  14 us (3%)
  local copies, waits for them, and re-layouts  10.6 us (3%)
  matrix products  6.13 us (1%)
    ppermute x33, waiting for transfers between devices, send_xor(): return lax.ppermute(value, 'req', [(i, i ^ by) for i in range(size)])  196 us
    pallas_call x4, Pallas kernels, attend(): pl.pallas_call(functools.partial(attend_kernel, q_column), grid_spec=pltp...  99.6 us
    ppermute x33, starting transfers between devices, send_xor(): return lax.ppermute(value, 'req', [(i, i ^ by) for i in range(size)])  49.5 us
    pallas_call x12, Pallas kernels, combine(): pl.pallas_call(combine_kernel, grid=(half,), in_specs=[low, high, low, hi...  12 us
  transfers between devices with their start and end apart: 38, of which 22 were waited for; matrix products, arithmetic and copies ran while one was open for 5% of the time, Pallas kernels for 28%

profile of v6, /device:TPU:0, one launch (start us, length us, event | category | flops | bytes accessed | tf_op | source)
XLA Modules:
  0.0 411.0 jit_solution(12101584707981088926)
XLA Ops:
  10.4 3.9 psum.7
  17.0 3.8 collective-permute-start
  20.9 8.2 %collective-permute-done = bf16[1,128,640]{2,1,0:T(8,128)(2,1)S(1)} collective-permute-done((bf16[1,128,640]{2,1,0:T(8,128)(2,1)S(1)}, bf16[1,128,640]{2,1,0:T(8,128)(2,1)S(1)}, u32[]{:S(2)}, u32[]{:S(2)}) %collective-permute-start) | collective-permute-done | bytes 163872 | tf_op jit(solution)/shard_map/ppermute | solution.py:22
  29.9 14.8 %collective-permute-done.1 = bf16[2,128,640]{2,1,0:T(8,128)(2,1)S(1)} collective-permute-done((bf16[2,128,640]{2,1,0:T(8,128)(2,1)S(1)}, bf16[2,128,640]{2,1,0:T(8,128)(2,1)S(1)}, u32[]{:S(2)}, u32[]{:S(2)}) %collective-permute-start.1) | collective-permute-done | bytes 327712 | tf_op jit(solution)/shard_map/ppermute | solution.py:22
  47.0 23.7 %collective-permute-done.2 = bf16[4,128,640]{2,1,0:T(8,128)(2,1)S(1)} collective-permute-done((bf16[4,128,640]{2,1,0:T(8,128)(2,1)S(1)}, bf16[4,128,640]{2,1,0:T(8,128)(2,1)S(1)}, u32[]{:S(2)}, u32[]{:S(2)}) %collective-permute-start.2) | collective-permute-done | bytes 655392 | tf_op jit(solution)/shard_map/ppermute | solution.py:22
  77.7 7.6 %collective-permute-done.4 = bf16[1,128,640]{2,1,0:T(8,128)(2,1)S(1)} collective-permute-done((bf16[1,128,640]{2,1,0:T(8,128)(2,1)S(1)}, bf16[1,128,640]{2,1,0:T(8,128)(2,1)S(1)}, u32[]{:S(2)}, u32[]{:S(2)}) %collective-permute-start.4) | collective-permute-done | bytes 163872 | tf_op jit(solution)/shard_map/ppermute | solution.py:22
  86.8 21.9 %collective-permute-done.5 = bf16[2,128,640]{2,1,0:T(8,128)(2,1)S(1)} collective-permute-done((bf16[2,128,640]{2,1,0:T(8,128)(2,1)S(1)}, bf16[2,128,640]{2,1,0:T(8,128)(2,1)S(1)}, u32[]{:S(2)}, u32[]{:S(2)}) %collective-permute-start.5) | collective-permute-done | bytes 327712 | tf_op jit(solution)/shard_map/ppermute | solution.py:22
  109.6 6.7 %collective-permute-done.3.refs_1_ = bf16[8,128,640]{2,1,0:T(8,128)(2,1)} collective-permute-done((bf16[8,128,640]{2,1,0:T(8,128)(2,1)}, bf16[8,128,640]{2,1,0:T(8,128)(2,1)}, u32[]{:S(2)}, u32[]{:S(2)}) %collective-permute-start.3) | collective-permute-done | bytes 1310752 | tf_op jit(solution)/shard_map/ppermute | solution.py:22
  116.3 24.9 %cache_attend.4 = (bf16[8,672,128]{2,1,0:T(8,128)(2,1)}, bf16[8,672,128]{2,1,0:T(8,128)(2,1)}) custom-call(s32[64]{0:T(128)} %reshape.325.table_ref, s32[18]{0:T(128)} %fusion.15.slot_ref.q_slot_ref, s32[18]{0:T(128)} %fusion.15.slot_ref.q_slot_ref, bf16[8,128,640]{2,1,0:T(8,128)(2,1)} %pad_maximum_fusion.1.refs_0_, ...), custom_call_target="tpu_custom_call" | custom-call | flops 5368709120 | bytes 10485760 | tf_op jit(solution)/shard_map/cache_attend/pallas_call | solution.py:243
  145.3 25.0 %cache_attend.5 = (bf16[8,672,128]{2,1,0:T(8,128)(2,1)}, bf16[8,672,128]{2,1,0:T(8,128)(2,1)}) custom-call(s32[64]{0:T(128)} %reshape.325.table_ref, s32[18]{0:T(128)} %fusion.16.slot_ref.q_slot_ref, s32[18]{0:T(128)} %fusion.17.q_slot_ref, bf16[16,128,1280]{2,1,0:T(8,128)(2,1)} %bitcast.44, bf16[16,256,2560]{2,1,0:T(8,128)(2,1)} %refs_2_.7, ...), custom_call_target="tpu_custom_call" | custom-call | flops 5368709120 | bytes 10485760 | tf_op jit(solution)/shard_map/cache_attend/pallas_call | solution.py:243
  175.6 5.0 %collective-permute-done.9.refs_2_.refs_3_ = bf16[8,672,128]{2,1,0:T(8,128)(2,1)S(1)} collective-permute-done((bf16[8,672,128]{2,1,0:T(8,128)(2,1)}, bf16[8,672,128]{2,1,0:T(8,128)(2,1)S(1)}, u32[]{:S(2)}, u32[]{:S(2)}) %collective-permute-start.9) | collective-permute-done | bytes 1376288 | tf_op jit(solution)/shard_map/ppermute | solution.py:22
  183.1 3.7 collective-permute-start.10
  186.8 24.9 %cache_attend.6 = (bf16[8,672,128]{2,1,0:T(8,128)(2,1)}, bf16[8,672,128]{2,1,0:T(8,128)(2,1)}) custom-call(s32[64]{0:T(128)} %reshape.325.table_ref, s32[18]{0:T(128)} %fusion.15.slot_ref.q_slot_ref, s32[18]{0:T(128)} %fusion.17.q_slot_ref, bf16[16,128,1280]{2,1,0:T(8,128)(2,1)} %bitcast.45, bf16[16,256,2560]{2,1,0:T(8,128)(2,1)} %refs_2_.7, ...), custom_call_target="tpu_custom_call" | custom-call | flops 5368709120 | bytes 10485760 | tf_op jit(solution)/shard_map/cache_attend/pallas_call | solution.py:243
  213.5 26.5 %collective-permute-done.10.refs_2_.refs_3_ = bf16[4,672,128]{2,1,0:T(8,128)(2,1)S(1)} collective-permute-done((bf16[4,672,128]{2,1,0:T(8,128)(2,1)}, bf16[4,672,128]{2,1,0:T(8,128)(2,1)S(1)}, u32[]{:S(2)}, u32[]{:S(2)}) %collective-permute-start.10) | collective-permute-done | bytes 688160 | tf_op jit(solution)/shard_map/ppermute | solution.py:22
  243.3 24.8 %cache_attend.7 = (bf16[8,672,128]{2,1,0:T(8,128)(2,1)}, bf16[8,672,128]{2,1,0:T(8,128)(2,1)}) custom-call(s32[64]{0:T(128)} %reshape.325.table_ref, s32[18]{0:T(128)} %fusion.16.slot_ref.q_slot_ref, s32[18]{0:T(128)} %fusion.16.slot_ref.q_slot_ref, bf16[8,128,640]{2,1,0:T(8,128)(2,1)} %pad_maximum_fusion.2.refs_0_, ...), custom_call_target="tpu_custom_call" | custom-call | flops 5368709120 | bytes 10485760 | tf_op jit(solution)/shard_map/cache_attend/pallas_call | solution.py:243
  274.0 4.0 collective-permute-done.13.refs_2_.refs_3_
  282.6 18.8 %collective-permute-done.11.refs_2_.refs_3_ = bf16[8,672,128]{2,1,0:T(8,128)(2,1)S(1)} collective-permute-done((bf16[8,672,128]{2,1,0:T(8,128)(2,1)}, bf16[8,672,128]{2,1,0:T(8,128)(2,1)S(1)}, u32[]{:S(2)}, u32[]{:S(2)}) %collective-permute-start.11) | collective-permute-done | bytes 1376288 | tf_op jit(solution)/shard_map/ppermute | solution.py:22
  303.1 5.1 %collective-permute-start.16 = (bf16[1,672,128]{2,1,0:T(8,128)(2,1)}, bf16[1,672,128]{2,1,0:T(8,128)(2,1)}, u32[]{:S(2)}, u32[]{:S(2)}) collective-permute-start(bf16[1,672,128]{2,1,0:T(8,128)(2,1)} %get-tuple-element.83), channel_id=1, source_target_pairs={{0,16},{2,18},{4,20},{6,22},{8,24},{10,26},{12,28},{14,30},{16,0},... | collective-permute-start | bytes 516104 | tf_op jit(solution)/shard_map/ppermute | solution.py:22
  327.3 11.2 %collective-permute-done.18.got_ref = bf16[1,672,128]{2,1,0:T(8,128)(2,1)S(1)} collective-permute-done((bf16[1,672,128]{2,1,0:T(8,128)(2,1)S(1)}, bf16[1,672,128]{2,1,0:T(8,128)(2,1)S(1)}, u32[]{:S(2)}, u32[]{:S(2)}) %collective-permute-start.18) | collective-permute-done | bytes 172064 | tf_op jit(solution)/shard_map/ppermute | solution.py:22
  343.7 5.0 %collective-permute-start.24 = (bf16[1920,128]{1,0:T(8,128)(2,1)S(1)}, bf16[1920,128]{1,0:T(8,128)(2,1)S(1)}, u32[]{:S(2)}, u32[]{:S(2)}) collective-permute-start(bf16[1920,128]{1,0:T(8,128)(2,1)S(1)} %pad_maximum_fusion.7), channel_id=1, source_target_pairs={{0,4},{2,6},{4,0},{6,2},{8,12},{10,14},{12,8},{14,10},{16,20},{18,... | collective-permute-start | bytes 1474568 | tf_op jit(solution)/shard_map/ppermute | solution.py:22
  348.7 7.8 %collective-permute-done.26.got_ref = bf16[1,672,128]{2,1,0:T(8,128)(2,1)S(1)} collective-permute-done((bf16[1,672,128]{2,1,0:T(8,128)(2,1)S(1)}, bf16[1,672,128]{2,1,0:T(8,128)(2,1)S(1)}, u32[]{:S(2)}, u32[]{:S(2)}) %collective-permute-start.26) | collective-permute-done | bytes 172064 | tf_op jit(solution)/shard_map/ppermute | solution.py:22
  356.6 13.8 %collective-permute-done.24 = bf16[1920,128]{1,0:T(8,128)(2,1)S(1)} collective-permute-done((bf16[1920,128]{1,0:T(8,128)(2,1)S(1)}, bf16[1920,128]{1,0:T(8,128)(2,1)S(1)}, u32[]{:S(2)}, u32[]{:S(2)}) %collective-permute-start.24) | collective-permute-done | bytes 491552 | tf_op jit(solution)/shard_map/ppermute | solution.py:22
  377.3 3.5 collective-permute-done.29
  393.4 6.6 %collective-permute-done.34 = bf16[640,128]{1,0:T(8,128)(2,1)S(1)} collective-permute-done((bf16[640,128]{1,0:T(8,128)(2,1)S(1)}, bf16[640,128]{1,0:T(8,128)(2,1)S(1)}, u32[]{:S(2)}, u32[]{:S(2)}) %collective-permute-start.34) | collective-permute-done | bytes 163872 | tf_op jit(solution)/shard_map/ppermute | solution.py:22
  (184 shorter events, 95.8 us)
Async XLA Ops:
  6.6 138.7 %all-gather.6.cloned.1.call-start = ((), (), s32[]{:S(2)}) async-start(), calls=%async_computation.1 | async-start | bytes 5570560 | tf_op jit(solution)/shard_map/all_gather | solution.py:464
  16.6 300.0 %all-gather.4.cloned.1.call-start = ((), (), s32[]{:S(2)}) async-start(), calls=%async_computation | async-start | bytes 8192000 | tf_op jit(solution)/shard_map/all_gather | solution.py:471
  29.1 15.6 %collective-permute-start.1 = (bf16[2,128,640]{2,1,0:T(8,128)(2,1)S(1)}, bf16[2,128,640]{2,1,0:T(8,128)(2,1)S(1)}, u32[]{:S(2)}, u32[]{:S(2)}) collective-permute-start(bf16[2,128,640]{2,1,0:T(8,128)(2,1)S(1)} %pad_maximum_fusion.8), channel_id=1, source_target_pairs={{0,8},{2,10},{4,12},{6,14},{8,0},{10,2},{12,4},{14,6},{16,24},{18,... | collective-permute-start | bytes 983048 | tf_op jit(solution)/shard_map/ppermute | solution.py:22
  44.8 25.9 %collective-permute-start.2 = (bf16[4,128,640]{2,1,0:T(8,128)(2,1)S(1)}, bf16[4,128,640]{2,1,0:T(8,128)(2,1)S(1)}, u32[]{:S(2)}, u32[]{:S(2)}) collective-permute-start(bf16[4,128,640]{2,1,0:T(8,128)(2,1)S(1)} %pad_maximum_fusion.4._), channel_id=1, source_target_pairs={{0,2},{2,0},{4,6},{6,4},{8,10},{10,8},{12,14},{14,12},{16,18},{18,... | collective-permute-start | bytes 1966088 | tf_op jit(solution)/shard_map/ppermute | solution.py:22
  72.0 44.3 %collective-permute-start.3 = (bf16[8,128,640]{2,1,0:T(8,128)(2,1)}, bf16[8,128,640]{2,1,0:T(8,128)(2,1)}, u32[]{:S(2)}, u32[]{:S(2)}) collective-permute-start(bf16[8,128,640]{2,1,0:T(8,128)(2,1)} %pad_maximum_fusion.1.refs_0_), channel_id=1, source_target_pairs={{0,4},{2,6},{4,0},{6,2},{8,12},{10,14},{12,8},{14,10},{16,20},{18,... | collective-permute-start | bytes 3932168 | tf_op jit(solution)/shard_map/ppermute | solution.py:22
  85.4 23.4 %collective-permute-start.5 = (bf16[2,128,640]{2,1,0:T(8,128)(2,1)S(1)}, bf16[2,128,640]{2,1,0:T(8,128)(2,1)S(1)}, u32[]{:S(2)}, u32[]{:S(2)}) collective-permute-start(bf16[2,128,640]{2,1,0:T(8,128)(2,1)S(1)} %pad_maximum_fusion.9), channel_id=1, source_target_pairs={{0,8},{2,10},{4,12},{6,14},{8,0},{10,2},{12,4},{14,6},{16,24},{18,... | collective-permute-start | bytes 983048 | tf_op jit(solution)/shard_map/ppermute | solution.py:22
  141.2 31.7 %collective-permute-start.6 = (bf16[4,128,640]{2,1,0:T(8,128)(2,1)}, bf16[4,128,640]{2,1,0:T(8,128)(2,1)}, u32[]{:S(2)}, u32[]{:S(2)}) collective-permute-start(bf16[4,128,640]{2,1,0:T(8,128)(2,1)} %pad_maximum_fusion.5.refs_8_), channel_id=1, source_target_pairs={{0,4},{2,6},{4,0},{6,2},{8,12},{10,14},{12,8},{14,10},{16,20},{18,... | collective-permute-start | bytes 1966088 | tf_op jit(solution)/shard_map/ppermute | solution.py:22
  144.7 35.8 %collective-permute-start.9 = (bf16[8,672,128]{2,1,0:T(8,128)(2,1)}, bf16[8,672,128]{2,1,0:T(8,128)(2,1)S(1)}, u32[]{:S(2)}, u32[]{:S(2)}) collective-permute-start(bf16[8,672,128]{2,1,0:T(8,128)(2,1)} %get-tuple-element.66), channel_id=1, source_target_pairs={{0,4},{2,6},{4,0},{6,2},{8,12},{10,14},{12,8},{14,10},{16,20},{18,... | collective-permute-start | bytes 4128776 | tf_op jit(solution)/shard_map/ppermute | solution.py:22
  170.3 71.3 %collective-permute-start.8 = (bf16[8,672,128]{2,1,0:T(8,128)(2,1)}, bf16[8,672,128]{2,1,0:T(8,128)(2,1)S(1)}, u32[]{:S(2)}, u32[]{:S(2)}) collective-permute-start(bf16[8,672,128]{2,1,0:T(8,128)(2,1)} %get-tuple-element.65), channel_id=1, source_target_pairs={{0,2},{2,0},{4,6},{6,4},{8,10},{10,8},{12,14},{14,12},{16,18},{18,... | collective-permute-start | bytes 4128776 | tf_op jit(solution)/shard_map/ppermute | solution.py:22
  175.5 67.8 %collective-permute-start.7 = (bf16[8,128,640]{2,1,0:T(8,128)(2,1)}, bf16[8,128,640]{2,1,0:T(8,128)(2,1)}, u32[]{:S(2)}, u32[]{:S(2)}) collective-permute-start(bf16[8,128,640]{2,1,0:T(8,128)(2,1)} %pad_maximum_fusion.2.refs_0_), channel_id=1, source_target_pairs={{0,2},{2,0},{4,6},{6,4},{8,10},{10,8},{12,14},{14,12},{16,18},{18,... | collective-permute-start | bytes 3932168 | tf_op jit(solution)/shard_map/ppermute | solution.py:22
  183.1 56.9 %collective-permute-start.10 = (bf16[4,672,128]{2,1,0:T(8,128)(2,1)}, bf16[4,672,128]{2,1,0:T(8,128)(2,1)S(1)}, u32[]{:S(2)}, u32[]{:S(2)}) collective-permute-start(bf16[4,672,128]{2,1,0:T(8,128)(2,1)} %get-tuple-element.68), channel_id=1, source_target_pairs={{0,2},{2,0},{4,6},{6,4},{8,10},{10,8},{12,14},{14,12},{16,18},{18,... | collective-permute-start | bytes 2064392 | tf_op jit(solution)/shard_map/ppermute | solution.py:22
  211.6 59.1 %collective-permute-start.14 = (bf16[8,672,128]{2,1,0:T(8,128)(2,1)}, bf16[8,672,128]{2,1,0:T(8,128)(2,1)S(1)}, u32[]{:S(2)}, u32[]{:S(2)}) collective-permute-start(bf16[8,672,128]{2,1,0:T(8,128)(2,1)} %get-tuple-element.76), channel_id=1, source_target_pairs={{0,4},{2,6},{4,0},{6,2},{8,12},{10,14},{12,8},{14,10},{16,20},{18,... | collective-permute-start | bytes 4128776 | tf_op jit(solution)/shard_map/ppermute | solution.py:22
  268.1 33.3 %collective-permute-start.11 = (bf16[8,672,128]{2,1,0:T(8,128)(2,1)}, bf16[8,672,128]{2,1,0:T(8,128)(2,1)S(1)}, u32[]{:S(2)}, u32[]{:S(2)}) collective-permute-start(bf16[8,672,128]{2,1,0:T(8,128)(2,1)} %get-tuple-element.73), channel_id=1, source_target_pairs={{0,2},{2,0},{4,6},{6,4},{8,10},{10,8},{12,14},{14,12},{16,18},{18,... | collective-permute-start | bytes 4128776 | tf_op jit(solution)/shard_map/ppermute | solution.py:22
  273.8 35.1 %collective-permute-start.17 = (bf16[4,672,128]{2,1,0:T(8,128)(2,1)}, bf16[4,672,128]{2,1,0:T(8,128)(2,1)}, u32[]{:S(2)}, u32[]{:S(2)}) collective-permute-start(bf16[4,672,128]{2,1,0:T(8,128)(2,1)} %get-tuple-element.84), channel_id=1, source_target_pairs={{0,2},{2,0},{4,6},{6,4},{8,10},{10,8},{12,14},{14,12},{16,18},{18,... | collective-permute-start | bytes 2064392 | tf_op jit(solution)/shard_map/ppermute | solution.py:22
  303.1 13.7 %collective-permute-start.20 = (bf16[4,672,128]{2,1,0:T(8,128)(2,1)}, bf16[4,672,128]{2,1,0:T(8,128)(2,1)S(1)}, u32[]{:S(2)}, u32[]{:S(2)}) collective-permute-start(bf16[4,672,128]{2,1,0:T(8,128)(2,1)} %get-tuple-element.89), channel_id=1, source_target_pairs={{0,4},{2,6},{4,0},{6,2},{8,12},{10,14},{12,8},{14,10},{16,20},{18,... | collective-permute-start | bytes 2064392 | tf_op jit(solution)/shard_map/ppermute | solution.py:22
  310.9 13.5 %collective-permute-start.19 = (bf16[2,672,128]{2,1,0:T(8,128)(2,1)}, bf16[2,672,128]{2,1,0:T(8,128)(2,1)}, u32[]{:S(2)}, u32[]{:S(2)}) collective-permute-start(bf16[2,672,128]{2,1,0:T(8,128)(2,1)} %get-tuple-element.88), channel_id=1, source_target_pairs={{0,8},{2,10},{4,12},{6,14},{8,0},{10,2},{12,4},{14,6},{16,24},{18,... | collective-permute-start | bytes 1032200 | tf_op jit(solution)/shard_map/ppermute | solution.py:22
  317.4 21.1 %collective-permute-start.21 = (bf16[2,672,128]{2,1,0:T(8,128)(2,1)S(1)}, bf16[2,672,128]{2,1,0:T(8,128)(2,1)S(1)}, u32[]{:S(2)}, u32[]{:S(2)}) collective-permute-start(bf16[2,672,128]{2,1,0:T(8,128)(2,1)S(1)} %get-tuple-element.92), channel_id=1, source_target_pairs={{0,8},{2,10},{4,12},{6,14},{8,0},{10,2},{12,4},{14,6},{16,24},{18,... | collective-permute-start | bytes 1032200 | tf_op jit(solution)/shard_map/ppermute | solution.py:22
  322.9 64.4 %collective-permute-start.27 = (bf16[640,2560]{1,0:T(8,128)(2,1)S(1)}, bf16[640,2560]{1,0:T(8,128)(2,1)S(1)}, u32[]{:S(2)}, u32[]{:S(2)}) collective-permute-start(bf16[640,2560]{1,0:T(8,128)(2,1)S(1)} %get-tuple-element.109), channel_id=1, source_target_pairs={{0,1},{1,0},{2,3},{3,2},{4,5},{5,4},{6,7},{7,6},{8,9},{9,8},{10,11... | collective-permute-start | bytes 9830408 | tf_op jit(solution)/shard_map/ppermute | solution.py:31
  323.0 15.4 %collective-permute-start.18 = (bf16[1,672,128]{2,1,0:T(8,128)(2,1)S(1)}, bf16[1,672,128]{2,1,0:T(8,128)(2,1)S(1)}, u32[]{:S(2)}, u32[]{:S(2)}) collective-permute-start(bf16[1,672,128]{2,1,0:T(8,128)(2,1)S(1)} %get-tuple-element.87), channel_id=1, source_target_pairs={{0,16},{2,18},{4,20},{6,22},{8,24},{10,26},{12,28},{14,30},{16,0},... | collective-permute-start | bytes 516104 | tf_op jit(solution)/shard_map/ppermute | solution.py:22
  325.6 16.2 %collective-permute-start.22 = (bf16[1,672,128]{2,1,0:T(8,128)(2,1)S(1)}, bf16[1,672,128]{2,1,0:T(8,128)(2,1)S(1)}, u32[]{:S(2)}, u32[]{:S(2)}) collective-permute-start(bf16[1,672,128]{2,1,0:T(8,128)(2,1)S(1)} %get-tuple-element.95), channel_id=1, source_target_pairs={{0,16},{2,18},{4,20},{6,22},{8,24},{10,26},{12,28},{14,30},{16,0},... | collective-permute-start | bytes 516104 | tf_op jit(solution)/shard_map/ppermute | solution.py:22
  341.9 14.7 %collective-permute-start.23 = (bf16[1920,128]{1,0:T(8,128)(2,1)S(1)}, bf16[1920,128]{1,0:T(8,128)(2,1)S(1)}, u32[]{:S(2)}, u32[]{:S(2)}) collective-permute-start(bf16[1920,128]{1,0:T(8,128)(2,1)S(1)} %pad_maximum_fusion.7), channel_id=1, source_target_pairs={{0,2},{2,0},{4,6},{6,4},{8,10},{10,8},{12,14},{14,12},{16,18},{18,... | collective-permute-start | bytes 1474568 | tf_op jit(solution)/shard_map/ppermute | solution.py:22
  343.7 26.7 %collective-permute-start.24 = (bf16[1920,128]{1,0:T(8,128)(2,1)S(1)}, bf16[1920,128]{1,0:T(8,128)(2,1)S(1)}, u32[]{:S(2)}, u32[]{:S(2)}) collective-permute-start(bf16[1920,128]{1,0:T(8,128)(2,1)S(1)} %pad_maximum_fusion.7), channel_id=1, source_target_pairs={{0,4},{2,6},{4,0},{6,2},{8,12},{10,14},{12,8},{14,10},{16,20},{18,... | collective-permute-start | bytes 1474568 | tf_op jit(solution)/shard_map/ppermute | solution.py:22
  348.7 21.7 %collective-permute-start.25 = (bf16[1920,128]{1,0:T(8,128)(2,1)S(1)}, bf16[1920,128]{1,0:T(8,128)(2,1)S(1)}, u32[]{:S(2)}, u32[]{:S(2)}) collective-permute-start(bf16[1920,128]{1,0:T(8,128)(2,1)S(1)} %pad_maximum_fusion.7), channel_id=1, source_target_pairs={{0,6},{2,4},{4,2},{6,0},{8,14},{10,12},{12,10},{14,8},{16,22},{18,... | collective-permute-start | bytes 1474568 | tf_op jit(solution)/shard_map/ppermute | solution.py:22
  373.6 13.8 %collective-permute-start.28 = (bf16[1920,512]{1,0:T(8,128)(2,1)S(1)}, bf16[1920,512]{1,0:T(8,128)(2,1)S(1)}, u32[]{:S(2)}, u32[]{:S(2)}) collective-permute-start(bf16[1920,512]{1,0:T(8,128)(2,1)S(1)} %pad_maximum_fusion), channel_id=1, source_target_pairs={{0,1},{1,0},{2,3},{3,2},{4,5},{5,4},{6,7},{7,6},{8,9},{9,8},{10,11... | collective-permute-start | bytes 5898248 | tf_op jit(solution)/shard_map/ppermute | solution.py:31
  (39 other events, 843.2 us)
Sparse Core Ops, SparseCore 0:
  16.7 114.9 all-gather.5
  141.3 121.3 all-gather.3

commit v7 on v6

--- a/solution.py
+++ b/solution.py
@@ -440,11 +440,13 @@
     tp_device = lax.axis_index("tp")
 
     groups = group_count(local_width)
-    orders = [masks if group in (0, 3) else [2, 1] + masks[2:] for group in range(groups)]
-    slots = []
-    for order in orders:
-        slot = sum(jnp.where((apart & m) > 0, size >> (i + 1), 0) for i, m in enumerate(order))
-        slots.append(jnp.concatenate([slot, beyond]))
+    gather_order = [2, 1] + masks[2:]
+    slots, gather_slots = [
+        jnp.concatenate(
+            [sum(jnp.where((apart & m) > 0, size >> (i + 1), 0) for i, m in enumerate(order)), beyond]
+        )
+        for order in (masks, gather_order)
+    ]
     gathered, near_keys, parts, stages = [None] * groups, [None] * groups, [None] * groups, []
     after = scales
     for group in [0, 2, 1, 3] if groups > 1 else [0]:
@@ -455,7 +457,7 @@
         if group % 2 == 0:
             continue
         held = parts[group][None]
-        for m in orders[group][:0:-1]:
+        for m in gather_order[:0:-1]:
             held = lax.optimization_barrier(jnp.concatenate([held, send_xor(held, m)], axis=0))
             stages.append(held)
             if held.shape[0] == line:
@@ -481,8 +483,8 @@
 
     last = len(masks) - 1
     if groups > 1:
-        turns = ("a1", "a0", "c1", "a2", "c1", "c0", "a3", "c2", "c1", "c0", "c3", "c2", "l1", "c0", "c3")
-        turns += ("c2", "l0", "c3", "l2", "l3")
+        turns = ("a1", "a0", "c1", "a2", "c0", "c1", "a3", "c2", "c0", "c1", "c0", "c2", "l1", "c3", "l0")
+        turns += ("c2", "c3", "l2", "c3", "l3")
     else:
         turns = ("a0",) + ("c0",) * last + ("l0",)
     state, stage, attended = {}, {}, []
@@ -495,13 +497,12 @@
         step, names = turn_name[0], turn_name[1:]
         if step == "a":
             group = int(names)
-            order = orders[group]
             if group % 2 == 0:
                 q_parts = [whole_blocks]
             else:
-                q_parts = [gathered[group], send_xor(gathered[group], order[0])]
+                q_parts = [gathered[group], send_xor(gathered[group], gather_order[0])]
             state[names] = attend(
-                group, table, slots[group], natural if group % 2 == 0 else slots[group], q_parts,
+                group, table, slots, natural if group % 2 == 0 else gather_slots, q_parts,
                 cache_keys, cache_values, near_keys[group], new_values, near_starts,
                 (before, waits[group]),
             )
@@ -517,11 +518,13 @@
         pairs = []
         for part in parts:
             keep, send = state[part]
-            pairs.append((keep, send_xor(send, orders[int(part[0])][stage[part]])))
+            pairs.append((keep, send_xor(send, masks[stage[part]])))
         stage[names] = stage[parts[0]] + 1
         if step == "c":
             state[names] = combine(pairs, before)
-            before = latest = state[names][0]
+            before = state[names][0]
+            if stage[names] == last - 1:
+                latest = before
             if weights is None and names in ("3", str(groups - 1)):
                 weights = swap_weights(weight, before)
         else:

time: 409 us -> 364 us (0.89)
  waiting for transfers between devices: 196 us -> 155 us
  starting transfers between devices: 49.8 us -> 45.3 us
    ppermute x33, waiting for transfers between devices: 196 us -> 155 us  [send_xor(): return lax.ppermute(value, 'req', [(i, i ^ by) for i in range(size)])]
    ppermute x33, starting transfers between devices: 49.5 us -> 45 us  [send_xor(): return lax.ppermute(value, 'req', [(i, i ^ by) for i in range(size)])]
  transfers between devices with their start and end apart: 38 -> 38, of which waited for: 22 -> 21; matrix products, arithmetic and copies ran while one was open for 5% -> 5% of each run, Pallas kernels for 28% -> 31%
where the time goes in v7:
time: 364 us
  waiting for transfers between devices  155 us (43%)
  Pallas kernels  114 us (31%)
  starting transfers between devices  45.3 us (12%)
  other arithmetic  15.5 us (4%)
  between operations  14 us (4%)
  local copies, waits for them, and re-layouts  10.6 us (3%)
  matrix products  6.1 us (2%)
  blocking collectives  3.87 us (1%)
    ppermute x33, waiting for transfers between devices, send_xor(): return lax.ppermute(value, 'req', [(i, i ^ by) for i in range(size)])  155 us
    pallas_call x4, Pallas kernels, attend(): pl.pallas_call(functools.partial(attend_kernel, q_column), grid_spec=pltp...  98 us
    ppermute x33, starting transfers between devices, send_xor(): return lax.ppermute(value, 'req', [(i, i ^ by) for i in range(size)])  45 us
    pallas_call x12, Pallas kernels, combine(): pl.pallas_call(combine_kernel, grid=(half,), in_specs=[low, high, low, hi...  12.9 us
  transfers between devices with their start and end apart: 38, of which 21 were waited for; matrix products, arithmetic and copies ran while one was open for 5% of the time, Pallas kernels for 31%

profile of v7, /device:TPU:0, one launch (start us, length us, event | category | flops | bytes accessed | tf_op | source)
XLA Modules:
  0.0 363.7 jit_solution(1523363203025171310)
XLA Ops:
  10.4 3.9 %psum.7 = f32[128,2]{1,0:T(8,128)S(1)} all-reduce(f32[128,2]{1,0:T(8,128)S(1)} %copy.43), channel_id=1, replica_groups=mesh['req'=16,'tp'=2] {'tp'}, use_global_device_ids=true, to_apply=%region_9.10 | all-reduce | flops 256 | bytes 2048 | tf_op jit(solution)/shard_map/psum | solution.py:394
  17.0 3.8 %collective-permute-start = (bf16[1,128,640]{2,1,0:T(8,128)(2,1)S(1)}, bf16[1,128,640]{2,1,0:T(8,128)(2,1)S(1)}, u32[]{:S(2)}, u32[]{:S(2)}) collective-permute-start(bf16[1,128,640]{2,1,0:T(8,128)(2,1)S(1)} %bitcast.42), channel_id=1, source_target_pairs={{0,16},{2,18},{4,20},{6,22},{8,24},{10,26},{12,28},{14,30},{16,0},... | collective-permute-start | bytes 491528 | tf_op jit(solution)/shard_map/ppermute | solution.py:22
  20.8 8.2 %collective-permute-done = bf16[1,128,640]{2,1,0:T(8,128)(2,1)S(1)} collective-permute-done((bf16[1,128,640]{2,1,0:T(8,128)(2,1)S(1)}, bf16[1,128,640]{2,1,0:T(8,128)(2,1)S(1)}, u32[]{:S(2)}, u32[]{:S(2)}) %collective-permute-start) | collective-permute-done | bytes 163872 | tf_op jit(solution)/shard_map/ppermute | solution.py:22
  30.2 14.6 %collective-permute-done.1 = bf16[2,128,640]{2,1,0:T(8,128)(2,1)S(1)} collective-permute-done((bf16[2,128,640]{2,1,0:T(8,128)(2,1)S(1)}, bf16[2,128,640]{2,1,0:T(8,128)(2,1)S(1)}, u32[]{:S(2)}, u32[]{:S(2)}) %collective-permute-start.1) | collective-permute-done | bytes 327712 | tf_op jit(solution)/shard_map/ppermute | solution.py:22
  46.8 23.9 %collective-permute-done.2 = bf16[4,128,640]{2,1,0:T(8,128)(2,1)S(1)} collective-permute-done((bf16[4,128,640]{2,1,0:T(8,128)(2,1)S(1)}, bf16[4,128,640]{2,1,0:T(8,128)(2,1)S(1)}, u32[]{:S(2)}, u32[]{:S(2)}) %collective-permute-start.2) | collective-permute-done | bytes 655392 | tf_op jit(solution)/shard_map/ppermute | solution.py:22
  77.4 7.9 %collective-permute-done.4 = bf16[1,128,640]{2,1,0:T(8,128)(2,1)S(1)} collective-permute-done((bf16[1,128,640]{2,1,0:T(8,128)(2,1)S(1)}, bf16[1,128,640]{2,1,0:T(8,128)(2,1)S(1)}, u32[]{:S(2)}, u32[]{:S(2)}) %collective-permute-start.4) | collective-permute-done | bytes 163872 | tf_op jit(solution)/shard_map/ppermute | solution.py:22
  86.8 21.7 %collective-permute-done.5 = bf16[2,128,640]{2,1,0:T(8,128)(2,1)S(1)} collective-permute-done((bf16[2,128,640]{2,1,0:T(8,128)(2,1)S(1)}, bf16[2,128,640]{2,1,0:T(8,128)(2,1)S(1)}, u32[]{:S(2)}, u32[]{:S(2)}) %collective-permute-start.5) | collective-permute-done | bytes 327712 | tf_op jit(solution)/shard_map/ppermute | solution.py:22
  109.3 4.1 %collective-permute-done.3.refs_1_ = bf16[8,128,640]{2,1,0:T(8,128)(2,1)} collective-permute-done((bf16[8,128,640]{2,1,0:T(8,128)(2,1)S(1)}, bf16[8,128,640]{2,1,0:T(8,128)(2,1)}, u32[]{:S(2)}, u32[]{:S(2)}) %collective-permute-start.3) | collective-permute-done | bytes 1310752 | tf_op jit(solution)/shard_map/ppermute | solution.py:22
  113.5 24.5 %cache_attend.4 = (bf16[8,672,128]{2,1,0:T(8,128)(2,1)}, bf16[8,672,128]{2,1,0:T(8,128)(2,1)}) custom-call(s32[64]{0:T(128)} %reshape.325.table_ref, s32[18]{0:T(128)} %fusion.15.slot_ref, s32[18]{0:T(128)} %fusion.16.q_slot_ref, bf16[8,128,640]{2,1,0:T(8,128)(2,1)} %copy-done.19, bf16[8,128,640]{2,1,0:T(8,128)(2,1)} %collective-permute-done.3.refs_1_, ...), custom_call_target="tpu_custom_call" | custom-call | flops 5368709120 | bytes 10485760 | tf_op jit(solution)/shard_map/cache_attend/pallas_call | solution.py:243
  142.8 24.6 %cache_attend.5 = (bf16[8,672,128]{2,1,0:T(8,128)(2,1)}, bf16[8,672,128]{2,1,0:T(8,128)(2,1)}) custom-call(s32[64]{0:T(128)} %reshape.325.table_ref, s32[18]{0:T(128)} %fusion.15.slot_ref, s32[18]{0:T(128)} %fusion.17.q_slot_ref, bf16[16,128,1280]{2,1,0:T(8,128)(2,1)} %bitcast.44, bf16[16,256,2560]{2,1,0:T(8,128)(2,1)} %refs_2_.7, ...), custom_call_target="tpu_custom_call" | custom-call | flops 5368709120 | bytes 10485760 | tf_op jit(solution)/shard_map/cache_attend/pallas_call | solution.py:243
  171.9 14.4 %collective-permute-done.8.refs_2_.refs_3_ = bf16[8,672,128]{2,1,0:T(8,128)(2,1)S(1)} collective-permute-done((bf16[8,672,128]{2,1,0:T(8,128)(2,1)S(1)}, bf16[8,672,128]{2,1,0:T(8,128)(2,1)S(1)}, u32[]{:S(2)}, u32[]{:S(2)}) %collective-permute-start.8) | collective-permute-done | bytes 1376288 | tf_op jit(solution)/shard_map/ppermute | solution.py:22
  189.4 24.4 %cache_attend.6 = (bf16[8,672,128]{2,1,0:T(8,128)(2,1)}, bf16[8,672,128]{2,1,0:T(8,128)(2,1)}) custom-call(s32[64]{0:T(128)} %reshape.325.table_ref, s32[18]{0:T(128)} %fusion.15.slot_ref, s32[18]{0:T(128)} %fusion.17.q_slot_ref, bf16[16,128,1280]{2,1,0:T(8,128)(2,1)} %bitcast.45, bf16[16,256,2560]{2,1,0:T(8,128)(2,1)} %refs_2_.7, ...), custom_call_target="tpu_custom_call" | custom-call | flops 5368709120 | bytes 10485760 | tf_op jit(solution)/shard_map/cache_attend/pallas_call | solution.py:243
  221.2 24.5 %cache_attend.7 = (bf16[8,672,128]{2,1,0:T(8,128)(2,1)}, bf16[8,672,128]{2,1,0:T(8,128)(2,1)}) custom-call(s32[64]{0:T(128)} %reshape.325.table_ref, s32[18]{0:T(128)} %fusion.15.slot_ref, s32[18]{0:T(128)} %fusion.16.q_slot_ref, bf16[8,128,640]{2,1,0:T(8,128)(2,1)} %pad_maximum_fusion.2.refs_0_, bf16[8,128,640]{2,1,0:T(8,128)(2,1)} %collective-permute-done.7.refs_1_, ...), custom_call_target="tpu_custom_call" | custom-call | flops 5368709120 | bytes 10485760 | tf_op jit(solution)/shard_map/cache_attend/pallas_call | solution.py:243
  252.1 7.4 %collective-permute-done.13.refs_2_.refs_3_ = bf16[4,672,128]{2,1,0:T(8,128)(2,1)S(1)} collective-permute-done((bf16[4,672,128]{2,1,0:T(8,128)(2,1)}, bf16[4,672,128]{2,1,0:T(8,128)(2,1)S(1)}, u32[]{:S(2)}, u32[]{:S(2)}) %collective-permute-start.13) | collective-permute-done | bytes 688160 | tf_op jit(solution)/shard_map/ppermute | solution.py:22
  260.4 7.1 %collective-permute-done.12.refs_2_.refs_3_ = bf16[2,672,128]{2,1,0:T(8,128)(2,1)S(1)} collective-permute-done((bf16[2,672,128]{2,1,0:T(8,128)(2,1)}, bf16[2,672,128]{2,1,0:T(8,128)(2,1)S(1)}, u32[]{:S(2)}, u32[]{:S(2)}) %collective-permute-start.12) | collective-permute-done | bytes 344096 | tf_op jit(solution)/shard_map/ppermute | solution.py:22
  268.3 4.6 %collective-permute-start.15 = (bf16[1,672,128]{2,1,0:T(8,128)(2,1)}, bf16[1,672,128]{2,1,0:T(8,128)(2,1)}, u32[]{:S(2)}, u32[]{:S(2)}) collective-permute-start(bf16[1,672,128]{2,1,0:T(8,128)(2,1)} %get-tuple-element.80), channel_id=1, source_target_pairs={{0,16},{2,18},{4,20},{6,22},{8,24},{10,26},{12,28},{14,30},{16,0},... | collective-permute-start | bytes 516104 | tf_op jit(solution)/shard_map/ppermute | solution.py:22
  283.9 3.4 dynamic-slice_bitcast_fusion
  290.8 7.0 %collective-permute-done.19.refs_2_.refs_3_ = bf16[4,672,128]{2,1,0:T(8,128)(2,1)S(1)} collective-permute-done((bf16[4,672,128]{2,1,0:T(8,128)(2,1)}, bf16[4,672,128]{2,1,0:T(8,128)(2,1)S(1)}, u32[]{:S(2)}, u32[]{:S(2)}) %collective-permute-start.19) | collective-permute-done | bytes 688160 | tf_op jit(solution)/shard_map/ppermute | solution.py:22
  303.8 2.9 collective-permute-done.25.refs_2_.refs_3_
  307.0 7.6 %collective-permute-done.26.got_ref = bf16[1,672,128]{2,1,0:T(8,128)(2,1)S(1)} collective-permute-done((bf16[1,672,128]{2,1,0:T(8,128)(2,1)S(1)}, bf16[1,672,128]{2,1,0:T(8,128)(2,1)S(1)}, u32[]{:S(2)}, u32[]{:S(2)}) %collective-permute-start.26) | collective-permute-done | bytes 172064 | tf_op jit(solution)/shard_map/ppermute | solution.py:22
  314.7 10.9 %collective-permute-done.23 = bf16[1920,128]{1,0:T(8,128)(2,1)S(1)} collective-permute-done((bf16[1920,128]{1,0:T(8,128)(2,1)S(1)}, bf16[1920,128]{1,0:T(8,128)(2,1)S(1)}, u32[]{:S(2)}, u32[]{:S(2)}) %collective-permute-start.23) | collective-permute-done | bytes 491552 | tf_op jit(solution)/shard_map/ppermute | solution.py:22
  325.6 3.2 pad_maximum_fusion
  336.2 3.1 collective-permute-done.31
  346.1 6.6 %collective-permute-done.34 = bf16[640,128]{1,0:T(8,128)(2,1)S(1)} collective-permute-done((bf16[640,128]{1,0:T(8,128)(2,1)S(1)}, bf16[640,128]{1,0:T(8,128)(2,1)S(1)}, u32[]{:S(2)}, u32[]{:S(2)}) %collective-permute-start.34) | collective-permute-done | bytes 163872 | tf_op jit(solution)/shard_map/ppermute | solution.py:22
  (192 shorter events, 85.3 us)
Async XLA Ops:
  6.6 136.2 %all-gather.6.cloned.1.call-start = ((), (), s32[]{:S(2)}) async-start(), calls=%async_computation.1 | async-start | bytes 5570560 | tf_op jit(solution)/shard_map/all_gather | solution.py:466
  16.6 267.3 %all-gather.4.cloned.1.call-start = ((), (), s32[]{:S(2)}) async-start(), calls=%async_computation | async-start | bytes 8192000 | tf_op jit(solution)/shard_map/all_gather | solution.py:473
  17.0 12.0 %collective-permute-start = (bf16[1,128,640]{2,1,0:T(8,128)(2,1)S(1)}, bf16[1,128,640]{2,1,0:T(8,128)(2,1)S(1)}, u32[]{:S(2)}, u32[]{:S(2)}) collective-permute-start(bf16[1,128,640]{2,1,0:T(8,128)(2,1)S(1)} %bitcast.42), channel_id=1, source_target_pairs={{0,16},{2,18},{4,20},{6,22},{8,24},{10,26},{12,28},{14,30},{16,0},... | collective-permute-start | bytes 491528 | tf_op jit(solution)/shard_map/ppermute | solution.py:22
  29.1 15.6 %collective-permute-start.1 = (bf16[2,128,640]{2,1,0:T(8,128)(2,1)S(1)}, bf16[2,128,640]{2,1,0:T(8,128)(2,1)S(1)}, u32[]{:S(2)}, u32[]{:S(2)}) collective-permute-start(bf16[2,128,640]{2,1,0:T(8,128)(2,1)S(1)} %pad_maximum_fusion.8), channel_id=1, source_target_pairs={{0,8},{2,10},{4,12},{6,14},{8,0},{10,2},{12,4},{14,6},{16,24},{18,... | collective-permute-start | bytes 983048 | tf_op jit(solution)/shard_map/ppermute | solution.py:22
  44.8 25.9 %collective-permute-start.2 = (bf16[4,128,640]{2,1,0:T(8,128)(2,1)S(1)}, bf16[4,128,640]{2,1,0:T(8,128)(2,1)S(1)}, u32[]{:S(2)}, u32[]{:S(2)}) collective-permute-start(bf16[4,128,640]{2,1,0:T(8,128)(2,1)S(1)} %pad_maximum_fusion.4._), channel_id=1, source_target_pairs={{0,2},{2,0},{4,6},{6,4},{8,10},{10,8},{12,14},{14,12},{16,18},{18,... | collective-permute-start | bytes 1966088 | tf_op jit(solution)/shard_map/ppermute | solution.py:22
  70.9 42.6 %collective-permute-start.3 = (bf16[8,128,640]{2,1,0:T(8,128)(2,1)S(1)}, bf16[8,128,640]{2,1,0:T(8,128)(2,1)}, u32[]{:S(2)}, u32[]{:S(2)}) collective-permute-start(bf16[8,128,640]{2,1,0:T(8,128)(2,1)S(1)} %pad_maximum_fusion.1.refs_0_), channel_id=1, source_target_pairs={{0,4},{2,6},{4,0},{6,2},{8,12},{10,14},{12,8},{14,10},{16,20},{18,... | collective-permute-start | bytes 3932168 | tf_op jit(solution)/shard_map/ppermute | solution.py:22
  85.4 23.1 %collective-permute-start.5 = (bf16[2,128,640]{2,1,0:T(8,128)(2,1)S(1)}, bf16[2,128,640]{2,1,0:T(8,128)(2,1)S(1)}, u32[]{:S(2)}, u32[]{:S(2)}) collective-permute-start(bf16[2,128,640]{2,1,0:T(8,128)(2,1)S(1)} %pad_maximum_fusion.9), channel_id=1, source_target_pairs={{0,8},{2,10},{4,12},{6,14},{8,0},{10,2},{12,4},{14,6},{16,24},{18,... | collective-permute-start | bytes 983048 | tf_op jit(solution)/shard_map/ppermute | solution.py:22
  138.0 31.4 %collective-permute-start.6 = (bf16[4,128,640]{2,1,0:T(8,128)(2,1)}, bf16[4,128,640]{2,1,0:T(8,128)(2,1)}, u32[]{:S(2)}, u32[]{:S(2)}) collective-permute-start(bf16[4,128,640]{2,1,0:T(8,128)(2,1)} %pad_maximum_fusion.5.refs_8_), channel_id=1, source_target_pairs={{0,2},{2,0},{4,6},{6,4},{8,10},{10,8},{12,14},{14,12},{16,18},{18,... | collective-permute-start | bytes 1966088 | tf_op jit(solution)/shard_map/ppermute | solution.py:22
  140.9 45.4 %collective-permute-start.8 = (bf16[8,672,128]{2,1,0:T(8,128)(2,1)S(1)}, bf16[8,672,128]{2,1,0:T(8,128)(2,1)S(1)}, u32[]{:S(2)}, u32[]{:S(2)}) collective-permute-start(bf16[8,672,128]{2,1,0:T(8,128)(2,1)S(1)} %copy-done.28), channel_id=1, source_target_pairs={{0,2},{2,0},{4,6},{6,4},{8,10},{10,8},{12,14},{14,12},{16,18},{18,... | collective-permute-start | bytes 4128776 | tf_op jit(solution)/shard_map/ppermute | solution.py:22
  167.4 49.1 %collective-permute-start.10 = (bf16[8,672,128]{2,1,0:T(8,128)(2,1)}, bf16[8,672,128]{2,1,0:T(8,128)(2,1)S(1)}, u32[]{:S(2)}, u32[]{:S(2)}) collective-permute-start(bf16[8,672,128]{2,1,0:T(8,128)(2,1)} %get-tuple-element.68), channel_id=1, source_target_pairs={{0,2},{2,0},{4,6},{6,4},{8,10},{10,8},{12,14},{14,12},{16,18},{18,... | collective-permute-start | bytes 4128776 | tf_op jit(solution)/shard_map/ppermute | solution.py:22
  171.9 49.3 %collective-permute-start.7 = (bf16[8,128,640]{2,1,0:T(8,128)(2,1)}, bf16[8,128,640]{2,1,0:T(8,128)(2,1)}, u32[]{:S(2)}, u32[]{:S(2)}) collective-permute-start(bf16[8,128,640]{2,1,0:T(8,128)(2,1)} %pad_maximum_fusion.2.refs_0_), channel_id=1, source_target_pairs={{0,4},{2,6},{4,0},{6,2},{8,12},{10,14},{12,8},{14,10},{16,20},{18,... | collective-permute-start | bytes 3932168 | tf_op jit(solution)/shard_map/ppermute | solution.py:22
  188.8 30.7 %collective-permute-start.9 = (bf16[4,672,128]{2,1,0:T(8,128)(2,1)}, bf16[4,672,128]{2,1,0:T(8,128)(2,1)S(1)}, u32[]{:S(2)}, u32[]{:S(2)}) collective-permute-start(bf16[4,672,128]{2,1,0:T(8,128)(2,1)} %get-tuple-element.67), channel_id=1, source_target_pairs={{0,4},{2,6},{4,0},{6,2},{8,12},{10,14},{12,8},{14,10},{16,20},{18,... | collective-permute-start | bytes 2064392 | tf_op jit(solution)/shard_map/ppermute | solution.py:22
  213.7 33.2 %collective-permute-start.14 = (bf16[8,672,128]{2,1,0:T(8,128)(2,1)}, bf16[8,672,128]{2,1,0:T(8,128)(2,1)S(1)}, u32[]{:S(2)}, u32[]{:S(2)}) collective-permute-start(bf16[8,672,128]{2,1,0:T(8,128)(2,1)} %get-tuple-element.76), channel_id=1, source_target_pairs={{0,2},{2,0},{4,6},{6,4},{8,10},{10,8},{12,14},{14,12},{16,18},{18,... | collective-permute-start | bytes 4128776 | tf_op jit(solution)/shard_map/ppermute | solution.py:22
  245.7 34.9 %collective-permute-start.11 = (bf16[8,672,128]{2,1,0:T(8,128)(2,1)}, bf16[8,672,128]{2,1,0:T(8,128)(2,1)S(1)}, u32[]{:S(2)}, u32[]{:S(2)}) collective-permute-start(bf16[8,672,128]{2,1,0:T(8,128)(2,1)} %get-tuple-element.73), channel_id=1, source_target_pairs={{0,2},{2,0},{4,6},{6,4},{8,10},{10,8},{12,14},{14,12},{16,18},{18,... | collective-permute-start | bytes 4128776 | tf_op jit(solution)/shard_map/ppermute | solution.py:22
  247.0 12.5 %collective-permute-start.13 = (bf16[4,672,128]{2,1,0:T(8,128)(2,1)}, bf16[4,672,128]{2,1,0:T(8,128)(2,1)S(1)}, u32[]{:S(2)}, u32[]{:S(2)}) collective-permute-start(bf16[4,672,128]{2,1,0:T(8,128)(2,1)} %get-tuple-element.75), channel_id=1, source_target_pairs={{0,4},{2,6},{4,0},{6,2},{8,12},{10,14},{12,8},{14,10},{16,20},{18,... | collective-permute-start | bytes 2064392 | tf_op jit(solution)/shard_map/ppermute | solution.py:22
  250.0 25.7 %collective-permute-start.16 = (bf16[4,672,128]{2,1,0:T(8,128)(2,1)}, bf16[4,672,128]{2,1,0:T(8,128)(2,1)S(1)}, u32[]{:S(2)}, u32[]{:S(2)}) collective-permute-start(bf16[4,672,128]{2,1,0:T(8,128)(2,1)} %get-tuple-element.81), channel_id=1, source_target_pairs={{0,4},{2,6},{4,0},{6,2},{8,12},{10,14},{12,8},{14,10},{16,20},{18,... | collective-permute-start | bytes 2064392 | tf_op jit(solution)/shard_map/ppermute | solution.py:22
  252.0 15.5 %collective-permute-start.12 = (bf16[2,672,128]{2,1,0:T(8,128)(2,1)}, bf16[2,672,128]{2,1,0:T(8,128)(2,1)S(1)}, u32[]{:S(2)}, u32[]{:S(2)}) collective-permute-start(bf16[2,672,128]{2,1,0:T(8,128)(2,1)} %get-tuple-element.74), channel_id=1, source_target_pairs={{0,8},{2,10},{4,12},{6,14},{8,0},{10,2},{12,4},{14,6},{16,24},{18,... | collective-permute-start | bytes 1032200 | tf_op jit(solution)/shard_map/ppermute | solution.py:22
  260.4 13.5 %collective-permute-start.17 = (bf16[2,672,128]{2,1,0:T(8,128)(2,1)}, bf16[2,672,128]{2,1,0:T(8,128)(2,1)}, u32[]{:S(2)}, u32[]{:S(2)}) collective-permute-start(bf16[2,672,128]{2,1,0:T(8,128)(2,1)} %get-tuple-element.82), channel_id=1, source_target_pairs={{0,8},{2,10},{4,12},{6,14},{8,0},{10,2},{12,4},{14,6},{16,24},{18,... | collective-permute-start | bytes 1032200 | tf_op jit(solution)/shard_map/ppermute | solution.py:22
  276.7 12.4 %collective-permute-start.20 = (bf16[2,672,128]{2,1,0:T(8,128)(2,1)}, bf16[2,672,128]{2,1,0:T(8,128)(2,1)S(1)}, u32[]{:S(2)}, u32[]{:S(2)}) collective-permute-start(bf16[2,672,128]{2,1,0:T(8,128)(2,1)} %get-tuple-element.89), channel_id=1, source_target_pairs={{0,8},{2,10},{4,12},{6,14},{8,0},{10,2},{12,4},{14,6},{16,24},{18,... | collective-permute-start | bytes 1032200 | tf_op jit(solution)/shard_map/ppermute | solution.py:22
  282.4 15.4 %collective-permute-start.19 = (bf16[4,672,128]{2,1,0:T(8,128)(2,1)}, bf16[4,672,128]{2,1,0:T(8,128)(2,1)S(1)}, u32[]{:S(2)}, u32[]{:S(2)}) collective-permute-start(bf16[4,672,128]{2,1,0:T(8,128)(2,1)} %get-tuple-element.88), channel_id=1, source_target_pairs={{0,4},{2,6},{4,0},{6,2},{8,12},{10,14},{12,8},{14,10},{16,20},{18,... | collective-permute-start | bytes 2064392 | tf_op jit(solution)/shard_map/ppermute | solution.py:22
  287.3 52.9 %collective-permute-start.27 = (bf16[640,2560]{1,0:T(8,128)(2,1)S(1)}, bf16[640,2560]{1,0:T(8,128)(2,1)S(1)}, u32[]{:S(2)}, u32[]{:S(2)}) collective-permute-start(bf16[640,2560]{1,0:T(8,128)(2,1)S(1)} %get-tuple-element.109), channel_id=1, source_target_pairs={{0,1},{1,0},{2,3},{3,2},{4,5},{5,4},{6,7},{7,6},{8,9},{9,8},{10,11... | collective-permute-start | bytes 9830408 | tf_op jit(solution)/shard_map/ppermute | solution.py:31
  299.6 15.1 %collective-permute-start.22 = (bf16[1920,128]{1,0:T(8,128)(2,1)S(1)}, bf16[1920,128]{1,0:T(8,128)(2,1)S(1)}, u32[]{:S(2)}, u32[]{:S(2)}) collective-permute-start(bf16[1920,128]{1,0:T(8,128)(2,1)S(1)} %pad_maximum_fusion.7), channel_id=1, source_target_pairs={{0,2},{2,0},{4,6},{6,4},{8,10},{10,8},{12,14},{14,12},{16,18},{18,... | collective-permute-start | bytes 1474568 | tf_op jit(solution)/shard_map/ppermute | solution.py:22
  302.2 23.3 %collective-permute-start.23 = (bf16[1920,128]{1,0:T(8,128)(2,1)S(1)}, bf16[1920,128]{1,0:T(8,128)(2,1)S(1)}, u32[]{:S(2)}, u32[]{:S(2)}) collective-permute-start(bf16[1920,128]{1,0:T(8,128)(2,1)S(1)} %pad_maximum_fusion.7), channel_id=1, source_target_pairs={{0,4},{2,6},{4,0},{6,2},{8,12},{10,14},{12,8},{14,10},{16,20},{18,... | collective-permute-start | bytes 1474568 | tf_op jit(solution)/shard_map/ppermute | solution.py:22
  303.1 22.4 %collective-permute-start.24 = (bf16[1920,128]{1,0:T(8,128)(2,1)S(1)}, bf16[1920,128]{1,0:T(8,128)(2,1)S(1)}, u32[]{:S(2)}, u32[]{:S(2)}) collective-permute-start(bf16[1920,128]{1,0:T(8,128)(2,1)S(1)} %pad_maximum_fusion.7), channel_id=1, source_target_pairs={{0,6},{2,4},{4,2},{6,0},{8,14},{10,12},{12,10},{14,8},{16,22},{18,... | collective-permute-start | bytes 1474568 | tf_op jit(solution)/shard_map/ppermute | solution.py:22
  (43 other events, 756.8 us)
Sparse Core Ops, SparseCore 0:
  16.7 113.6 all-gather.5
  138.1 128.9 all-gather.3

commit v8 on v7

--- a/solution.py
+++ b/solution.py
@@ -483,7 +483,7 @@
 
     last = len(masks) - 1
     if groups > 1:
-        turns = ("a1", "a0", "c1", "a2", "c0", "c1", "a3", "c2", "c0", "c1", "c0", "c2", "l1", "c3", "l0")
+        turns = ("a1", "a0", "c1", "a2", "c0", "c1", "a3", "c2", "c0", "c1", "c3", "c0", "c2", "l1", "l0")
         turns += ("c2", "c3", "l2", "c3", "l3")
     else:
         turns = ("a0",) + ("c0",) * last + ("l0",)
@@ -491,7 +491,8 @@
     before = near_starts
     waits = [near_starts] * 4
     if groups > 1:
-        waits[1] = stages[-2]
+        waits[1] = stages[-1]
+        gathered[1], _ = lax.optimization_barrier((gathered[1], stages[-2]))
     weight, weights = None, None
     for turn_name in turns:
         step, names = turn_name[0], turn_name[1:]

time: 364 us -> 371 us (1.019)
  starting transfers between devices: 45.3 us -> 51.5 us
    ppermute x33, starting transfers between devices: 45 us -> 51.2 us  [send_xor(): return lax.ppermute(value, 'req', [(i, i ^ by) for i in range(size)])]
  transfers between devices with their start and end apart: 38 -> 38, of which waited for: 21 -> 22; matrix products, arithmetic and copies ran while one was open for 5% -> 4% of each run, Pallas kernels for 31% -> 30%
where the time goes in v8:
time: 371 us; the launch traced here: 368 us
  waiting for transfers between devices  156 us (42%)
  Pallas kernels  112 us (30%)
  starting transfers between devices  51.5 us (14%)
  between operations  14 us (4%)
  other arithmetic  13.4 us (4%)
  local copies, waits for them, and re-layouts  11.3 us (3%)
  matrix products  6.05 us (2%)
  blocking collectives  3.86 us (1%)
    ppermute x33, waiting for transfers between devices, send_xor(): return lax.ppermute(value, 'req', [(i, i ^ by) for i in range(size)])  156 us
    pallas_call x4, Pallas kernels, attend(): pl.pallas_call(functools.partial(attend_kernel, q_column), grid_spec=pltp...  94.6 us
    ppermute x33, starting transfers between devices, send_xor(): return lax.ppermute(value, 'req', [(i, i ^ by) for i in range(size)])  51.2 us
    pallas_call x12, Pallas kernels, combine(): pl.pallas_call(combine_kernel, grid=(half,), in_specs=[low, high, low, hi...  14.8 us
  transfers between devices with their start and end apart: 38, of which 22 were waited for; matrix products, arithmetic and copies ran while one was open for 4% of the time, Pallas kernels for 30%

profile of v8, /device:TPU:0, one launch (start us, length us, event | category | flops | bytes accessed | tf_op | source)
XLA Modules:
  0.0 367.8 jit_solution(1781297130678217630)
XLA Ops:
  10.4 3.9 %psum.7 = f32[128,2]{1,0:T(8,128)S(1)} all-reduce(f32[128,2]{1,0:T(8,128)S(1)} %copy.43), channel_id=1, replica_groups=mesh['req'=16,'tp'=2] {'tp'}, use_global_device_ids=true, to_apply=%region_9.10 | all-reduce | flops 256 | bytes 2048 | tf_op jit(solution)/shard_map/psum | solution.py:394
  17.0 3.8 %collective-permute-start = (bf16[1,128,640]{2,1,0:T(8,128)(2,1)S(1)}, bf16[1,128,640]{2,1,0:T(8,128)(2,1)S(1)}, u32[]{:S(2)}, u32[]{:S(2)}) collective-permute-start(bf16[1,128,640]{2,1,0:T(8,128)(2,1)S(1)} %bitcast.42), channel_id=1, source_target_pairs={{0,16},{2,18},{4,20},{6,22},{8,24},{10,26},{12,28},{14,30},{16,0},... | collective-permute-start | bytes 491528 | tf_op jit(solution)/shard_map/ppermute | solution.py:22
  20.8 8.2 %collective-permute-done = bf16[1,128,640]{2,1,0:T(8,128)(2,1)S(1)} collective-permute-done((bf16[1,128,640]{2,1,0:T(8,128)(2,1)S(1)}, bf16[1,128,640]{2,1,0:T(8,128)(2,1)S(1)}, u32[]{:S(2)}, u32[]{:S(2)}) %collective-permute-start) | collective-permute-done | bytes 163872 | tf_op jit(solution)/shard_map/ppermute | solution.py:22
  29.9 14.8 %collective-permute-done.1 = bf16[2,128,640]{2,1,0:T(8,128)(2,1)S(1)} collective-permute-done((bf16[2,128,640]{2,1,0:T(8,128)(2,1)S(1)}, bf16[2,128,640]{2,1,0:T(8,128)(2,1)S(1)}, u32[]{:S(2)}, u32[]{:S(2)}) %collective-permute-start.1) | collective-permute-done | bytes 327712 | tf_op jit(solution)/shard_map/ppermute | solution.py:22
  49.3 11.9 %collective-permute-done.3 = bf16[1,128,640]{2,1,0:T(8,128)(2,1)S(1)} collective-permute-done((bf16[1,128,640]{2,1,0:T(8,128)(2,1)S(1)}, bf16[1,128,640]{2,1,0:T(8,128)(2,1)S(1)}, u32[]{:S(2)}, u32[]{:S(2)}) %collective-permute-start.3) | collective-permute-done | bytes 163872 | tf_op jit(solution)/shard_map/ppermute | solution.py:22
  62.3 11.0 %collective-permute-done.4 = bf16[2,128,640]{2,1,0:T(8,128)(2,1)S(1)} collective-permute-done((bf16[2,128,640]{2,1,0:T(8,128)(2,1)S(1)}, bf16[2,128,640]{2,1,0:T(8,128)(2,1)S(1)}, u32[]{:S(2)}, u32[]{:S(2)}) %collective-permute-start.4) | collective-permute-done | bytes 327712 | tf_op jit(solution)/shard_map/ppermute | solution.py:22
  82.2 21.2 %collective-permute-done.6 = bf16[4,128,640]{2,1,0:T(8,128)(2,1)S(1)} collective-permute-done((bf16[4,128,640]{2,1,0:T(8,128)(2,1)S(1)}, bf16[4,128,640]{2,1,0:T(8,128)(2,1)S(1)}, u32[]{:S(2)}, u32[]{:S(2)}) %collective-permute-start.6) | collective-permute-done | bytes 655392 | tf_op jit(solution)/shard_map/ppermute | solution.py:22
  104.6 17.9 %collective-permute-done.5.refs_1_ = bf16[8,128,640]{2,1,0:T(8,128)(2,1)} collective-permute-done((bf16[8,128,640]{2,1,0:T(8,128)(2,1)S(1)}, bf16[8,128,640]{2,1,0:T(8,128)(2,1)}, u32[]{:S(2)}, u32[]{:S(2)}) %collective-permute-start.5) | collective-permute-done | bytes 1310752 | tf_op jit(solution)/shard_map/ppermute | solution.py:22
  122.5 23.5 %cache_attend.4 = (bf16[8,672,128]{2,1,0:T(8,128)(2,1)}, bf16[8,672,128]{2,1,0:T(8,128)(2,1)}) custom-call(s32[64]{0:T(128)} %reshape.325.table_ref, s32[18]{0:T(128)} %fusion.15.slot_ref, s32[18]{0:T(128)} %fusion.16.q_slot_ref, bf16[8,128,640]{2,1,0:T(8,128)(2,1)} %copy-done.21, bf16[8,128,640]{2,1,0:T(8,128)(2,1)} %collective-permute-done.5.refs_1_, ...), custom_call_target="tpu_custom_call" | custom-call | flops 5368709120 | bytes 10485760 | tf_op jit(solution)/shard_map/cache_attend/pallas_call | solution.py:243
  149.4 24.0 %cache_attend.5 = (bf16[8,672,128]{2,1,0:T(8,128)(2,1)}, bf16[8,672,128]{2,1,0:T(8,128)(2,1)}) custom-call(s32[64]{0:T(128)} %reshape.325.table_ref, s32[18]{0:T(128)} %fusion.15.slot_ref, s32[18]{0:T(128)} %fusion.17.q_slot_ref, bf16[16,128,1280]{2,1,0:T(8,128)(2,1)} %bitcast.44, bf16[16,256,2560]{2,1,0:T(8,128)(2,1)} %refs_2_.7, ...), custom_call_target="tpu_custom_call" | custom-call | flops 5368709120 | bytes 10485760 | tf_op jit(solution)/shard_map/cache_attend/pallas_call | solution.py:243
  180.9 3.5 collective-permute-start.9
  184.4 23.5 %cache_attend.6 = (bf16[8,672,128]{2,1,0:T(8,128)(2,1)}, bf16[8,672,128]{2,1,0:T(8,128)(2,1)}) custom-call(s32[64]{0:T(128)} %reshape.325.table_ref, s32[18]{0:T(128)} %fusion.15.slot_ref, s32[18]{0:T(128)} %fusion.17.q_slot_ref, bf16[16,128,1280]{2,1,0:T(8,128)(2,1)} %bitcast.45, bf16[16,256,2560]{2,1,0:T(8,128)(2,1)} %refs_2_.7, ...), custom_call_target="tpu_custom_call" | custom-call | flops 5368709120 | bytes 10485760 | tf_op jit(solution)/shard_map/cache_attend/pallas_call | solution.py:243
  216.0 23.5 %cache_attend.7 = (bf16[8,672,128]{2,1,0:T(8,128)(2,1)}, bf16[8,672,128]{2,1,0:T(8,128)(2,1)}) custom-call(s32[64]{0:T(128)} %reshape.325.table_ref, s32[18]{0:T(128)} %fusion.15.slot_ref, s32[18]{0:T(128)} %fusion.16.q_slot_ref, bf16[8,128,640]{2,1,0:T(8,128)(2,1)} %pad_maximum_fusion.2.refs_8_.refs_0_, ...), custom_call_target="tpu_custom_call" | custom-call | flops 5368709120 | bytes 10485760 | tf_op jit(solution)/shard_map/cache_attend/pallas_call | solution.py:243
  247.5 13.3 %collective-permute-done.13.refs_2_.refs_3_ = bf16[4,672,128]{2,1,0:T(8,128)(2,1)S(1)} collective-permute-done((bf16[4,672,128]{2,1,0:T(8,128)(2,1)}, bf16[4,672,128]{2,1,0:T(8,128)(2,1)S(1)}, u32[]{:S(2)}, u32[]{:S(2)}) %collective-permute-start.13) | collective-permute-done | bytes 688160 | tf_op jit(solution)/shard_map/ppermute | solution.py:22
  261.9 7.1 %collective-permute-done.12.refs_2_.refs_3_ = bf16[2,672,128]{2,1,0:T(8,128)(2,1)S(1)} collective-permute-done((bf16[2,672,128]{2,1,0:T(8,128)(2,1)}, bf16[2,672,128]{2,1,0:T(8,128)(2,1)S(1)}, u32[]{:S(2)}, u32[]{:S(2)}) %collective-permute-start.12) | collective-permute-done | bytes 344096 | tf_op jit(solution)/shard_map/ppermute | solution.py:22
  269.9 3.6 combine_pairs.18
  282.8 4.1 %collective-permute-start.16 = (bf16[1,672,128]{2,1,0:T(8,128)(2,1)}, bf16[1,672,128]{2,1,0:T(8,128)(2,1)S(1)}, u32[]{:S(2)}, u32[]{:S(2)}) collective-permute-start(bf16[1,672,128]{2,1,0:T(8,128)(2,1)} %get-tuple-element.86), channel_id=1, source_target_pairs={{0,16},{2,18},{4,20},{6,22},{8,24},{10,26},{12,28},{14,30},{16,0},... | collective-permute-start | bytes 516104 | tf_op jit(solution)/shard_map/ppermute | solution.py:22
  287.0 3.4 dynamic-slice_bitcast_fusion
  299.9 5.8 %collective-permute-done.21.got_ref = bf16[1,672,128]{2,1,0:T(8,128)(2,1)S(1)} collective-permute-done((bf16[1,672,128]{2,1,0:T(8,128)(2,1)S(1)}, bf16[1,672,128]{2,1,0:T(8,128)(2,1)S(1)}, u32[]{:S(2)}, u32[]{:S(2)}) %collective-permute-start.21) | collective-permute-done | bytes 172064 | tf_op jit(solution)/shard_map/ppermute | solution.py:22
  310.7 8.5 %collective-permute-done.26.got_ref = bf16[1,672,128]{2,1,0:T(8,128)(2,1)S(1)} collective-permute-done((bf16[1,672,128]{2,1,0:T(8,128)(2,1)S(1)}, bf16[1,672,128]{2,1,0:T(8,128)(2,1)S(1)}, u32[]{:S(2)}, u32[]{:S(2)}) %collective-permute-start.26) | collective-permute-done | bytes 172064 | tf_op jit(solution)/shard_map/ppermute | solution.py:22
  320.1 8.5 %collective-permute-done.23 = bf16[1920,128]{1,0:T(8,128)(2,1)S(1)} collective-permute-done((bf16[1920,128]{1,0:T(8,128)(2,1)S(1)}, bf16[1920,128]{1,0:T(8,128)(2,1)S(1)}, u32[]{:S(2)}, u32[]{:S(2)}) %collective-permute-start.23) | collective-permute-done | bytes 491552 | tf_op jit(solution)/shard_map/ppermute | solution.py:22
  328.6 3.2 pad_maximum_fusion
  338.9 4.4 %collective-permute-done.30 = bf16[640,128]{1,0:T(8,128)(2,1)S(1)} collective-permute-done((bf16[640,128]{1,0:T(8,128)(2,1)S(1)}, bf16[640,128]{1,0:T(8,128)(2,1)S(1)}, u32[]{:S(2)}, u32[]{:S(2)}) %collective-permute-start.30) | collective-permute-done | bytes 163872 | tf_op jit(solution)/shard_map/ppermute | solution.py:22
  350.1 6.6 %collective-permute-done.34 = bf16[640,128]{1,0:T(8,128)(2,1)S(1)} collective-permute-done((bf16[640,128]{1,0:T(8,128)(2,1)S(1)}, bf16[640,128]{1,0:T(8,128)(2,1)S(1)}, u32[]{:S(2)}, u32[]{:S(2)}) %collective-permute-start.34) | collective-permute-done | bytes 163872 | tf_op jit(solution)/shard_map/ppermute | solution.py:22
  (194 shorter events, 94.4 us)
Async XLA Ops:
  6.6 142.8 %all-gather.6.cloned.1.call-start = ((), (), s32[]{:S(2)}) async-start(), calls=%async_computation.1 | async-start | bytes 5570560 | tf_op jit(solution)/shard_map/all_gather | solution.py:466
  16.5 270.4 %all-gather.4.cloned.1.call-start = ((), (), s32[]{:S(2)}) async-start(), calls=%async_computation | async-start | bytes 8192000 | tf_op jit(solution)/shard_map/all_gather | solution.py:473
  29.1 15.6 %collective-permute-start.1 = (bf16[2,128,640]{2,1,0:T(8,128)(2,1)S(1)}, bf16[2,128,640]{2,1,0:T(8,128)(2,1)S(1)}, u32[]{:S(2)}, u32[]{:S(2)}) collective-permute-start(bf16[2,128,640]{2,1,0:T(8,128)(2,1)S(1)} %pad_maximum_fusion.8), channel_id=1, source_target_pairs={{0,8},{2,10},{4,12},{6,14},{8,0},{10,2},{12,4},{14,6},{16,24},{18,... | collective-permute-start | bytes 983048 | tf_op jit(solution)/shard_map/ppermute | solution.py:22
  45.2 16.1 %collective-permute-start.3 = (bf16[1,128,640]{2,1,0:T(8,128)(2,1)S(1)}, bf16[1,128,640]{2,1,0:T(8,128)(2,1)S(1)}, u32[]{:S(2)}, u32[]{:S(2)}) collective-permute-start(bf16[1,128,640]{2,1,0:T(8,128)(2,1)S(1)} %bitcast.40), channel_id=1, source_target_pairs={{0,16},{2,18},{4,20},{6,22},{8,24},{10,26},{12,28},{14,30},{16,0},... | collective-permute-start | bytes 491528 | tf_op jit(solution)/shard_map/ppermute | solution.py:22
  47.8 25.6 %collective-permute-start.2 = (bf16[4,128,640]{2,1,0:T(8,128)(2,1)S(1)}, bf16[4,128,640]{2,1,0:T(8,128)(2,1)S(1)}, u32[]{:S(2)}, u32[]{:S(2)}) collective-permute-start(bf16[4,128,640]{2,1,0:T(8,128)(2,1)S(1)} %pad_maximum_fusion.4._), channel_id=1, source_target_pairs={{0,2},{2,0},{4,6},{6,4},{8,10},{10,8},{12,14},{14,12},{16,18},{18,... | collective-permute-start | bytes 1966088 | tf_op jit(solution)/shard_map/ppermute | solution.py:22
  73.6 48.9 %collective-permute-start.5 = (bf16[8,128,640]{2,1,0:T(8,128)(2,1)S(1)}, bf16[8,128,640]{2,1,0:T(8,128)(2,1)}, u32[]{:S(2)}, u32[]{:S(2)}) collective-permute-start(bf16[8,128,640]{2,1,0:T(8,128)(2,1)S(1)} %pad_maximum_fusion.1.refs_0_), channel_id=1, source_target_pairs={{0,4},{2,6},{4,0},{6,2},{8,12},{10,14},{12,8},{14,10},{16,20},{18,... | collective-permute-start | bytes 3932168 | tf_op jit(solution)/shard_map/ppermute | solution.py:22
  77.3 26.1 %collective-permute-start.6 = (bf16[4,128,640]{2,1,0:T(8,128)(2,1)S(1)}, bf16[4,128,640]{2,1,0:T(8,128)(2,1)S(1)}, u32[]{:S(2)}, u32[]{:S(2)}) collective-permute-start(bf16[4,128,640]{2,1,0:T(8,128)(2,1)S(1)} %pad_maximum_fusion.5), channel_id=1, source_target_pairs={{0,2},{2,0},{4,6},{6,4},{8,10},{10,8},{12,14},{14,12},{16,18},{18,... | collective-permute-start | bytes 1966088 | tf_op jit(solution)/shard_map/ppermute | solution.py:22
  146.0 32.0 %collective-permute-start.8 = (bf16[8,672,128]{2,1,0:T(8,128)(2,1)}, bf16[8,672,128]{2,1,0:T(8,128)(2,1)S(1)}, u32[]{:S(2)}, u32[]{:S(2)}) collective-permute-start(bf16[8,672,128]{2,1,0:T(8,128)(2,1)} %get-tuple-element.64), channel_id=1, source_target_pairs={{0,2},{2,0},{4,6},{6,4},{8,10},{10,8},{12,14},{14,12},{16,18},{18,... | collective-permute-start | bytes 4128776 | tf_op jit(solution)/shard_map/ppermute | solution.py:22
  173.4 35.8 %collective-permute-start.10 = (bf16[8,672,128]{2,1,0:T(8,128)(2,1)}, bf16[8,672,128]{2,1,0:T(8,128)(2,1)S(1)}, u32[]{:S(2)}, u32[]{:S(2)}) collective-permute-start(bf16[8,672,128]{2,1,0:T(8,128)(2,1)} %get-tuple-element.70), channel_id=1, source_target_pairs={{0,2},{2,0},{4,6},{6,4},{8,10},{10,8},{12,14},{14,12},{16,18},{18,... | collective-permute-start | bytes 4128776 | tf_op jit(solution)/shard_map/ppermute | solution.py:22
  174.1 41.9 %collective-permute-start.7 = (bf16[8,128,640]{2,1,0:T(8,128)(2,1)S(1)}, bf16[8,128,640]{2,1,0:T(8,128)(2,1)}, u32[]{:S(2)}, u32[]{:S(2)}) collective-permute-start(bf16[8,128,640]{2,1,0:T(8,128)(2,1)S(1)} %copy-done.20), channel_id=1, source_target_pairs={{0,4},{2,6},{4,0},{6,2},{8,12},{10,14},{12,8},{14,10},{16,20},{18,... | collective-permute-start | bytes 3932168 | tf_op jit(solution)/shard_map/ppermute | solution.py:22
  180.9 33.4 %collective-permute-start.9 = (bf16[4,672,128]{2,1,0:T(8,128)(2,1)S(1)}, bf16[4,672,128]{2,1,0:T(8,128)(2,1)S(1)}, u32[]{:S(2)}, u32[]{:S(2)}) collective-permute-start(bf16[4,672,128]{2,1,0:T(8,128)(2,1)S(1)} %get-tuple-element.69), channel_id=1, source_target_pairs={{0,4},{2,6},{4,0},{6,2},{8,12},{10,14},{12,8},{14,10},{16,20},{18,... | collective-permute-start | bytes 2064392 | tf_op jit(solution)/shard_map/ppermute | solution.py:22
  207.9 34.6 %collective-permute-start.14 = (bf16[8,672,128]{2,1,0:T(8,128)(2,1)}, bf16[8,672,128]{2,1,0:T(8,128)(2,1)S(1)}, u32[]{:S(2)}, u32[]{:S(2)}) collective-permute-start(bf16[8,672,128]{2,1,0:T(8,128)(2,1)} %get-tuple-element.78), channel_id=1, source_target_pairs={{0,2},{2,0},{4,6},{6,4},{8,10},{10,8},{12,14},{14,12},{16,18},{18,... | collective-permute-start | bytes 4128776 | tf_op jit(solution)/shard_map/ppermute | solution.py:22
  239.5 30.4 %collective-permute-start.11 = (bf16[8,672,128]{2,1,0:T(8,128)(2,1)}, bf16[8,672,128]{2,1,0:T(8,128)(2,1)}, u32[]{:S(2)}, u32[]{:S(2)}) collective-permute-start(bf16[8,672,128]{2,1,0:T(8,128)(2,1)} %get-tuple-element.75), channel_id=1, source_target_pairs={{0,2},{2,0},{4,6},{6,4},{8,10},{10,8},{12,14},{14,12},{16,18},{18,... | collective-permute-start | bytes 4128776 | tf_op jit(solution)/shard_map/ppermute | solution.py:22
  242.2 18.6 %collective-permute-start.13 = (bf16[4,672,128]{2,1,0:T(8,128)(2,1)}, bf16[4,672,128]{2,1,0:T(8,128)(2,1)S(1)}, u32[]{:S(2)}, u32[]{:S(2)}) collective-permute-start(bf16[4,672,128]{2,1,0:T(8,128)(2,1)} %get-tuple-element.77), channel_id=1, source_target_pairs={{0,4},{2,6},{4,0},{6,2},{8,12},{10,14},{12,8},{14,10},{16,20},{18,... | collective-permute-start | bytes 2064392 | tf_op jit(solution)/shard_map/ppermute | solution.py:22
  245.5 33.9 %collective-permute-start.18 = (bf16[4,672,128]{2,1,0:T(8,128)(2,1)}, bf16[4,672,128]{2,1,0:T(8,128)(2,1)}, u32[]{:S(2)}, u32[]{:S(2)}) collective-permute-start(bf16[4,672,128]{2,1,0:T(8,128)(2,1)} %get-tuple-element.88), channel_id=1, source_target_pairs={{0,4},{2,6},{4,0},{6,2},{8,12},{10,14},{12,8},{14,10},{16,20},{18,... | collective-permute-start | bytes 2064392 | tf_op jit(solution)/shard_map/ppermute | solution.py:22
  247.2 21.8 %collective-permute-start.12 = (bf16[2,672,128]{2,1,0:T(8,128)(2,1)}, bf16[2,672,128]{2,1,0:T(8,128)(2,1)S(1)}, u32[]{:S(2)}, u32[]{:S(2)}) collective-permute-start(bf16[2,672,128]{2,1,0:T(8,128)(2,1)} %get-tuple-element.76), channel_id=1, source_target_pairs={{0,8},{2,10},{4,12},{6,14},{8,0},{10,2},{12,4},{14,6},{16,24},{18,... | collective-permute-start | bytes 1032200 | tf_op jit(solution)/shard_map/ppermute | solution.py:22
  261.7 16.0 %collective-permute-start.15 = (bf16[2,672,128]{2,1,0:T(8,128)(2,1)}, bf16[2,672,128]{2,1,0:T(8,128)(2,1)}, u32[]{:S(2)}, u32[]{:S(2)}) collective-permute-start(bf16[2,672,128]{2,1,0:T(8,128)(2,1)} %get-tuple-element.84), channel_id=1, source_target_pairs={{0,8},{2,10},{4,12},{6,14},{8,0},{10,2},{12,4},{14,6},{16,24},{18,... | collective-permute-start | bytes 1032200 | tf_op jit(solution)/shard_map/ppermute | solution.py:22
  269.9 20.6 %collective-permute-start.17 = (bf16[1,672,128]{2,1,0:T(8,128)(2,1)}, bf16[1,672,128]{2,1,0:T(8,128)(2,1)}, u32[]{:S(2)}, u32[]{:S(2)}) collective-permute-start(bf16[1,672,128]{2,1,0:T(8,128)(2,1)} %get-tuple-element.87), channel_id=1, source_target_pairs={{0,16},{2,18},{4,20},{6,22},{8,24},{10,26},{12,28},{14,30},{16,0},... | collective-permute-start | bytes 516104 | tf_op jit(solution)/shard_map/ppermute | solution.py:22
  273.4 23.7 %collective-permute-start.19 = (bf16[4,672,128]{2,1,0:T(8,128)(2,1)}, bf16[4,672,128]{2,1,0:T(8,128)(2,1)S(1)}, u32[]{:S(2)}, u32[]{:S(2)}) collective-permute-start(bf16[4,672,128]{2,1,0:T(8,128)(2,1)} %get-tuple-element.90), channel_id=1, source_target_pairs={{0,4},{2,6},{4,0},{6,2},{8,12},{10,14},{12,8},{14,10},{16,20},{18,... | collective-permute-start | bytes 2064392 | tf_op jit(solution)/shard_map/ppermute | solution.py:22
  281.5 13.9 %collective-permute-start.20 = (bf16[2,672,128]{2,1,0:T(8,128)(2,1)}, bf16[2,672,128]{2,1,0:T(8,128)(2,1)S(1)}, u32[]{:S(2)}, u32[]{:S(2)}) collective-permute-start(bf16[2,672,128]{2,1,0:T(8,128)(2,1)} %get-tuple-element.91), channel_id=1, source_target_pairs={{0,8},{2,10},{4,12},{6,14},{8,0},{10,2},{12,4},{14,6},{16,24},{18,... | collective-permute-start | bytes 1032200 | tf_op jit(solution)/shard_map/ppermute | solution.py:22
  290.3 53.9 %collective-permute-start.27 = (bf16[640,2560]{1,0:T(8,128)(2,1)S(1)}, bf16[640,2560]{1,0:T(8,128)(2,1)S(1)}, u32[]{:S(2)}, u32[]{:S(2)}) collective-permute-start(bf16[640,2560]{1,0:T(8,128)(2,1)S(1)} %get-tuple-element.111), channel_id=1, source_target_pairs={{0,1},{1,0},{2,3},{3,2},{4,5},{5,4},{6,7},{7,6},{8,9},{9,8},{10,11... | collective-permute-start | bytes 9830408 | tf_op jit(solution)/shard_map/ppermute | solution.py:31
  305.8 14.2 %collective-permute-start.22 = (bf16[1920,128]{1,0:T(8,128)(2,1)S(1)}, bf16[1920,128]{1,0:T(8,128)(2,1)S(1)}, u32[]{:S(2)}, u32[]{:S(2)}) collective-permute-start(bf16[1920,128]{1,0:T(8,128)(2,1)S(1)} %pad_maximum_fusion.7), channel_id=1, source_target_pairs={{0,2},{2,0},{4,6},{6,4},{8,10},{10,8},{12,14},{14,12},{16,18},{18,... | collective-permute-start | bytes 1474568 | tf_op jit(solution)/shard_map/ppermute | solution.py:22
  305.9 22.7 %collective-permute-start.23 = (bf16[1920,128]{1,0:T(8,128)(2,1)S(1)}, bf16[1920,128]{1,0:T(8,128)(2,1)S(1)}, u32[]{:S(2)}, u32[]{:S(2)}) collective-permute-start(bf16[1920,128]{1,0:T(8,128)(2,1)S(1)} %pad_maximum_fusion.7), channel_id=1, source_target_pairs={{0,4},{2,6},{4,0},{6,2},{8,12},{10,14},{12,8},{14,10},{16,20},{18,... | collective-permute-start | bytes 1474568 | tf_op jit(solution)/shard_map/ppermute | solution.py:22
  307.2 21.4 %collective-permute-start.24 = (bf16[1920,128]{1,0:T(8,128)(2,1)S(1)}, bf16[1920,128]{1,0:T(8,128)(2,1)S(1)}, u32[]{:S(2)}, u32[]{:S(2)}) collective-permute-start(bf16[1920,128]{1,0:T(8,128)(2,1)S(1)} %pad_maximum_fusion.7), channel_id=1, source_target_pairs={{0,6},{2,4},{4,2},{6,0},{8,14},{10,12},{12,10},{14,8},{16,22},{18,... | collective-permute-start | bytes 1474568 | tf_op jit(solution)/shard_map/ppermute | solution.py:22
  (44 other events, 807.8 us)
Sparse Core Ops, SparseCore 0:
  16.7 117.1 all-gather.5
  146.1 128.6 all-gather.3

commit v9 on v8

--- a/solution.py
+++ b/solution.py
@@ -484,7 +484,7 @@
     last = len(masks) - 1
     if groups > 1:
         turns = ("a1", "a0", "c1", "a2", "c0", "c1", "a3", "c2", "c0", "c1", "c3", "c0", "c2", "l1", "l0")
-        turns += ("c2", "c3", "l2", "c3", "l3")
+        turns += ("c3", "c2", "c3", "l2", "l3")
     else:
         turns = ("a0",) + ("c0",) * last + ("l0",)
     state, stage, attended = {}, {}, []
@@ -510,7 +510,7 @@
             stage[names] = 0
             before = state[names][0]
             if weight is None:
-                weight = gather_weights(before)
+                weight = gather_weights(stages[2] if groups > 1 else before)
             continue
         if names not in state:
             parts = list(names)

time: 371 us -> 394 us (1.062)
  waiting for transfers between devices: 156 us -> 184 us
  starting transfers between devices: 51.5 us -> 40.1 us
  local copies, waits for them, and re-layouts: 11.3 us -> 16.1 us
    ppermute x33, waiting for transfers between devices: 156 us -> 184 us  [send_xor(): return lax.ppermute(value, 'req', [(i, i ^ by) for i in range(size)])]
    ppermute x33, starting transfers between devices: 51.2 us -> 39.8 us  [send_xor(): return lax.ppermute(value, 'req', [(i, i ^ by) for i in range(size)])]
    pallas_call x4, Pallas kernels: 94.6 us -> 101 us  [attend(): pl.pallas_call(functools.partial(attend_kernel, q_column), grid_spec=pltp...]
    pallas_call x12, Pallas kernels: 14.8 us -> 9.94 us  [combine(): pl.pallas_call(combine_kernel, grid=(half,), in_specs=[low, high, low, hi...]
    unnamed x60 -> x62, local copies, waits for them, and re-layouts: 6.37 us -> 11.2 us
  transfers between devices with their start and end apart: 38 -> 38, of which waited for: 22 -> 21; matrix products, arithmetic and copies ran while one was open for 4% -> 4% of each run, Pallas kernels for 30% -> 29%
where the time goes in v9:
time: 394 us; the launch traced here: 393 us
  waiting for transfers between devices  184 us (47%)
  Pallas kernels  114 us (29%)
  starting transfers between devices  40.1 us (10%)
  local copies, waits for them, and re-layouts  16.1 us (4%)
  other arithmetic  14.4 us (4%)
  between operations  14.1 us (4%)
  matrix products  6.08 us (2%)
    ppermute x33, waiting for transfers between devices, send_xor(): return lax.ppermute(value, 'req', [(i, i ^ by) for i in range(size)])  184 us
    pallas_call x4, Pallas kernels, attend(): pl.pallas_call(functools.partial(attend_kernel, q_column), grid_spec=pltp...  101 us
    ppermute x33, starting transfers between devices, send_xor(): return lax.ppermute(value, 'req', [(i, i ^ by) for i in range(size)])  39.8 us
    unnamed x62, local copies, waits for them, and re-layouts  11.2 us
    pallas_call x12, Pallas kernels, combine(): pl.pallas_call(combine_kernel, grid=(half,), in_specs=[low, high, low, hi...  9.94 us
  transfers between devices with their start and end apart: 38, of which 21 were waited for; matrix products, arithmetic and copies ran while one was open for 4% of the time, Pallas kernels for 29%

profile of v9, /device:TPU:0, one launch (start us, length us, event | category | flops | bytes accessed | tf_op | source)
XLA Modules:
  0.0 392.7 jit_solution(10183811298185997568)
XLA Ops:
  10.4 3.9 psum.7
  17.0 3.8 collective-permute-start
  20.8 8.2 %collective-permute-done = bf16[1,128,640]{2,1,0:T(8,128)(2,1)S(1)} collective-permute-done((bf16[1,128,640]{2,1,0:T(8,128)(2,1)S(1)}, bf16[1,128,640]{2,1,0:T(8,128)(2,1)S(1)}, u32[]{:S(2)}, u32[]{:S(2)}) %collective-permute-start) | collective-permute-done | bytes 163872 | tf_op jit(solution)/shard_map/ppermute | solution.py:22
  29.9 14.8 %collective-permute-done.1 = bf16[2,128,640]{2,1,0:T(8,128)(2,1)S(1)} collective-permute-done((bf16[2,128,640]{2,1,0:T(8,128)(2,1)S(1)}, bf16[2,128,640]{2,1,0:T(8,128)(2,1)S(1)}, u32[]{:S(2)}, u32[]{:S(2)}) %collective-permute-start.1) | collective-permute-done | bytes 327712 | tf_op jit(solution)/shard_map/ppermute | solution.py:22
  46.3 24.4 %collective-permute-done.2 = bf16[4,128,640]{2,1,0:T(8,128)(2,1)S(1)} collective-permute-done((bf16[4,128,640]{2,1,0:T(8,128)(2,1)S(1)}, bf16[4,128,640]{2,1,0:T(8,128)(2,1)S(1)}, u32[]{:S(2)}, u32[]{:S(2)}) %collective-permute-start.2) | collective-permute-done | bytes 655392 | tf_op jit(solution)/shard_map/ppermute | solution.py:22
  75.5 9.6 %collective-permute-done.3 = bf16[1,128,640]{2,1,0:T(8,128)(2,1)S(1)} collective-permute-done((bf16[1,128,640]{2,1,0:T(8,128)(2,1)S(1)}, bf16[1,128,640]{2,1,0:T(8,128)(2,1)S(1)}, u32[]{:S(2)}, u32[]{:S(2)}) %collective-permute-start.3) | collective-permute-done | bytes 163872 | tf_op jit(solution)/shard_map/ppermute | solution.py:22
  85.8 23.5 %collective-permute-done.4 = bf16[2,128,640]{2,1,0:T(8,128)(2,1)S(1)} collective-permute-done((bf16[2,128,640]{2,1,0:T(8,128)(2,1)S(1)}, bf16[2,128,640]{2,1,0:T(8,128)(2,1)S(1)}, u32[]{:S(2)}, u32[]{:S(2)}) %collective-permute-start.4) | collective-permute-done | bytes 327712 | tf_op jit(solution)/shard_map/ppermute | solution.py:22
  114.9 9.9 %collective-permute-done.5 = bf16[4,128,640]{2,1,0:T(8,128)(2,1)S(1)} collective-permute-done((bf16[4,128,640]{2,1,0:T(8,128)(2,1)S(1)}, bf16[4,128,640]{2,1,0:T(8,128)(2,1)S(1)}, u32[]{:S(2)}, u32[]{:S(2)}) %collective-permute-start.5) | collective-permute-done | bytes 655392 | tf_op jit(solution)/shard_map/ppermute | solution.py:22
  125.9 10.6 %collective-permute-done.7.refs_1_ = bf16[8,128,640]{2,1,0:T(8,128)(2,1)S(1)} collective-permute-done((bf16[8,128,640]{2,1,0:T(8,128)(2,1)S(1)}, bf16[8,128,640]{2,1,0:T(8,128)(2,1)S(1)}, u32[]{:S(2)}, u32[]{:S(2)}) %collective-permute-start.7) | collective-permute-done | bytes 1310752 | tf_op jit(solution)/shard_map/ppermute | solution.py:22
  137.6 25.4 %cache_attend.4 = (bf16[8,672,128]{2,1,0:T(8,128)(2,1)}, bf16[8,672,128]{2,1,0:T(8,128)(2,1)}) custom-call(s32[64]{0:T(128)} %reshape.326.table_ref, s32[18]{0:T(128)} %fusion.15.slot_ref, s32[18]{0:T(128)} %fusion.16.q_slot_ref, bf16[8,128,640]{2,1,0:T(8,128)(2,1)} %pad_maximum_fusion.1.refs_0_, bf16[8,128,640]{2,1,0:T(8,128)(2,1)} %copy-done.22, ...), custom_call_target="tpu_custom_call" | custom-call | flops 5368709120 | bytes 10485760 | tf_op jit(solution)/shard_map/cache_attend/pallas_call | solution.py:243
  165.3 25.1 %cache_attend.5 = (bf16[8,672,128]{2,1,0:T(8,128)(2,1)}, bf16[8,672,128]{2,1,0:T(8,128)(2,1)}) custom-call(s32[64]{0:T(128)} %reshape.326.table_ref, s32[18]{0:T(128)} %fusion.15.slot_ref, s32[18]{0:T(128)} %fusion.17.q_slot_ref, bf16[16,128,1280]{2,1,0:T(8,128)(2,1)} %bitcast.44, bf16[16,256,2560]{2,1,0:T(8,128)(2,1)} %refs_2_.7, ...), custom_call_target="tpu_custom_call" | custom-call | flops 5368709120 | bytes 10485760 | tf_op jit(solution)/shard_map/cache_attend/pallas_call | solution.py:243
  190.8 4.0 %collective-permute-start.6 = (bf16[8,128,640]{2,1,0:T(8,128)(2,1)}, bf16[8,128,640]{2,1,0:T(8,128)(2,1)}, u32[]{:S(2)}, u32[]{:S(2)}) collective-permute-start(bf16[8,128,640]{2,1,0:T(8,128)(2,1)} %pad_maximum_fusion.2.refs_8_.refs_0_), channel_id=1, source_target_pairs={{0,4},{2,6},{4,0},{6,2},{8,12},{10,14},{12,8},{14,10},{16,20},{18,... | collective-permute-start | bytes 3932168 | tf_op jit(solution)/shard_map/ppermute | solution.py:22
  200.6 25.1 %cache_attend.6 = (bf16[8,672,128]{2,1,0:T(8,128)(2,1)}, bf16[8,672,128]{2,1,0:T(8,128)(2,1)}) custom-call(s32[64]{0:T(128)} %reshape.326.table_ref, s32[18]{0:T(128)} %fusion.15.slot_ref, s32[18]{0:T(128)} %fusion.17.q_slot_ref, bf16[16,128,1280]{2,1,0:T(8,128)(2,1)} %bitcast.45, bf16[16,256,2560]{2,1,0:T(8,128)(2,1)} %refs_2_.7, ...), custom_call_target="tpu_custom_call" | custom-call | flops 5368709120 | bytes 10485760 | tf_op jit(solution)/shard_map/cache_attend/pallas_call | solution.py:243
  229.4 5.3 %collective-permute-done.9.refs_2_.refs_3_ = bf16[4,672,128]{2,1,0:T(8,128)(2,1)S(1)} collective-permute-done((bf16[4,672,128]{2,1,0:T(8,128)(2,1)}, bf16[4,672,128]{2,1,0:T(8,128)(2,1)S(1)}, u32[]{:S(2)}, u32[]{:S(2)}) %collective-permute-start.9) | collective-permute-done | bytes 688160 | tf_op jit(solution)/shard_map/ppermute | solution.py:22
  235.8 25.1 %cache_attend.7 = (bf16[8,672,128]{2,1,0:T(8,128)(2,1)}, bf16[8,672,128]{2,1,0:T(8,128)(2,1)}) custom-call(s32[64]{0:T(128)} %reshape.326.table_ref, s32[18]{0:T(128)} %fusion.15.slot_ref, s32[18]{0:T(128)} %fusion.16.q_slot_ref, bf16[8,128,640]{2,1,0:T(8,128)(2,1)} %pad_maximum_fusion.2.refs_8_.refs_0_, ...), custom_call_target="tpu_custom_call" | custom-call | flops 5368709120 | bytes 10485760 | tf_op jit(solution)/shard_map/cache_attend/pallas_call | solution.py:243
  267.6 13.3 %collective-permute-done.13.refs_2_.refs_3_ = bf16[4,672,128]{2,1,0:T(8,128)(2,1)S(1)} collective-permute-done((bf16[4,672,128]{2,1,0:T(8,128)(2,1)S(1)}, bf16[4,672,128]{2,1,0:T(8,128)(2,1)S(1)}, u32[]{:S(2)}, u32[]{:S(2)}) %collective-permute-start.13) | collective-permute-done | bytes 688160 | tf_op jit(solution)/shard_map/ppermute | solution.py:22
  282.6 6.2 %collective-permute-done.11.refs_2_.refs_3_ = bf16[8,672,128]{2,1,0:T(8,128)(2,1)S(1)} collective-permute-done((bf16[8,672,128]{2,1,0:T(8,128)(2,1)}, bf16[8,672,128]{2,1,0:T(8,128)(2,1)S(1)}, u32[]{:S(2)}, u32[]{:S(2)}) %collective-permute-start.11) | collective-permute-done | bytes 1376288 | tf_op jit(solution)/shard_map/ppermute | solution.py:22
  292.6 8.4 %collective-permute-done.15.refs_2_.refs_3_ = bf16[2,672,128]{2,1,0:T(8,128)(2,1)S(1)} collective-permute-done((bf16[2,672,128]{2,1,0:T(8,128)(2,1)S(1)}, bf16[2,672,128]{2,1,0:T(8,128)(2,1)S(1)}, u32[]{:S(2)}, u32[]{:S(2)}) %collective-permute-start.15) | collective-permute-done | bytes 344096 | tf_op jit(solution)/shard_map/ppermute | solution.py:22
  306.4 4.2 %collective-permute-done.16.got_ref = bf16[1,672,128]{2,1,0:T(8,128)(2,1)} collective-permute-done((bf16[1,672,128]{2,1,0:T(8,128)(2,1)}, bf16[1,672,128]{2,1,0:T(8,128)(2,1)}, u32[]{:S(2)}, u32[]{:S(2)}) %collective-permute-start.16) | collective-permute-done | bytes 172064 | tf_op jit(solution)/shard_map/ppermute | solution.py:22
  320.8 7.4 %collective-permute-done.21.got_ref = bf16[1,672,128]{2,1,0:T(8,128)(2,1)S(1)} collective-permute-done((bf16[1,672,128]{2,1,0:T(8,128)(2,1)S(1)}, bf16[1,672,128]{2,1,0:T(8,128)(2,1)S(1)}, u32[]{:S(2)}, u32[]{:S(2)}) %collective-permute-start.21) | collective-permute-done | bytes 172064 | tf_op jit(solution)/shard_map/ppermute | solution.py:22
  331.9 9.0 %collective-permute-done.26.got_ref = bf16[1,672,128]{2,1,0:T(8,128)(2,1)S(1)} collective-permute-done((bf16[1,672,128]{2,1,0:T(8,128)(2,1)S(1)}, bf16[1,672,128]{2,1,0:T(8,128)(2,1)S(1)}, u32[]{:S(2)}, u32[]{:S(2)}) %collective-permute-start.26) | collective-permute-done | bytes 172064 | tf_op jit(solution)/shard_map/ppermute | solution.py:22
  342.6 10.7 %collective-permute-done.24 = bf16[1920,128]{1,0:T(8,128)(2,1)S(1)} collective-permute-done((bf16[1920,128]{1,0:T(8,128)(2,1)S(1)}, bf16[1920,128]{1,0:T(8,128)(2,1)S(1)}, u32[]{:S(2)}, u32[]{:S(2)}) %collective-permute-start.24) | collective-permute-done | bytes 491552 | tf_op jit(solution)/shard_map/ppermute | solution.py:22
  360.1 3.5 collective-permute-done.29
  375.1 6.6 %collective-permute-done.34 = bf16[640,128]{1,0:T(8,128)(2,1)S(1)} collective-permute-done((bf16[640,128]{1,0:T(8,128)(2,1)S(1)}, bf16[640,128]{1,0:T(8,128)(2,1)S(1)}, u32[]{:S(2)}, u32[]{:S(2)}) %collective-permute-start.34) | collective-permute-done | bytes 163872 | tf_op jit(solution)/shard_map/ppermute | solution.py:22
  (196 shorter events, 90.6 us)
Async XLA Ops:
  6.6 158.7 %all-gather.6.cloned.1.call-start = ((), (), s32[]{:S(2)}) async-start(), calls=%async_computation.1 | async-start | bytes 5570560 | tf_op jit(solution)/shard_map/all_gather | solution.py:466
  16.5 289.8 %all-gather.4.cloned.1.call-start = ((), (), s32[]{:S(2)}) async-start(), calls=%async_computation | async-start | bytes 8192000 | tf_op jit(solution)/shard_map/all_gather | solution.py:473
  29.1 15.6 %collective-permute-start.1 = (bf16[2,128,640]{2,1,0:T(8,128)(2,1)S(1)}, bf16[2,128,640]{2,1,0:T(8,128)(2,1)S(1)}, u32[]{:S(2)}, u32[]{:S(2)}) collective-permute-start(bf16[2,128,640]{2,1,0:T(8,128)(2,1)S(1)} %pad_maximum_fusion.8), channel_id=1, source_target_pairs={{0,8},{2,10},{4,12},{6,14},{8,0},{10,2},{12,4},{14,6},{16,24},{18,... | collective-permute-start | bytes 983048 | tf_op jit(solution)/shard_map/ppermute | solution.py:22
  44.8 25.9 %collective-permute-start.2 = (bf16[4,128,640]{2,1,0:T(8,128)(2,1)S(1)}, bf16[4,128,640]{2,1,0:T(8,128)(2,1)S(1)}, u32[]{:S(2)}, u32[]{:S(2)}) collective-permute-start(bf16[4,128,640]{2,1,0:T(8,128)(2,1)S(1)} %pad_maximum_fusion.4._), channel_id=1, source_target_pairs={{0,2},{2,0},{4,6},{6,4},{8,10},{10,8},{12,14},{14,12},{16,18},{18,... | collective-permute-start | bytes 1966088 | tf_op jit(solution)/shard_map/ppermute | solution.py:22
  85.2 24.1 %collective-permute-start.4 = (bf16[2,128,640]{2,1,0:T(8,128)(2,1)S(1)}, bf16[2,128,640]{2,1,0:T(8,128)(2,1)S(1)}, u32[]{:S(2)}, u32[]{:S(2)}) collective-permute-start(bf16[2,128,640]{2,1,0:T(8,128)(2,1)S(1)} %pad_maximum_fusion.9), channel_id=1, source_target_pairs={{0,8},{2,10},{4,12},{6,14},{8,0},{10,2},{12,4},{14,6},{16,24},{18,... | collective-permute-start | bytes 983048 | tf_op jit(solution)/shard_map/ppermute | solution.py:22
  109.4 27.1 %collective-permute-start.7 = (bf16[8,128,640]{2,1,0:T(8,128)(2,1)S(1)}, bf16[8,128,640]{2,1,0:T(8,128)(2,1)S(1)}, u32[]{:S(2)}, u32[]{:S(2)}) collective-permute-start(bf16[8,128,640]{2,1,0:T(8,128)(2,1)S(1)} %copy-done.21), channel_id=1, source_target_pairs={{0,4},{2,6},{4,0},{6,2},{8,12},{10,14},{12,8},{14,10},{16,20},{18,... | collective-permute-start | bytes 3932168 | tf_op jit(solution)/shard_map/ppermute | solution.py:22
  111.9 12.8 %collective-permute-start.5 = (bf16[4,128,640]{2,1,0:T(8,128)(2,1)S(1)}, bf16[4,128,640]{2,1,0:T(8,128)(2,1)S(1)}, u32[]{:S(2)}, u32[]{:S(2)}) collective-permute-start(bf16[4,128,640]{2,1,0:T(8,128)(2,1)S(1)} %pad_maximum_fusion.5), channel_id=1, source_target_pairs={{0,2},{2,0},{4,6},{6,4},{8,10},{10,8},{12,14},{14,12},{16,18},{18,... | collective-permute-start | bytes 1966088 | tf_op jit(solution)/shard_map/ppermute | solution.py:22
  163.0 31.7 %collective-permute-start.8 = (bf16[8,672,128]{2,1,0:T(8,128)(2,1)}, bf16[8,672,128]{2,1,0:T(8,128)(2,1)S(1)}, u32[]{:S(2)}, u32[]{:S(2)}) collective-permute-start(bf16[8,672,128]{2,1,0:T(8,128)(2,1)} %get-tuple-element.64), channel_id=1, source_target_pairs={{0,2},{2,0},{4,6},{6,4},{8,10},{10,8},{12,14},{14,12},{16,18},{18,... | collective-permute-start | bytes 4128776 | tf_op jit(solution)/shard_map/ppermute | solution.py:22
  190.4 37.0 %collective-permute-start.10 = (bf16[8,672,128]{2,1,0:T(8,128)(2,1)}, bf16[8,672,128]{2,1,0:T(8,128)(2,1)S(1)}, u32[]{:S(2)}, u32[]{:S(2)}) collective-permute-start(bf16[8,672,128]{2,1,0:T(8,128)(2,1)} %get-tuple-element.70), channel_id=1, source_target_pairs={{0,2},{2,0},{4,6},{6,4},{8,10},{10,8},{12,14},{14,12},{16,18},{18,... | collective-permute-start | bytes 4128776 | tf_op jit(solution)/shard_map/ppermute | solution.py:22
  190.8 45.0 %collective-permute-start.6 = (bf16[8,128,640]{2,1,0:T(8,128)(2,1)}, bf16[8,128,640]{2,1,0:T(8,128)(2,1)}, u32[]{:S(2)}, u32[]{:S(2)}) collective-permute-start(bf16[8,128,640]{2,1,0:T(8,128)(2,1)} %pad_maximum_fusion.2.refs_8_.refs_0_), channel_id=1, source_target_pairs={{0,4},{2,6},{4,0},{6,2},{8,12},{10,14},{12,8},{14,10},{16,20},{18,... | collective-permute-start | bytes 3932168 | tf_op jit(solution)/shard_map/ppermute | solution.py:22
  198.7 36.0 %collective-permute-start.9 = (bf16[4,672,128]{2,1,0:T(8,128)(2,1)}, bf16[4,672,128]{2,1,0:T(8,128)(2,1)S(1)}, u32[]{:S(2)}, u32[]{:S(2)}) collective-permute-start(bf16[4,672,128]{2,1,0:T(8,128)(2,1)} %get-tuple-element.69), channel_id=1, source_target_pairs={{0,4},{2,6},{4,0},{6,2},{8,12},{10,14},{12,8},{14,10},{16,20},{18,... | collective-permute-start | bytes 2064392 | tf_op jit(solution)/shard_map/ppermute | solution.py:22
  225.7 38.8 %collective-permute-start.14 = (bf16[8,672,128]{2,1,0:T(8,128)(2,1)}, bf16[8,672,128]{2,1,0:T(8,128)(2,1)S(1)}, u32[]{:S(2)}, u32[]{:S(2)}) collective-permute-start(bf16[8,672,128]{2,1,0:T(8,128)(2,1)} %get-tuple-element.78), channel_id=1, source_target_pairs={{0,2},{2,0},{4,6},{6,4},{8,10},{10,8},{12,14},{14,12},{16,18},{18,... | collective-permute-start | bytes 4128776 | tf_op jit(solution)/shard_map/ppermute | solution.py:22
  261.0 27.9 %collective-permute-start.11 = (bf16[8,672,128]{2,1,0:T(8,128)(2,1)}, bf16[8,672,128]{2,1,0:T(8,128)(2,1)S(1)}, u32[]{:S(2)}, u32[]{:S(2)}) collective-permute-start(bf16[8,672,128]{2,1,0:T(8,128)(2,1)} %get-tuple-element.75), channel_id=1, source_target_pairs={{0,2},{2,0},{4,6},{6,4},{8,10},{10,8},{12,14},{14,12},{16,18},{18,... | collective-permute-start | bytes 4128776 | tf_op jit(solution)/shard_map/ppermute | solution.py:22
  261.3 19.6 %collective-permute-start.13 = (bf16[4,672,128]{2,1,0:T(8,128)(2,1)S(1)}, bf16[4,672,128]{2,1,0:T(8,128)(2,1)S(1)}, u32[]{:S(2)}, u32[]{:S(2)}) collective-permute-start(bf16[4,672,128]{2,1,0:T(8,128)(2,1)S(1)} %get-tuple-element.77), channel_id=1, source_target_pairs={{0,4},{2,6},{4,0},{6,2},{8,12},{10,14},{12,8},{14,10},{16,20},{18,... | collective-permute-start | bytes 2064392 | tf_op jit(solution)/shard_map/ppermute | solution.py:22
  264.5 16.7 %collective-permute-start.12 = (bf16[2,672,128]{2,1,0:T(8,128)(2,1)S(1)}, bf16[2,672,128]{2,1,0:T(8,128)(2,1)S(1)}, u32[]{:S(2)}, u32[]{:S(2)}) collective-permute-start(bf16[2,672,128]{2,1,0:T(8,128)(2,1)S(1)} %get-tuple-element.76), channel_id=1, source_target_pairs={{0,8},{2,10},{4,12},{6,14},{8,0},{10,2},{12,4},{14,6},{16,24},{18,... | collective-permute-start | bytes 1032200 | tf_op jit(solution)/shard_map/ppermute | solution.py:22
  267.6 34.9 %collective-permute-start.18 = (bf16[4,672,128]{2,1,0:T(8,128)(2,1)}, bf16[4,672,128]{2,1,0:T(8,128)(2,1)S(1)}, u32[]{:S(2)}, u32[]{:S(2)}) collective-permute-start(bf16[4,672,128]{2,1,0:T(8,128)(2,1)} %get-tuple-element.88), channel_id=1, source_target_pairs={{0,4},{2,6},{4,0},{6,2},{8,12},{10,14},{12,8},{14,10},{16,20},{18,... | collective-permute-start | bytes 2064392 | tf_op jit(solution)/shard_map/ppermute | solution.py:22
  290.5 22.0 %collective-permute-start.19 = (bf16[4,672,128]{2,1,0:T(8,128)(2,1)}, bf16[4,672,128]{2,1,0:T(8,128)(2,1)S(1)}, u32[]{:S(2)}, u32[]{:S(2)}) collective-permute-start(bf16[4,672,128]{2,1,0:T(8,128)(2,1)} %get-tuple-element.90), channel_id=1, source_target_pairs={{0,4},{2,6},{4,0},{6,2},{8,12},{10,14},{12,8},{14,10},{16,20},{18,... | collective-permute-start | bytes 2064392 | tf_op jit(solution)/shard_map/ppermute | solution.py:22
  292.3 13.1 %collective-permute-start.17 = (bf16[1,672,128]{2,1,0:T(8,128)(2,1)}, bf16[1,672,128]{2,1,0:T(8,128)(2,1)}, u32[]{:S(2)}, u32[]{:S(2)}) collective-permute-start(bf16[1,672,128]{2,1,0:T(8,128)(2,1)} %get-tuple-element.87), channel_id=1, source_target_pairs={{0,16},{2,18},{4,20},{6,22},{8,24},{10,26},{12,28},{14,30},{16,0},... | collective-permute-start | bytes 516104 | tf_op jit(solution)/shard_map/ppermute | solution.py:22
  304.4 12.3 %collective-permute-start.20 = (bf16[2,672,128]{2,1,0:T(8,128)(2,1)}, bf16[2,672,128]{2,1,0:T(8,128)(2,1)S(1)}, u32[]{:S(2)}, u32[]{:S(2)}) collective-permute-start(bf16[2,672,128]{2,1,0:T(8,128)(2,1)} %get-tuple-element.93), channel_id=1, source_target_pairs={{0,8},{2,10},{4,12},{6,14},{8,0},{10,2},{12,4},{14,6},{16,24},{18,... | collective-permute-start | bytes 1032200 | tf_op jit(solution)/shard_map/ppermute | solution.py:22
  316.5 52.6 %collective-permute-start.27 = (bf16[640,2560]{1,0:T(8,128)(2,1)S(1)}, bf16[640,2560]{1,0:T(8,128)(2,1)S(1)}, u32[]{:S(2)}, u32[]{:S(2)}) collective-permute-start(bf16[640,2560]{1,0:T(8,128)(2,1)S(1)} %get-tuple-element.111), channel_id=1, source_target_pairs={{0,1},{1,0},{2,3},{3,2},{4,5},{5,4},{6,7},{7,6},{8,9},{9,8},{10,11... | collective-permute-start | bytes 9830408 | tf_op jit(solution)/shard_map/ppermute | solution.py:31
  328.4 14.2 %collective-permute-start.23 = (bf16[1920,128]{1,0:T(8,128)(2,1)S(1)}, bf16[1920,128]{1,0:T(8,128)(2,1)S(1)}, u32[]{:S(2)}, u32[]{:S(2)}) collective-permute-start(bf16[1920,128]{1,0:T(8,128)(2,1)S(1)} %pad_maximum_fusion.7), channel_id=1, source_target_pairs={{0,2},{2,0},{4,6},{6,4},{8,10},{10,8},{12,14},{14,12},{16,18},{18,... | collective-permute-start | bytes 1474568 | tf_op jit(solution)/shard_map/ppermute | solution.py:22
  330.2 23.1 %collective-permute-start.24 = (bf16[1920,128]{1,0:T(8,128)(2,1)S(1)}, bf16[1920,128]{1,0:T(8,128)(2,1)S(1)}, u32[]{:S(2)}, u32[]{:S(2)}) collective-permute-start(bf16[1920,128]{1,0:T(8,128)(2,1)S(1)} %pad_maximum_fusion.7), channel_id=1, source_target_pairs={{0,4},{2,6},{4,0},{6,2},{8,12},{10,14},{12,8},{14,10},{16,20},{18,... | collective-permute-start | bytes 1474568 | tf_op jit(solution)/shard_map/ppermute | solution.py:22
  330.2 23.1 %collective-permute-start.25 = (bf16[1920,128]{1,0:T(8,128)(2,1)S(1)}, bf16[1920,128]{1,0:T(8,128)(2,1)S(1)}, u32[]{:S(2)}, u32[]{:S(2)}) collective-permute-start(bf16[1920,128]{1,0:T(8,128)(2,1)S(1)} %pad_maximum_fusion.7), channel_id=1, source_target_pairs={{0,6},{2,4},{4,2},{6,0},{8,14},{10,12},{12,10},{14,8},{16,22},{18,... | collective-permute-start | bytes 1474568 | tf_op jit(solution)/shard_map/ppermute | solution.py:22
  356.5 12.7 %collective-permute-start.28 = (bf16[1920,512]{1,0:T(8,128)(2,1)S(1)}, bf16[1920,512]{1,0:T(8,128)(2,1)S(1)}, u32[]{:S(2)}, u32[]{:S(2)}) collective-permute-start(bf16[1920,512]{1,0:T(8,128)(2,1)S(1)} %pad_maximum_fusion), channel_id=1, source_target_pairs={{0,1},{1,0},{2,3},{3,2},{4,5},{5,4},{6,7},{7,6},{8,9},{9,8},{10,11... | collective-permute-start | bytes 5898248 | tf_op jit(solution)/shard_map/ppermute | solution.py:31
  (45 other events, 788.9 us)
Sparse Core Ops, SparseCore 0:
  16.7 114.1 all-gather.5
  132.4 115.8 all-gather.3
